TPU v7x, 32 devices: a whole 2x2x4 slice. The times are simulated.
32 devices in a mesh: groups: 2 (over x), tensor: 16 (over z, y, core).
Axes of the slice: x: 2, y: 2, z: 4, core: 2. Of those that a mesh axis runs over, the one named last changes fastest.
Arguments:
- gate_act: bfloat16 [53248, 32], P('tensor', 'groups'), parts along dimension 1, may hold values from -6 to 6
- up_act: bfloat16 [53248, 32], P('tensor', 'groups'), parts along dimension 1, may hold values from -6 to 6
- codes: int32 [26624, 8192], P('tensor'), may hold values from 0 to 255
- scales: bfloat16 [1664, 8192], P('tensor'), may hold values from 0.00039863586 to 0.0015945435
Outputs:
- ffn_out: bfloat16 [32, 8192], P(('groups', 'tensor')), parts along dimension 0
There are 2 independent parts, one for each index of `groups`. A program takes and returns all parts, laid end to end along the dimension named above; an argument that names none is the same for every part. Nothing has to cross between parts.
All inputs are finite; a program needn't handle non-finite values.
Results may differ from a plain program's by a relative error of at most 0.007.
Values may be sent and summed in bfloat16 or wider, within the bound.
No kernel may reach another device: no remote copies, remote signals or barrier semaphores. Data moves between devices by JAX's collectives and lax.ppermute only.
A program may use at most 384 MiB of HBM per device.

v0:
```python
import math

import jax
import jax.numpy as jnp
import numpy as np
from jax import lax
from jax.sharding import PartitionSpec as P

HAD_CROSS = 128
GROUP = 32
HAD_LOCAL = 416


def swapped(value, axis, distance):
    mask = 2**distance
    pairs = [(source, source ^ mask) for source in range(lax.axis_size(axis))]
    return lax.ppermute(value, axis, pairs)


def paley_table():
    squares = set()
    for real_part in range(5):
        for root_part in range(5):
            squares.add(
                (
                    (real_part * real_part + 2 * root_part * root_part) % 5,
                    2 * real_part * root_part % 5,
                )
            )
    jacobsthal = np.zeros((25, 25))
    for first in range(25):
        for second in range(25):
            differ = ((first // 5 - second // 5) % 5, (first % 5 - second % 5) % 5)
            if differ == (0, 0):
                jacobsthal[first, second] = 0.0
            elif differ in squares:
                jacobsthal[first, second] = 1.0
            else:
                jacobsthal[first, second] = -1.0
    conference = np.zeros((26, 26))
    conference[0, 1:] = 1.0
    conference[1:, 0] = 1.0
    conference[1:, 1:] = jacobsthal
    return np.kron(conference, np.array([[1.0, 1.0], [1.0, -1.0]])) + np.kron(
        np.eye(26), np.array([[1.0, -1.0], [-1.0, -1.0]])
    )


def walsh_table(order):
    matrix = np.ones((1, 1))
    while matrix.shape[0] < order:
        matrix = np.kron(np.array([[1.0, 1.0], [1.0, -1.0]]), matrix)
    return matrix


def hadamard_local(order):
    matrix = np.kron(walsh_table(order // 52), paley_table()) / math.sqrt(order)
    return jnp.asarray(matrix, dtype=jnp.float32).astype(jnp.bfloat16)


def sign_table(order):
    row_index = jnp.arange(order, dtype=jnp.int32)[:, None]
    col_index = jnp.arange(order, dtype=jnp.int32)[None, :]
    shared = jnp.zeros((order, order), jnp.int32)
    for bit_pos in range(order.bit_length() - 1):
        shared = shared + row_index // 2**bit_pos % 2 * (col_index // 2**bit_pos % 2)
    return (1 - 2 * (shared % 2)).astype(jnp.float32)


def dequantize(words, group_scales):
    low_codes = words % 16
    high_codes = words // 16
    unpacked = jnp.stack([low_codes, high_codes], axis=1).reshape(
        2 * words.shape[0], words.shape[1]
    )
    spread = jnp.repeat(group_scales.astype(jnp.float32), GROUP, axis=0)
    return ((unpacked - 8).astype(jnp.float32) * spread).astype(jnp.bfloat16)


def body(gate_act, up_act, codes, scales):
    units_here = gate_act.shape[0]
    total_rows = gate_act.shape[1]
    blocks_here = units_here // HAD_LOCAL
    factor = 1.0 / math.sqrt(HAD_CROSS)
    hidden = (jax.nn.silu(gate_act.astype(jnp.float32)) * up_act.astype(jnp.float32)).astype(
        jnp.bfloat16
    )
    hidden = hidden.reshape(blocks_here, HAD_LOCAL, total_rows)
    local_table = hadamard_local(HAD_LOCAL)
    local = jnp.einsum(
        "kn,anr->akr", local_table, hidden, preferred_element_type=jnp.float32
    ).astype(jnp.bfloat16)
    partial_sums = jnp.einsum(
        "abr,ae->ebr",
        local.astype(jnp.float32),
        sign_table(blocks_here),
        precision=lax.Precision.HIGHEST,
    )
    my_index = lax.axis_index("tensor")
    for bit_pos in range(lax.axis_size("tensor").bit_length() - 1):
        partner = swapped(partial_sums, "tensor", bit_pos)
        upper = my_index // 2**bit_pos % 2
        partial_sums = jnp.where(upper == 0, partial_sums + partner, partner - partial_sums)
    rotated = (partial_sums * factor).astype(jnp.bfloat16)
    rotated = rotated.reshape(units_here, total_rows)
    weight = dequantize(codes, scales)
    summed = lax.psum_scatter(
        lax.dot_general(
            rotated, weight, (((0,), (0,)), ((), ())), preferred_element_type=jnp.float32
        ),
        "tensor",
        scatter_dimension=0,
        tiled=True,
    )
    return summed.astype(jnp.bfloat16)


def solution(mesh):
    placed = (P("tensor", "groups"), P("tensor", "groups"), P("tensor", None), P("tensor", None))
    return jax.shard_map(
        body, mesh=mesh, in_specs=placed, out_specs=P(("groups", "tensor"), None), check_vma=False
    )
```

profile of v0, /device:TPU:0, one launch (start us, length us, event | category | flops | bytes accessed | tf_op | source)
XLA Modules:
  0.0 578.5 jit_solution(2207300311553692333)
XLA Ops:
  0.0 1.0 fusion.10
  1.0 0.2 reshape.291
  1.3 1.3 fusion.5
  2.5 0.3 fusion.16
  2.9 0.5 collective-permute-start
  3.4 1.2 collective-permute-done
  4.6 3.0 collective-permute-start.1
  7.6 53.2 %fusion.1 = (s32[1664,1,8192]{2,0,1:T(8,128)}, s32[1664,1,8192]{2,0,1:T(8,128)}) fusion(s32[1664,8192]{1,0:T(8,128)} %param.7), kind=kLoop, calls=%fused_computation.8 | loop fusion | flops 258998272 | bytes 163577856 | tf_op jit(solution)/shard_map/stack | solution.py:73
  60.7 0.0 collective-permute-done.1
  60.7 0.8 subtract_select_fusion.1
  61.5 1.6 collective-permute-start.2
  63.1 70.4 %fusion = f32[1664,2,8192]{2,0,1:T(8,128)} fusion(s32[1664,1,8192]{2,0,1:T(8,128)} %get-tuple-element.6, s32[1664,1,8192]{2,0,1:T(8,128)} %get-tuple-element.5), kind=kLoop, calls=%fused_computation.1 | loop fusion | flops 81788928 | bytes 218103808 | tf_op jit(solution)/shard_map/convert_element_type | solution.py:77
  133.5 173.9 %copy.7 = f32[1664,2,8192]{2,1,0:T(2,128)} copy(f32[1664,2,8192]{2,0,1:T(8,128)} %fusion) | data formatting | bytes 218103808 | tf_op jit(solution)/shard_map/convert_element_type | solution.py:77
  307.4 126.4 %convert_element_type.65 = f32[104,32,8192]{2,1,0:T(8,128)} reshape(f32[1664,2,8192]{2,1,0:T(2,128)} %copy.7) | data formatting | bytes 218103808 | tf_op jit(solution)/shard_map/convert_element_type | solution.py:77
  433.8 1.8 convert_element_type.66
  435.6 1.8 subtract_select_fusion
  437.4 2.6 collective-permute-start.3
  439.9 52.2 %multiply_convert_fusion = bf16[104,32,8192]{2,1,0:T(8,128)(2,1)} fusion(f32[104,32,8192]{2,1,0:T(8,128)} %convert_element_type.65, f32[104,8192]{1,0:T(8,128)S(1)} %convert_element_type.66), kind=kLoop, calls=%fused_computation.2 | loop fusion | flops 54525952 | bytes 166985728 | tf_op jit(solution)/shard_map/convert_element_type | solution.py:77
  492.2 0.6 dynamic-slice
  492.8 1.1 multiply_convert_fusion.1
  493.8 0.2 reshape.292
  494.0 20.3 %fusion.35 = f32[16,8192]{1,0:T(8,128)S(1)} fusion(bf16[3328,16]{0,1:T(8,128)(2,1)S(1)} %reshape.292, bf16[3328,8192]{1,0:T(8,128)(2,1)} %bitcast.21), kind=kOutput, calls=%fused_computation.67 | convolution fusion | flops 872415232 | bytes 55156736 | tf_op jit(solution)/shard_map/dot_general | solution.py:108
  514.3 62.9 %all-reduce.2 = bf16[16,8192]{1,0:T(8,128)(2,1)S(1)} all-reduce(f32[16,8192]{1,0:T(8,128)S(1)} %fusion.35), channel_id=2, replica_groups=mesh['groups'=2,'tensor'=16] {'tensor'}, use_global_device_ids=true, to_apply=%region_0.1.clone | all-reduce | flops 131072 | bytes 786432
  577.2 1.2 dynamic-slice_convert_fusion
  (7 shorter events, 0.1 us)
Async XLA Ops:
  2.9 1.7 collective-permute-start
  4.6 56.1 %collective-permute-start.1 = (f32[8,416,16]{1,0,2:T(8,128)S(1)}, f32[8,416,16]{1,0,2:T(8,128)S(1)}, u32[]{:S(2)}, u32[]{:S(2)}) collective-permute-start(f32[8,416,16]{1,0,2:T(8,128)S(1)} %subtract_select_fusion.2), channel_id=1, source_target_pairs={{0,2},{1,3},{2,0},{3,1},{4,6},{5,7},{6,4},{7,5},{8,10},{9,11},{10,... | collective-permute-start | bytes 638984 | tf_op jit(solution)/shard_map/ppermute | solution.py:17
  61.5 374.1 %collective-permute-start.2 = (f32[8,416,16]{1,0,2:T(8,128)}, f32[8,416,16]{1,0,2:T(8,128)}, u32[]{:S(2)}, u32[]{:S(2)}) collective-permute-start(f32[8,416,16]{1,0,2:T(8,128)} %subtract_select_fusion.1), channel_id=1, source_target_pairs={{0,4},{1,5},{2,6},{3,7},{4,0},{5,1},{6,2},{7,3},{8,12},{9,13},{10,... | collective-permute-start | bytes 638984 | tf_op jit(solution)/shard_map/ppermute | solution.py:17
  437.4 54.8 %copy-start = (u32[32]{0:T(128)S(1)}, u32[32]{0:T(128)}, u32[]{:S(2)}) copy-start(u32[32]{0:T(128)} %constant.212) | copy-start | bytes 388
  437.4 55.4 %collective-permute-start.3 = (f32[8,416,16]{1,0,2:T(8,128)}, f32[8,416,16]{1,0,2:T(8,128)}, u32[]{:S(2)}, u32[]{:S(2)}) collective-permute-start(f32[8,416,16]{1,0,2:T(8,128)} %subtract_select_fusion), channel_id=1, source_target_pairs={{0,8},{1,9},{2,10},{3,11},{4,12},{5,13},{6,14},{7,15},{8,0},{9,1},... | collective-permute-start | bytes 638984 | tf_op jit(solution)/shard_map/ppermute | solution.py:17
where the time goes:
time: 582 us; the launch traced here: 578 us
  local copies, waits for them, and re-layouts  302 us (52%)
  other arithmetic  182 us (31%)
  blocking collectives  62.9 us (11%)
  matrix products  21.9 us (4%)
  starting transfers between devices  7.64 us (1%)
    convert_element_type x2, local copies, waits for them, and re-layouts, dequantize(): return ((unpacked - 8).astype(jnp.float32) * spread).astype(jnp.bfloat16)  300 us
    convert_element_type x2, other arithmetic, dequantize(): return ((unpacked - 8).astype(jnp.float32) * spread).astype(jnp.bfloat16)  123 us
    unnamed x1, blocking collectives  62.9 us
    another operation x1, other arithmetic, dequantize(): jnp.stack([low_codes, high_codes], axis=1)  53.2 us
    dot_general x1, matrix products, body(): lax.dot_general(rotated, weight, (((0,), (0,)), ((), ())), preferred_elem...  20.3 us
  transfers between devices with their start and end apart: 4, of which 1 were waited for; matrix products, arithmetic and copies ran while one was open for 83% of the time, Pallas kernels for 0%

commit v1 on v0

--- a/solution.py
+++ b/solution.py
@@ -1,20 +1,21 @@
+import functools
 import math
 
 import jax
 import jax.numpy as jnp
 import numpy as np
 from jax import lax
+from jax.experimental import pallas as pl
+from jax.experimental.pallas import tpu as pltpu
 from jax.sharding import PartitionSpec as P
 
 HAD_CROSS = 128
 GROUP = 32
 HAD_LOCAL = 416
-
-
-def swapped(value, axis, distance):
-    mask = 2**distance
-    pairs = [(source, source ^ mask) for source in range(lax.axis_size(axis))]
-    return lax.ppermute(value, axis, pairs)
+PAIRS = HAD_LOCAL // 2
+WORDS_PER_GROUP = GROUP // 2
+AXES = ("groups", "tensor")
+MIB = 2**20
 
 
 def paley_table():
@@ -53,18 +54,22 @@
     return matrix
 
 
+def local_matrix(order):
+    return np.kron(walsh_table(order // 52), paley_table()) / math.sqrt(order)
+
+
 def hadamard_local(order):
-    matrix = np.kron(walsh_table(order // 52), paley_table()) / math.sqrt(order)
-    return jnp.asarray(matrix, dtype=jnp.float32).astype(jnp.bfloat16)
+    return jnp.asarray(local_matrix(order), dtype=jnp.float32).astype(jnp.bfloat16)
 
 
 def sign_table(order):
-    row_index = jnp.arange(order, dtype=jnp.int32)[:, None]
-    col_index = jnp.arange(order, dtype=jnp.int32)[None, :]
-    shared = jnp.zeros((order, order), jnp.int32)
-    for bit_pos in range(order.bit_length() - 1):
-        shared = shared + row_index // 2**bit_pos % 2 * (col_index // 2**bit_pos % 2)
-    return (1 - 2 * (shared % 2)).astype(jnp.float32)
+    return jnp.asarray(walsh_table(order), dtype=jnp.float32)
+
+
+def swapped(value, axis, distance):
+    mask = 2**distance
+    pairs = [(source, source ^ mask) for source in range(lax.axis_size(axis))]
+    return lax.ppermute(value, axis, pairs)
 
 
 def dequantize(words, group_scales):
@@ -77,7 +82,7 @@
     return ((unpacked - 8).astype(jnp.float32) * spread).astype(jnp.bfloat16)
 
 
-def body(gate_act, up_act, codes, scales):
+def general_body(gate_act, up_act, codes, scales):
     units_here = gate_act.shape[0]
     total_rows = gate_act.shape[1]
     blocks_here = units_here // HAD_LOCAL
@@ -86,9 +91,8 @@
         jnp.bfloat16
     )
     hidden = hidden.reshape(blocks_here, HAD_LOCAL, total_rows)
-    local_table = hadamard_local(HAD_LOCAL)
     local = jnp.einsum(
-        "kn,anr->akr", local_table, hidden, preferred_element_type=jnp.float32
+        "kn,anr->akr", hadamard_local(HAD_LOCAL), hidden, preferred_element_type=jnp.float32
     ).astype(jnp.bfloat16)
     partial_sums = jnp.einsum(
         "abr,ae->ebr",
@@ -115,6 +119,255 @@
     return summed.astype(jnp.bfloat16)
 
 
+def exchanged(value, group_mask, tensor_mask):
+    tensor_size = lax.axis_size("tensor")
+    pairs = [
+        (g * tensor_size + t, (g ^ group_mask) * tensor_size + (t ^ tensor_mask))
+        for g in range(lax.axis_size("groups"))
+        for t in range(tensor_size)
+    ]
+    return lax.ppermute(value, AXES, pairs)
+
+
+def parity_sign(bits, masks):
+    total = jnp.int32(0)
+    position = 1
+    while position <= masks:
+        if masks & position:
+            total = total + bits // position % 2
+        position *= 2
+    return (1 - 2 * (total % 2)).astype(jnp.float32)
+
+
+def local_kernel(group_ref, gate_ref, up_ref, table_ref, walsh_ref, out_ref, gate_sc, up_sc, mix_sc):
+    rows = gate_ref.shape[1]
+    blocks = gate_ref.shape[0] // HAD_LOCAL
+    half = blocks // 2
+    for a in range(blocks):
+        here = slice(a * HAD_LOCAL, (a + 1) * HAD_LOCAL)
+        there = slice(a * rows, (a + 1) * rows)
+        gate_sc[:, there] = gate_ref[here, :].astype(jnp.float32)
+        up_sc[:, there] = up_ref[here, :].astype(jnp.float32)
+    gate = gate_sc[...]
+    hidden = (gate / (1.0 + jnp.exp(-gate)) * up_sc[...]).astype(jnp.bfloat16)
+    local = lax.dot_general(
+        hidden, table_ref[...], (((0,), (0,)), ((), ())), preferred_element_type=jnp.float32
+    ).astype(jnp.bfloat16)
+    mix_sc[...] = jnp.dot(walsh_ref[...], local, preferred_element_type=jnp.float32).astype(
+        jnp.bfloat16
+    )
+    padded = table_ref.shape[1] // 2
+    group = group_ref[0]
+    for part in range(2):
+        first = (group if part == 0 else 1 - group) * half
+        for parity in range(2):
+            for e in range(half):
+                start = pl.multiple_of((first + e) * rows, rows)
+                offset = (parity * half + e) * PAIRS
+                out_ref[part, :, offset : offset + PAIRS] = mix_sc[
+                    pl.ds(start, rows), parity * padded : parity * padded + PAIRS
+                ]
+
+
+def local_rotation(group, gate_act, up_act):
+    units, rows = gate_act.shape
+    blocks = units // HAD_LOCAL
+    padded = -(-PAIRS // 128) * 128
+    by_parity = local_matrix(HAD_LOCAL).reshape(PAIRS, 2, HAD_LOCAL)
+    table = np.zeros((HAD_LOCAL, 2 * padded), np.float32)
+    table[:, :PAIRS] = by_parity[:, 0].T
+    table[:, padded : padded + PAIRS] = by_parity[:, 1].T
+    walsh = np.kron(walsh_table(blocks), np.eye(rows))
+    whole = pl.BlockSpec(memory_space=pltpu.VMEM)
+    return pl.pallas_call(
+        local_kernel,
+        in_specs=[pl.BlockSpec(memory_space=pltpu.SMEM)] + [whole] * 4,
+        out_specs=whole,
+        out_shape=jax.ShapeDtypeStruct((2, rows, units // 2), jnp.bfloat16),
+        scratch_shapes=[
+            pltpu.VMEM((HAD_LOCAL, blocks * rows), jnp.float32),
+            pltpu.VMEM((HAD_LOCAL, blocks * rows), jnp.float32),
+            pltpu.VMEM((blocks * rows, 2 * padded), jnp.bfloat16),
+        ],
+        compiler_params=pltpu.CompilerParams(vmem_limit_bytes=8 * MIB),
+        cost_estimate=pl.CostEstimate(flops=10**8, bytes_accessed=2 * MIB, transcendentals=10**5),
+        name="local_rotation",
+    )(
+        group,
+        gate_act,
+        up_act,
+        jnp.asarray(table, jnp.bfloat16),
+        jnp.asarray(walsh, jnp.bfloat16),
+    )
+
+
+def unpack_kernel(tile, group_ref, codes_ref, scales_ref, out_ref, scales_sc):
+    step = pl.program_id(0)
+    rows, columns = codes_ref.shape
+    steps = pl.num_programs(0)
+    spans = rows // WORDS_PER_GROUP
+    plane = out_ref.shape[0] // 2
+
+    @pl.when(step == 0)
+    def _():
+        scales_sc[...] = scales_ref[...].astype(jnp.float32)
+
+    first = (group_ref[0] * steps + step) * spans
+    for p in range(spans):
+        for q in range(0, columns, tile):
+            words = codes_ref[p * WORDS_PER_GROUP : (p + 1) * WORDS_PER_GROUP, q : q + tile]
+            scale = scales_sc[pl.ds(first + p, 1), q : q + tile]
+            low = ((words & 15) - 8).astype(jnp.float32) * scale
+            high = ((words >> 4) - 8).astype(jnp.float32) * scale
+            at = pl.multiple_of(step * rows + p * WORDS_PER_GROUP, WORDS_PER_GROUP)
+            out_ref[pl.ds(at, WORDS_PER_GROUP), q : q + tile] = low.astype(jnp.bfloat16)
+            at = pl.multiple_of(plane + step * rows + p * WORDS_PER_GROUP, WORDS_PER_GROUP)
+            out_ref[pl.ds(at, WORDS_PER_GROUP), q : q + tile] = high.astype(jnp.bfloat16)
+
+
+def unpack(group, codes, scales, chunk, columns):
+    words = codes.shape[0]
+    steps = words // PAIRS // 2
+    return pl.pallas_call(
+        functools.partial(unpack_kernel, 512),
+        grid_spec=pltpu.PrefetchScalarGridSpec(
+            num_scalar_prefetch=1,
+            grid=(steps,),
+            in_specs=[
+                pl.BlockSpec((PAIRS, columns), lambda i, g: (g[0] * steps + i, chunk)),
+                pl.BlockSpec((scales.shape[0], columns), lambda i, g: (0, chunk)),
+            ],
+            out_specs=pl.BlockSpec(memory_space=pltpu.VMEM),
+            scratch_shapes=[pltpu.VMEM((scales.shape[0], columns), jnp.float32)],
+        ),
+        out_shape=pltpu.VMEM((words, columns), jnp.bfloat16),
+        compiler_params=pltpu.CompilerParams(vmem_limit_bytes=12 * MIB),
+        cost_estimate=pl.CostEstimate(
+            flops=words * columns * 8, bytes_accessed=words * columns * 4, transcendentals=0
+        ),
+        name=f"unpack_{chunk}",
+    )(group, codes, scales)
+
+
+def product_kernel(tile, chunks, place_ref, own_ref, *refs):
+    others = refs[: len(refs) - chunks - 2]
+    weights = refs[len(others) : len(others) + chunks]
+    keep_ref, send_ref = refs[-2:]
+    rows = own_ref.shape[0]
+    place = place_ref[0]
+    count = len(others) + 1
+    far = 4 * (count - 1)
+    total = own_ref[...].astype(jnp.float32) * parity_sign(place, far)
+    for index, other in enumerate(others):
+        total = total + other[...].astype(jnp.float32) * parity_sign(
+            place & (place ^ (4 * (index + 1))), far
+        )
+    rotated = (total * (1.0 / math.sqrt(HAD_CROSS))).astype(jnp.bfloat16)
+    each = rows // (8 * count)
+    slot = lax.broadcasted_iota(jnp.int32, (rows, rows), 0)
+    column = lax.broadcasted_iota(jnp.int32, (rows, rows), 1)
+    unit = slot // each
+    away = unit // (4 * count) + 2 * (unit // count % 2) + 4 * (unit % count)
+    source = (unit // (2 * count) % 2) * (rows // 2) + (away ^ place) * each + slot % each
+    pick = (column == source).astype(jnp.float32).astype(jnp.bfloat16)
+    rotated = jnp.dot(pick, rotated, preferred_element_type=jnp.float32).astype(jnp.bfloat16)
+    for index, weight in enumerate(weights):
+        columns = weight.shape[1]
+
+        @pl.loop(0, columns // tile)
+        def _(i, weight=weight, index=index, columns=columns):
+            at = pl.multiple_of(i * tile, tile)
+            result = jnp.dot(
+                rotated, weight[:, pl.ds(at, tile)], preferred_element_type=jnp.float32
+            )
+            to = pl.ds(pl.multiple_of(index * columns + at, tile), tile)
+            keep_ref[:, to] = result[: rows // 2]
+            send_ref[:, to] = result[rows // 2 :].astype(jnp.bfloat16)
+
+
+def product(place, own, others, weights):
+    rows = own.shape[0]
+    width = sum(w.shape[1] for w in weights)
+    whole = pl.BlockSpec(memory_space=pltpu.VMEM)
+    weights = [pltpu.with_memory_space_constraint(w, pltpu.VMEM) for w in weights]
+    return pl.pallas_call(
+        functools.partial(product_kernel, 512, len(weights)),
+        in_specs=[pl.BlockSpec(memory_space=pltpu.SMEM)]
+        + [whole] * (1 + len(others) + len(weights)),
+        out_specs=[whole, whole],
+        out_shape=[
+            jax.ShapeDtypeStruct((rows // 2, width), jnp.float32),
+            jax.ShapeDtypeStruct((rows // 2, width), jnp.bfloat16),
+        ],
+        compiler_params=pltpu.CompilerParams(vmem_limit_bytes=8 * MIB),
+        name="product",
+    )(place, own, *others, *weights)
+
+
+def shared_body(gate_act, up_act, codes, scales):
+    rows = gate_act.shape[1]
+    width = codes.shape[1]
+    tensor_size = lax.axis_size("tensor")
+    count = tensor_size // 4
+    each = rows // tensor_size
+    group = lax.axis_index("groups").astype(jnp.int32)[None]
+    place = lax.axis_index("tensor").astype(jnp.int32)[None]
+
+    parts = local_rotation(group, gate_act, up_act)
+    near = exchanged(parts, 0, 1)
+    chunks = 4
+    weights = [unpack(group, codes, scales, c, width // chunks) for c in range(chunks)]
+    core = place[0] % 2
+    parts = jnp.where(
+        core == 0,
+        parts.astype(jnp.float32) + near.astype(jnp.float32),
+        near.astype(jnp.float32) - parts.astype(jnp.float32),
+    ).astype(jnp.bfloat16)
+    mine, theirs = parts[0], parts[1]
+    across_y = exchanged(mine, 0, 2).astype(jnp.float32)
+    across_x = exchanged(theirs, 1, 0).astype(jnp.float32)
+    across_xy = exchanged(theirs, 1, 2).astype(jnp.float32)
+    low = place[0] // 2 % 2 == 0
+    here = mine.astype(jnp.float32)
+    both = jnp.concatenate(
+        [
+            jnp.where(low, here + across_y, across_y - here),
+            jnp.where(low, across_x + across_xy, across_xy - across_x),
+        ]
+    ).astype(jnp.bfloat16)
+    others = [exchanged(both, 0, 4 * d) for d in range(1, count)]
+    keep, send = product(place, both, others, weights)
+
+    keep = keep + exchanged(send, 0, 1).astype(jnp.float32)
+    quarters = keep.reshape(4, count * each, width)
+    send = quarters[1:].astype(jnp.bfloat16)
+    keep = (
+        quarters[0]
+        + exchanged(send[0], 0, 2).astype(jnp.float32)
+        + exchanged(send[1], 1, 0).astype(jnp.float32)
+        + exchanged(send[2], 1, 2).astype(jnp.float32)
+    )
+    send = keep.astype(jnp.bfloat16)
+    total = keep[:each]
+    for d in range(1, count):
+        total = total + exchanged(send[d * each : (d + 1) * each], 0, 4 * d).astype(jnp.float32)
+    return total.astype(jnp.bfloat16)
+
+
+def body(gate_act, up_act, codes, scales):
+    tensor_size = lax.axis_size("tensor")
+    blocks = gate_act.shape[0] // HAD_LOCAL
+    if (
+        lax.axis_size("groups") == 2
+        and tensor_size >= 4
+        and blocks % 2 == 0
+        and gate_act.shape[1] % tensor_size == 0
+        and blocks * gate_act.shape[1] <= 128
+    ):
+        return shared_body(gate_act, up_act, codes, scales)
+    return general_body(gate_act, up_act, codes, scales)
+
+
 def solution(mesh):
     placed = (P("tensor", "groups"), P("tensor", "groups"), P("tensor", None), P("tensor", None))
     return jax.shard_map(

time: 582 us -> 66.3 us (0.11)
  local copies, waits for them, and re-layouts: 302 us -> 6.03 us
  other arithmetic: 182 us -> 0.92 us
  blocking collectives: 62.9 us -> 0 us
  Pallas kernels: 0 us -> 27.2 us
  matrix products: 21.9 us -> 0 us
  waiting for transfers between devices: 1.17 us -> 14.3 us
  starting transfers between devices: 7.64 us -> 17.3 us
    convert_element_type x3 -> x0, local copies, waits for them, and re-layouts: 302 us -> none  [the longest x2 300 us: dequantize(): return ((unpacked - 8).astype(jnp.float32) * spread).astype(jnp.bfloat16)]
    convert_element_type x5 -> x3, other arithmetic: 126 us -> 0.81 us  [the longest x1 0.7 us: shared_body(): return total.astype(jnp.bfloat16)]
    unnamed x1 -> x0, blocking collectives: 62.9 us -> none
    another operation x1 -> x3, other arithmetic: 53.2 us -> 0.1 us  [dequantize(): jnp.stack([low_codes, high_codes], axis=1)]
    pallas_call x0 -> x6, Pallas kernels: none -> 27.2 us  [the longest x4 19.5 us: unpack(): pl.pallas_call(functools.partial(unpack_kernel, 512), grid_spec=pltpu.Pre...]
    dot_general x3 -> x0, matrix products: 21.9 us -> none  [the longest x1 20.3 us: body(): lax.dot_general(rotated, weight, (((0,), (0,)), ((), ())), preferred_elem...]
    ppermute x4 -> x14, waiting for transfers between devices: 1.17 us -> 14.3 us  [exchanged(): return lax.ppermute(value, AXES, pairs)]
    ppermute x4 -> x14, starting transfers between devices: 7.64 us -> 17.3 us  [exchanged(): return lax.ppermute(value, AXES, pairs)]
  transfers between devices with their start and end apart: 4 -> 14, of which waited for: 1 -> 9; matrix products, arithmetic and copies ran while one was open for 83% -> 0% of each run, Pallas kernels for 0% -> 30%
where the time goes in v1:
time: 66.3 us; the launch traced here: 65.9 us
  Pallas kernels  27.2 us (41%)
  starting transfers between devices  17.3 us (26%)
  waiting for transfers between devices  14.3 us (22%)
  local copies, waits for them, and re-layouts  6.03 us (9%)
  other arithmetic  0.92 us (1%)
    pallas_call x4, Pallas kernels, unpack(): pl.pallas_call(functools.partial(unpack_kernel, 512), grid_spec=pltpu.Pre...  19.5 us
    ppermute x14, starting transfers between devices, exchanged(): return lax.ppermute(value, AXES, pairs)  17.3 us
    ppermute x14, waiting for transfers between devices, exchanged(): return lax.ppermute(value, AXES, pairs)  14.3 us
    pallas_call x1, Pallas kernels, product(): pl.pallas_call(functools.partial(product_kernel, 512, len(weights)), in_s...  6.79 us
    unnamed x8, local copies, waits for them, and re-layouts  5.85 us
  transfers between devices with their start and end apart: 14, of which 9 were waited for; matrix products, arithmetic and copies ran while one was open for 0% of the time, Pallas kernels for 30%

profile of v1, /device:TPU:0, one launch (start us, length us, event | category | flops | bytes accessed | tf_op | source)
XLA Modules:
  0.0 65.9 jit_solution(24386248195970169)
XLA Ops:
  0.0 1.3 %copy.7.gate_ref = bf16[3328,16]{1,0:T(8,128)(2,1)S(1)} copy(bf16[3328,16]{0,1:T(8,128)(2,1)} %param.6) | data formatting | bytes 212992 | tf_op args[0]
  1.3 1.3 %copy.8.up_ref = bf16[3328,16]{1,0:T(8,128)(2,1)S(1)} copy(bf16[3328,16]{0,1:T(8,128)(2,1)} %param.7) | data formatting | bytes 212992 | tf_op args[1]
  2.7 1.0 %copy-done.1 = bf16[416,512]{1,0:T(8,128)(2,1)S(1)} copy-done((bf16[416,512]{1,0:T(8,128)(2,1)S(1)}, bf16[416,512]{1,0:T(8,128)(2,1)}, u32[]{:S(2)}) %copy-start.1) | copy-done | bytes 426008
  4.4 0.9 %local_rotation.1 = bf16[2,16,1664]{2,1,0:T(8,128)(2,1)S(1)} custom-call(s32[1]{0:T(128)} %bitcast.1.group_ref, bf16[3328,16]{1,0:T(8,128)(2,1)S(1)} %copy.7.gate_ref, bf16[3328,16]{1,0:T(8,128)(2,1)S(1)} %copy.8.up_ref, bf16[416,512]{1,0:T(8,128)(2,1)S(1)} %copy-done.1, bf16[128,128]{1,0:T(8,128)(2,1)S(1)} %copy-done.2), custom_call_target="tpu_custom_call" | custom-call | flops 100000000 | bytes 2097152 | tf_op jit(solution)/shard_map/local_rotation/pallas_call | solution.py:182
  5.9 1.0 %collective-permute-done = bf16[2,16,1664]{2,1,0:T(8,128)(2,1)S(1)} collective-permute-done((bf16[2,16,1664]{2,1,0:T(8,128)(2,1)S(1)}, bf16[2,16,1664]{2,1,0:T(8,128)(2,1)S(1)}, u32[]{:S(2)}, u32[]{:S(2)}) %collective-permute-start) | collective-permute-done | bytes 106528 | tf_op jit(solution)/shard_map/ppermute | solution.py:129
  6.9 2.9 %collective-permute-start.1 = (bf16[16,1664]{1,0:T(8,128)(2,1)S(1)}, bf16[16,1664]{1,0:T(8,128)(2,1)S(1)}, u32[]{:S(2)}, u32[]{:S(2)}) collective-permute-start(bf16[16,1664]{1,0:T(8,128)(2,1)S(1)} %get-tuple-element.16), channel_id=1, source_target_pairs={{0,2},{1,3},{2,0},{3,1},{4,6},{5,7},{6,4},{7,5},{8,10},{9,11},{10,... | collective-permute-start | bytes 159752 | tf_op jit(solution)/shard_map/ppermute | solution.py:129
  9.8 1.4 %collective-permute-start.3 = (bf16[16,1664]{1,0:T(8,128)(2,1)S(1)}, bf16[16,1664]{1,0:T(8,128)(2,1)S(1)}, u32[]{:S(2)}, u32[]{:S(2)}) collective-permute-start(bf16[16,1664]{1,0:T(8,128)(2,1)S(1)} %get-tuple-element.17), channel_id=1, source_target_pairs={{0,18},{1,19},{2,16},{3,17},{4,22},{5,23},{6,20},{7,21},{8,26},{9,... | collective-permute-start | bytes 159752 | tf_op jit(solution)/shard_map/ppermute | solution.py:129
  12.1 3.2 %collective-permute-done.3 = bf16[16,1664]{1,0:T(8,128)(2,1)S(1)} collective-permute-done((bf16[16,1664]{1,0:T(8,128)(2,1)S(1)}, bf16[16,1664]{1,0:T(8,128)(2,1)S(1)}, u32[]{:S(2)}, u32[]{:S(2)}) %collective-permute-start.3) | collective-permute-done | bytes 53280 | tf_op jit(solution)/shard_map/ppermute | solution.py:129
  15.5 3.7 %collective-permute-start.6 = (bf16[32,1664]{1,0:T(8,128)(2,1)S(1)}, bf16[32,1664]{1,0:T(8,128)(2,1)S(1)}, u32[]{:S(2)}, u32[]{:S(2)}) collective-permute-start(bf16[32,1664]{1,0:T(8,128)(2,1)S(1)} %pad_maximum_fusion.own_ref), channel_id=1, source_target_pairs={{0,12},{1,13},{2,14},{3,15},{4,8},{5,9},{6,10},{7,11},{8,4},{9,5},... | collective-permute-start | bytes 319496 | tf_op jit(solution)/shard_map/ppermute | solution.py:129
  19.9 1.5 %copy-done = bf16[104,8192]{1,0:T(8,128)(2,1)S(1)} copy-done((bf16[104,8192]{1,0:T(8,128)(2,1)S(1)}, bf16[104,8192]{1,0:T(8,128)(2,1)}, u32[]{:S(2)}) %copy-start) | copy-done | bytes 1703960
  21.4 4.9 %unpack_1.1.refs_4_ = bf16[1664,2048]{1,0:T(8,128)(2,1)S(1)} custom-call(s32[1]{0:T(128)} %bitcast.1.group_ref, s32[1664,8192]{1,0:T(8,128)} %codes_ref.7, bf16[104,8192]{1,0:T(8,128)(2,1)S(1)} %copy-done), custom_call_target="tpu_custom_call" | custom-call | flops 27262976 | bytes 13631488 | tf_op jit(solution)/shard_map/unpack_1/pallas_call | solution.py:231
  26.2 4.9 %unpack_0.1.refs_3_ = bf16[1664,2048]{1,0:T(8,128)(2,1)S(1)} custom-call(s32[1]{0:T(128)} %bitcast.1.group_ref, s32[1664,8192]{1,0:T(8,128)} %codes_ref.7, bf16[104,8192]{1,0:T(8,128)(2,1)S(1)} %copy-done), custom_call_target="tpu_custom_call" | custom-call | flops 27262976 | bytes 13631488 | tf_op jit(solution)/shard_map/unpack_0/pallas_call | solution.py:231
  31.1 4.9 %unpack_3.1.refs_6_ = bf16[1664,2048]{1,0:T(8,128)(2,1)S(1)} custom-call(s32[1]{0:T(128)} %bitcast.1.group_ref, s32[1664,8192]{1,0:T(8,128)} %codes_ref.7, bf16[104,8192]{1,0:T(8,128)(2,1)S(1)} %copy-done), custom_call_target="tpu_custom_call" | custom-call | flops 27262976 | bytes 13631488 | tf_op jit(solution)/shard_map/unpack_3/pallas_call | solution.py:231
  36.0 4.9 %unpack_2.1.refs_5_ = bf16[1664,2048]{1,0:T(8,128)(2,1)S(1)} custom-call(s32[1]{0:T(128)} %bitcast.1.group_ref, s32[1664,8192]{1,0:T(8,128)} %codes_ref.7, bf16[104,8192]{1,0:T(8,128)(2,1)S(1)} %copy-done), custom_call_target="tpu_custom_call" | custom-call | flops 27262976 | bytes 13631488 | tf_op jit(solution)/shard_map/unpack_2/pallas_call | solution.py:231
  40.9 6.8 %product.1 = (f32[16,8192]{1,0:T(8,128)S(1)}, bf16[16,8192]{1,0:T(8,128)(2,1)S(1)}) custom-call(s32[1]{0:T(128)} %bitcast.place_ref, bf16[32,1664]{1,0:T(8,128)(2,1)S(1)} %pad_maximum_fusion.own_ref, bf16[32,1664]{1,0:T(8,128)(2,1)S(1)} %collective-permute-done.4.refs_0_, bf16[32,1664]{1,0:T(8,128)(2,1)S(1)} %collective-permute-done.5.refs_1_, ...), custom_call_target="tpu_custom_call" | custom-call | tf_op jit(solution)/shard_map/product/pallas_call | solution.py:293
  47.7 1.6 %collective-permute-done.7 = bf16[16,8192]{1,0:T(8,128)(2,1)S(1)} collective-permute-done((bf16[16,8192]{1,0:T(8,128)(2,1)S(1)}, bf16[16,8192]{1,0:T(8,128)(2,1)S(1)}, u32[]{:S(2)}, u32[]{:S(2)}) %collective-permute-start.7) | collective-permute-done | bytes 262176 | tf_op jit(solution)/shard_map/ppermute | solution.py:129
  49.4 1.6 %collective-permute-start.8 = (bf16[4,8192]{1,0:T(4,128)(2,1)S(1)}, bf16[4,8192]{1,0:T(4,128)(2,1)S(1)}, u32[]{:S(2)}, u32[]{:S(2)}) collective-permute-start(bf16[4,8192]{1,0:T(4,128)(2,1)S(1)} %get-tuple-element.13), channel_id=1, source_target_pairs={{0,2},{1,3},{2,0},{3,1},{4,6},{5,7},{6,4},{7,5},{8,10},{9,11},{10,... | collective-permute-start | bytes 196616 | tf_op jit(solution)/shard_map/ppermute | solution.py:129
  51.0 0.9 %collective-permute-start.10 = (bf16[4,8192]{1,0:T(4,128)(2,1)S(1)}, bf16[4,8192]{1,0:T(4,128)(2,1)S(1)}, u32[]{:S(2)}, u32[]{:S(2)}) collective-permute-start(bf16[4,8192]{1,0:T(4,128)(2,1)S(1)} %get-tuple-element.14), channel_id=1, source_target_pairs={{0,18},{1,19},{2,16},{3,17},{4,22},{5,23},{6,20},{7,21},{8,26},{9,... | collective-permute-start | bytes 196616 | tf_op jit(solution)/shard_map/ppermute | solution.py:129
  52.0 1.0 %collective-permute-start.9 = (bf16[4,8192]{1,0:T(4,128)(2,1)S(1)}, bf16[4,8192]{1,0:T(4,128)(2,1)S(1)}, u32[]{:S(2)}, u32[]{:S(2)}) collective-permute-start(bf16[4,8192]{1,0:T(4,128)(2,1)S(1)} %get-tuple-element.15), channel_id=1, source_target_pairs={{0,16},{1,17},{2,18},{3,19},{4,20},{5,21},{6,22},{7,23},{8,24},{9,... | collective-permute-start | bytes 196616 | tf_op jit(solution)/shard_map/ppermute | solution.py:129
  53.8 2.7 %collective-permute-done.10 = bf16[4,8192]{1,0:T(4,128)(2,1)S(1)} collective-permute-done((bf16[4,8192]{1,0:T(4,128)(2,1)S(1)}, bf16[4,8192]{1,0:T(4,128)(2,1)S(1)}, u32[]{:S(2)}, u32[]{:S(2)}) %collective-permute-start.10) | collective-permute-done | bytes 65568 | tf_op jit(solution)/shard_map/ppermute | solution.py:129
  56.6 1.3 %collective-permute-start.11 = (bf16[1,8192]{1,0:T(2,128)(2,1)S(1)}, bf16[1,8192]{1,0:T(2,128)(2,1)S(1)}, u32[]{:S(2)}, u32[]{:S(2)}) collective-permute-start(bf16[1,8192]{1,0:T(2,128)(2,1)S(1)} %get-tuple-element.18), channel_id=1, source_target_pairs={{0,4},{1,5},{2,6},{3,7},{4,0},{5,1},{6,2},{7,3},{8,12},{9,13},{10,... | collective-permute-start | bytes 49160 | tf_op jit(solution)/shard_map/ppermute | solution.py:129
  58.0 2.4 %collective-permute-start.13 = (bf16[1,8192]{1,0:T(2,128)(2,1)S(1)}, bf16[1,8192]{1,0:T(2,128)(2,1)S(1)}, u32[]{:S(2)}, u32[]{:S(2)}) collective-permute-start(bf16[1,8192]{1,0:T(2,128)(2,1)S(1)} %get-tuple-element.19), channel_id=1, source_target_pairs={{0,12},{1,13},{2,14},{3,15},{4,8},{5,9},{6,10},{7,11},{8,4},{9,5},... | collective-permute-start | bytes 49160 | tf_op jit(solution)/shard_map/ppermute | solution.py:129
  60.9 2.8 %collective-permute-done.13 = bf16[1,8192]{1,0:T(2,128)(2,1)S(1)} collective-permute-done((bf16[1,8192]{1,0:T(2,128)(2,1)S(1)}, bf16[1,8192]{1,0:T(2,128)(2,1)S(1)}, u32[]{:S(2)}, u32[]{:S(2)}) %collective-permute-start.13) | collective-permute-done | bytes 16416 | tf_op jit(solution)/shard_map/ppermute | solution.py:129
  63.7 1.5 %collective-permute-done.12 = bf16[1,8192]{1,0:T(2,128)(2,1)S(1)} collective-permute-done((bf16[1,8192]{1,0:T(2,128)(2,1)S(1)}, bf16[1,8192]{1,0:T(2,128)(2,1)S(1)}, u32[]{:S(2)}, u32[]{:S(2)}) %collective-permute-start.12) | collective-permute-done | bytes 16416 | tf_op jit(solution)/shard_map/ppermute | solution.py:129
  (28 shorter events, 5.4 us)
Async XLA Ops:
  2.6 1.0 %copy-start.1 = (bf16[416,512]{1,0:T(8,128)(2,1)S(1)}, bf16[416,512]{1,0:T(8,128)(2,1)}, u32[]{:S(2)}) copy-start(bf16[416,512]{1,0:T(8,128)(2,1)} %constant.42.clone.table_ref) | copy-start | bytes 1277956
  3.7 0.8 %copy-start.2 = (bf16[128,128]{1,0:T(8,128)(2,1)S(1)}, bf16[128,128]{1,0:T(8,128)(2,1)}, u32[]{:S(2)}) copy-start(bf16[128,128]{1,0:T(8,128)(2,1)} %constant.43.clone.walsh_ref) | copy-start | bytes 98308
  5.4 1.5 %collective-permute-start = (bf16[2,16,1664]{2,1,0:T(8,128)(2,1)S(1)}, bf16[2,16,1664]{2,1,0:T(8,128)(2,1)S(1)}, u32[]{:S(2)}, u32[]{:S(2)}) collective-permute-start(bf16[2,16,1664]{2,1,0:T(8,128)(2,1)S(1)} %local_rotation.1), channel_id=1, source_target_pairs={{0,1},{1,0},{2,3},{3,2},{4,5},{5,4},{6,7},{7,6},{8,9},{9,8},{10,11... | collective-permute-start | bytes 319496 | tf_op jit(solution)/shard_map/ppermute | solution.py:129
  6.9 5.2 %collective-permute-start.1 = (bf16[16,1664]{1,0:T(8,128)(2,1)S(1)}, bf16[16,1664]{1,0:T(8,128)(2,1)S(1)}, u32[]{:S(2)}, u32[]{:S(2)}) collective-permute-start(bf16[16,1664]{1,0:T(8,128)(2,1)S(1)} %get-tuple-element.16), channel_id=1, source_target_pairs={{0,2},{1,3},{2,0},{3,1},{4,6},{5,7},{6,4},{7,5},{8,10},{9,11},{10,... | collective-permute-start | bytes 159752 | tf_op jit(solution)/shard_map/ppermute | solution.py:129
  9.8 5.5 %collective-permute-start.3 = (bf16[16,1664]{1,0:T(8,128)(2,1)S(1)}, bf16[16,1664]{1,0:T(8,128)(2,1)S(1)}, u32[]{:S(2)}, u32[]{:S(2)}) collective-permute-start(bf16[16,1664]{1,0:T(8,128)(2,1)S(1)} %get-tuple-element.17), channel_id=1, source_target_pairs={{0,18},{1,19},{2,16},{3,17},{4,22},{5,23},{6,20},{7,21},{8,26},{9,... | collective-permute-start | bytes 159752 | tf_op jit(solution)/shard_map/ppermute | solution.py:129
  11.3 4.1 %collective-permute-start.2 = (bf16[16,1664]{1,0:T(8,128)(2,1)S(1)}, bf16[16,1664]{1,0:T(8,128)(2,1)S(1)}, u32[]{:S(2)}, u32[]{:S(2)}) collective-permute-start(bf16[16,1664]{1,0:T(8,128)(2,1)S(1)} %get-tuple-element.17), channel_id=1, source_target_pairs={{0,16},{1,17},{2,18},{3,19},{4,20},{5,21},{6,22},{7,23},{8,24},{9,... | collective-permute-start | bytes 159752 | tf_op jit(solution)/shard_map/ppermute | solution.py:129
  15.5 25.4 %collective-permute-start.6 = (bf16[32,1664]{1,0:T(8,128)(2,1)S(1)}, bf16[32,1664]{1,0:T(8,128)(2,1)S(1)}, u32[]{:S(2)}, u32[]{:S(2)}) collective-permute-start(bf16[32,1664]{1,0:T(8,128)(2,1)S(1)} %pad_maximum_fusion.own_ref), channel_id=1, source_target_pairs={{0,12},{1,13},{2,14},{3,15},{4,8},{5,9},{6,10},{7,11},{8,4},{9,5},... | collective-permute-start | bytes 319496 | tf_op jit(solution)/shard_map/ppermute | solution.py:129
  19.1 21.8 %collective-permute-start.5 = (bf16[32,1664]{1,0:T(8,128)(2,1)S(1)}, bf16[32,1664]{1,0:T(8,128)(2,1)S(1)}, u32[]{:S(2)}, u32[]{:S(2)}) collective-permute-start(bf16[32,1664]{1,0:T(8,128)(2,1)S(1)} %pad_maximum_fusion.own_ref), channel_id=1, source_target_pairs={{0,8},{1,9},{2,10},{3,11},{4,12},{5,13},{6,14},{7,15},{8,0},{9,1},... | collective-permute-start | bytes 319496 | tf_op jit(solution)/shard_map/ppermute | solution.py:129
  19.1 21.8 %collective-permute-start.4 = (bf16[32,1664]{1,0:T(8,128)(2,1)S(1)}, bf16[32,1664]{1,0:T(8,128)(2,1)S(1)}, u32[]{:S(2)}, u32[]{:S(2)}) collective-permute-start(bf16[32,1664]{1,0:T(8,128)(2,1)S(1)} %pad_maximum_fusion.own_ref), channel_id=1, source_target_pairs={{0,4},{1,5},{2,6},{3,7},{4,0},{5,1},{6,2},{7,3},{8,12},{9,13},{10,... | collective-permute-start | bytes 319496 | tf_op jit(solution)/shard_map/ppermute | solution.py:129
  19.9 1.5 %copy-start = (bf16[104,8192]{1,0:T(8,128)(2,1)S(1)}, bf16[104,8192]{1,0:T(8,128)(2,1)}, u32[]{:S(2)}) copy-start(bf16[104,8192]{1,0:T(8,128)(2,1)} %scales_ref.7) | copy-start | bytes 5111812
  47.7 1.6 %collective-permute-start.7 = (bf16[16,8192]{1,0:T(8,128)(2,1)S(1)}, bf16[16,8192]{1,0:T(8,128)(2,1)S(1)}, u32[]{:S(2)}, u32[]{:S(2)}) collective-permute-start(bf16[16,8192]{1,0:T(8,128)(2,1)S(1)} %get-tuple-element.8), channel_id=1, source_target_pairs={{0,1},{1,0},{2,3},{3,2},{4,5},{5,4},{6,7},{7,6},{8,9},{9,8},{10,11... | collective-permute-start | bytes 786440 | tf_op jit(solution)/shard_map/ppermute | solution.py:129
  49.4 4.3 %collective-permute-start.8 = (bf16[4,8192]{1,0:T(4,128)(2,1)S(1)}, bf16[4,8192]{1,0:T(4,128)(2,1)S(1)}, u32[]{:S(2)}, u32[]{:S(2)}) collective-permute-start(bf16[4,8192]{1,0:T(4,128)(2,1)S(1)} %get-tuple-element.13), channel_id=1, source_target_pairs={{0,2},{1,3},{2,0},{3,1},{4,6},{5,7},{6,4},{7,5},{8,10},{9,11},{10,... | collective-permute-start | bytes 196616 | tf_op jit(solution)/shard_map/ppermute | solution.py:129
  51.0 5.5 %collective-permute-start.10 = (bf16[4,8192]{1,0:T(4,128)(2,1)S(1)}, bf16[4,8192]{1,0:T(4,128)(2,1)S(1)}, u32[]{:S(2)}, u32[]{:S(2)}) collective-permute-start(bf16[4,8192]{1,0:T(4,128)(2,1)S(1)} %get-tuple-element.14), channel_id=1, source_target_pairs={{0,18},{1,19},{2,16},{3,17},{4,22},{5,23},{6,20},{7,21},{8,26},{9,... | collective-permute-start | bytes 196616 | tf_op jit(solution)/shard_map/ppermute | solution.py:129
  52.0 4.5 %collective-permute-start.9 = (bf16[4,8192]{1,0:T(4,128)(2,1)S(1)}, bf16[4,8192]{1,0:T(4,128)(2,1)S(1)}, u32[]{:S(2)}, u32[]{:S(2)}) collective-permute-start(bf16[4,8192]{1,0:T(4,128)(2,1)S(1)} %get-tuple-element.15), channel_id=1, source_target_pairs={{0,16},{1,17},{2,18},{3,19},{4,20},{5,21},{6,22},{7,23},{8,24},{9,... | collective-permute-start | bytes 196616 | tf_op jit(solution)/shard_map/ppermute | solution.py:129
  56.6 4.2 %collective-permute-start.11 = (bf16[1,8192]{1,0:T(2,128)(2,1)S(1)}, bf16[1,8192]{1,0:T(2,128)(2,1)S(1)}, u32[]{:S(2)}, u32[]{:S(2)}) collective-permute-start(bf16[1,8192]{1,0:T(2,128)(2,1)S(1)} %get-tuple-element.18), channel_id=1, source_target_pairs={{0,4},{1,5},{2,6},{3,7},{4,0},{5,1},{6,2},{7,3},{8,12},{9,13},{10,... | collective-permute-start | bytes 49160 | tf_op jit(solution)/shard_map/ppermute | solution.py:129
  58.0 5.7 %collective-permute-start.13 = (bf16[1,8192]{1,0:T(2,128)(2,1)S(1)}, bf16[1,8192]{1,0:T(2,128)(2,1)S(1)}, u32[]{:S(2)}, u32[]{:S(2)}) collective-permute-start(bf16[1,8192]{1,0:T(2,128)(2,1)S(1)} %get-tuple-element.19), channel_id=1, source_target_pairs={{0,12},{1,13},{2,14},{3,15},{4,8},{5,9},{6,10},{7,11},{8,4},{9,5},... | collective-permute-start | bytes 49160 | tf_op jit(solution)/shard_map/ppermute | solution.py:129
  60.4 4.8 %collective-permute-start.12 = (bf16[1,8192]{1,0:T(2,128)(2,1)S(1)}, bf16[1,8192]{1,0:T(2,128)(2,1)S(1)}, u32[]{:S(2)}, u32[]{:S(2)}) collective-permute-start(bf16[1,8192]{1,0:T(2,128)(2,1)S(1)} %get-tuple-element.20), channel_id=1, source_target_pairs={{0,8},{1,9},{2,10},{3,11},{4,12},{5,13},{6,14},{7,15},{8,0},{9,1},... | collective-permute-start | bytes 49160 | tf_op jit(solution)/shard_map/ppermute | solution.py:129

commit v2 on v1

--- a/solution.py
+++ b/solution.py
@@ -16,6 +16,8 @@
 WORDS_PER_GROUP = GROUP // 2
 AXES = ("groups", "tensor")
 MIB = 2**20
+TILE = 512
+LANES = 128
 
 
 def paley_table():
@@ -129,6 +131,10 @@
     return lax.ppermute(value, AXES, pairs)
 
 
+def in_hbm(array):
+    return pltpu.with_memory_space_constraint(array, pltpu.HBM)
+
+
 def parity_sign(bits, masks):
     total = jnp.int32(0)
     position = 1
@@ -139,24 +145,49 @@
     return (1 - 2 * (total % 2)).astype(jnp.float32)
 
 
-def local_kernel(group_ref, gate_ref, up_ref, table_ref, walsh_ref, out_ref, gate_sc, up_sc, mix_sc):
-    rows = gate_ref.shape[1]
-    blocks = gate_ref.shape[0] // HAD_LOCAL
+def local_kernel(
+    group_ref, gate_hbm, up_hbm, table_hbm, out_ref, gate_in, up_in, table, hidden_sc, stack_sc, mix_sc, sems
+):
+    copies = [
+        pltpu.make_async_copy(source, target, sems.at[index])
+        for index, (source, target) in enumerate(
+            ((gate_hbm, gate_in), (up_hbm, up_in), (table_hbm, table))
+        )
+    ]
+    for copy in copies:
+        copy.start()
+    rows = gate_in.shape[0]
+    blocks = gate_in.shape[1] // HAD_LOCAL
     half = blocks // 2
+    line = lax.broadcasted_iota(jnp.int32, (blocks * rows, blocks * rows), 0)
+    column = lax.broadcasted_iota(jnp.int32, (blocks * rows, blocks * rows), 1)
+    common = (line // rows) & (column // rows)
+    odd = jnp.zeros_like(common)
+    for bit_pos in range(blocks.bit_length() - 1):
+        odd = odd ^ ((common >> bit_pos) & 1)
+    walsh = jnp.where(line % rows == column % rows, 1 - 2 * odd, 0)
+    walsh = walsh.astype(jnp.float32).astype(jnp.bfloat16)
+    copies[0].wait()
+    copies[1].wait()
+    gate = gate_in[...].astype(jnp.float32)
+    hidden_sc[...] = gate / (1.0 + jnp.exp(-gate)) * up_in[...].astype(jnp.float32)
     for a in range(blocks):
-        here = slice(a * HAD_LOCAL, (a + 1) * HAD_LOCAL)
-        there = slice(a * rows, (a + 1) * rows)
-        gate_sc[:, there] = gate_ref[here, :].astype(jnp.float32)
-        up_sc[:, there] = up_ref[here, :].astype(jnp.float32)
-    gate = gate_sc[...]
-    hidden = (gate / (1.0 + jnp.exp(-gate)) * up_sc[...]).astype(jnp.bfloat16)
-    local = lax.dot_general(
-        hidden, table_ref[...], (((0,), (0,)), ((), ())), preferred_element_type=jnp.float32
-    ).astype(jnp.bfloat16)
-    mix_sc[...] = jnp.dot(walsh_ref[...], local, preferred_element_type=jnp.float32).astype(
-        jnp.bfloat16
-    )
-    padded = table_ref.shape[1] // 2
+        stack_sc[a * rows : (a + 1) * rows, :] = hidden_sc[
+            :, a * HAD_LOCAL : (a + 1) * HAD_LOCAL
+        ].astype(jnp.bfloat16)
+    copies[2].wait()
+    hidden = stack_sc[...]
+    wide = table.shape[0] // HAD_LOCAL
+    for piece in range(wide):
+        local = jnp.dot(
+            hidden,
+            table[piece * HAD_LOCAL : (piece + 1) * HAD_LOCAL, :],
+            preferred_element_type=jnp.float32,
+        ).astype(jnp.bfloat16)
+        mix_sc[:, piece * LANES : (piece + 1) * LANES] = jnp.dot(
+            walsh, local, preferred_element_type=jnp.float32
+        ).astype(jnp.bfloat16)
+    padded = wide * LANES // 2
     group = group_ref[0]
     for part in range(2):
         first = (group if part == 0 else 1 - group) * half
@@ -172,89 +203,127 @@
 def local_rotation(group, gate_act, up_act):
     units, rows = gate_act.shape
     blocks = units // HAD_LOCAL
-    padded = -(-PAIRS // 128) * 128
+    padded = -(-PAIRS // LANES) * LANES
     by_parity = local_matrix(HAD_LOCAL).reshape(PAIRS, 2, HAD_LOCAL)
     table = np.zeros((HAD_LOCAL, 2 * padded), np.float32)
     table[:, :PAIRS] = by_parity[:, 0].T
     table[:, padded : padded + PAIRS] = by_parity[:, 1].T
-    walsh = np.kron(walsh_table(blocks), np.eye(rows))
-    whole = pl.BlockSpec(memory_space=pltpu.VMEM)
+    table = np.concatenate(np.split(table, 2 * padded // LANES, axis=1))
+    hbm = pl.BlockSpec(memory_space=pltpu.HBM)
     return pl.pallas_call(
         local_kernel,
-        in_specs=[pl.BlockSpec(memory_space=pltpu.SMEM)] + [whole] * 4,
-        out_specs=whole,
+        in_specs=[pl.BlockSpec(memory_space=pltpu.SMEM), hbm, hbm, hbm],
+        out_specs=pl.BlockSpec(memory_space=pltpu.VMEM),
         out_shape=jax.ShapeDtypeStruct((2, rows, units // 2), jnp.bfloat16),
         scratch_shapes=[
-            pltpu.VMEM((HAD_LOCAL, blocks * rows), jnp.float32),
-            pltpu.VMEM((HAD_LOCAL, blocks * rows), jnp.float32),
+            pltpu.VMEM((rows, units), jnp.bfloat16),
+            pltpu.VMEM((rows, units), jnp.bfloat16),
+            pltpu.VMEM(table.shape, jnp.bfloat16),
+            pltpu.VMEM((rows, units), jnp.float32),
+            pltpu.VMEM((blocks * rows, HAD_LOCAL), jnp.bfloat16),
             pltpu.VMEM((blocks * rows, 2 * padded), jnp.bfloat16),
+            pltpu.SemaphoreType.DMA((3,)),
         ],
-        compiler_params=pltpu.CompilerParams(vmem_limit_bytes=8 * MIB),
+        compiler_params=pltpu.CompilerParams(vmem_limit_bytes=10 * MIB),
         cost_estimate=pl.CostEstimate(flops=10**8, bytes_accessed=2 * MIB, transcendentals=10**5),
         name="local_rotation",
-    )(
-        group,
-        gate_act,
-        up_act,
-        jnp.asarray(table, jnp.bfloat16),
-        jnp.asarray(walsh, jnp.bfloat16),
-    )
-
-
-def unpack_kernel(tile, group_ref, codes_ref, scales_ref, out_ref, scales_sc):
-    step = pl.program_id(0)
-    rows, columns = codes_ref.shape
-    steps = pl.num_programs(0)
+    )(group, in_hbm(gate_act.T), in_hbm(up_act.T), in_hbm(jnp.asarray(table, jnp.bfloat16)))
+
+
+def unpack_span(words, scale):
+    scale = jnp.broadcast_to(scale, words.shape).astype(jnp.bfloat16)
+    eight = jnp.bfloat16(8)
+    low = (words & 15).astype(jnp.float32).astype(jnp.bfloat16)
+    high = (words >> 4).astype(jnp.float32).astype(jnp.bfloat16)
+    return (low - eight) * scale, (high - eight) * scale
+
+
+def unpack_kernel(tile, group_ref, codes_hbm, scales_hbm, out_ref, rest_ref, words, scales, wide, sems):
+    count, rows, columns = words.shape
     spans = rows // WORDS_PER_GROUP
+    per = count * spans
     plane = out_ref.shape[0] // 2
-
-    @pl.when(step == 0)
-    def _():
-        scales_sc[...] = scales_ref[...].astype(jnp.float32)
-
-    first = (group_ref[0] * steps + step) * spans
-    for p in range(spans):
-        for q in range(0, columns, tile):
-            words = codes_ref[p * WORDS_PER_GROUP : (p + 1) * WORDS_PER_GROUP, q : q + tile]
-            scale = scales_sc[pl.ds(first + p, 1), q : q + tile]
-            low = ((words & 15) - 8).astype(jnp.float32) * scale
-            high = ((words >> 4) - 8).astype(jnp.float32) * scale
-            at = pl.multiple_of(step * rows + p * WORDS_PER_GROUP, WORDS_PER_GROUP)
-            out_ref[pl.ds(at, WORDS_PER_GROUP), q : q + tile] = low.astype(jnp.bfloat16)
-            at = pl.multiple_of(plane + step * rows + p * WORDS_PER_GROUP, WORDS_PER_GROUP)
-            out_ref[pl.ds(at, WORDS_PER_GROUP), q : q + tile] = high.astype(jnp.bfloat16)
-
-
-def unpack(group, codes, scales, chunk, columns):
-    words = codes.shape[0]
-    steps = words // PAIRS // 2
+    group = group_ref[0]
+    first = pltpu.make_async_copy(scales_hbm, scales, sems.at[count])
+    first.start()
+    copies = []
+    for step in range(count):
+        at = pl.multiple_of((group * count + step) * rows, rows)
+        copies.append(
+            pltpu.make_async_copy(
+                codes_hbm.at[pl.ds(at, rows), pl.ds(0, columns)], words.at[step], sems.at[step]
+            )
+        )
+        copies[-1].start()
+    first.wait()
+    wide[...] = scales[...].astype(jnp.float32)
+    rest_ref[...] = jnp.where(group == 0, wide[:per, columns:], wide[per:, columns:])
+    for step in range(count):
+        copies[step].wait()
+
+        @pl.loop(0, columns // tile)
+        def _(i, step=step):
+            here = pl.ds(pl.multiple_of(i * tile, tile), tile)
+            for p in range(spans):
+                top = p * WORDS_PER_GROUP
+                low, high = unpack_span(
+                    words[step, top : top + WORDS_PER_GROUP, here],
+                    wide[pl.ds(group * per + step * spans + p, 1), here],
+                )
+                at = step * rows + top
+                out_ref[at : at + WORDS_PER_GROUP, here] = low
+                out_ref[plane + at : plane + at + WORDS_PER_GROUP, here] = high
+
+
+def unpack(group, codes, scales, columns, tile):
+    words, width = codes.shape
+    half = words // 2
+    hbm = pl.BlockSpec(memory_space=pltpu.HBM)
+    vmem = pl.BlockSpec(memory_space=pltpu.VMEM)
+    count = half // PAIRS
+    per = half // WORDS_PER_GROUP
     return pl.pallas_call(
-        functools.partial(unpack_kernel, 512),
-        grid_spec=pltpu.PrefetchScalarGridSpec(
-            num_scalar_prefetch=1,
-            grid=(steps,),
-            in_specs=[
-                pl.BlockSpec((PAIRS, columns), lambda i, g: (g[0] * steps + i, chunk)),
-                pl.BlockSpec((scales.shape[0], columns), lambda i, g: (0, chunk)),
-            ],
-            out_specs=pl.BlockSpec(memory_space=pltpu.VMEM),
-            scratch_shapes=[pltpu.VMEM((scales.shape[0], columns), jnp.float32)],
-        ),
-        out_shape=pltpu.VMEM((words, columns), jnp.bfloat16),
-        compiler_params=pltpu.CompilerParams(vmem_limit_bytes=12 * MIB),
+        functools.partial(unpack_kernel, tile),
+        in_specs=[pl.BlockSpec(memory_space=pltpu.SMEM), hbm, hbm],
+        out_specs=[vmem, vmem],
+        out_shape=[
+            pltpu.VMEM((words, columns), jnp.bfloat16),
+            pltpu.VMEM((per, width - columns), jnp.float32),
+        ],
+        scratch_shapes=[
+            pltpu.VMEM((count, PAIRS, columns), jnp.int32),
+            pltpu.VMEM(scales.shape, jnp.bfloat16),
+            pltpu.VMEM(scales.shape, jnp.float32),
+            pltpu.SemaphoreType.DMA((count + 1,)),
+        ],
+        compiler_params=pltpu.CompilerParams(vmem_limit_bytes=24 * MIB),
         cost_estimate=pl.CostEstimate(
             flops=words * columns * 8, bytes_accessed=words * columns * 4, transcendentals=0
         ),
-        name=f"unpack_{chunk}",
-    )(group, codes, scales)
-
-
-def product_kernel(tile, chunks, place_ref, own_ref, *refs):
-    others = refs[: len(refs) - chunks - 2]
-    weights = refs[len(others) : len(others) + chunks]
-    keep_ref, send_ref = refs[-2:]
+        name="unpack",
+    )(group, in_hbm(codes), in_hbm(scales))
+
+
+def product_kernel(
+    tile, place_ref, codes_hbm, own_ref, *refs
+):
+    *others, ready_ref, scales_ref, keep_ref, send_ref, words, first_sc, second_sc, sems = refs
     rows = own_ref.shape[0]
-    place = place_ref[0]
+    group, place = place_ref[0], place_ref[1]
+    height = words.shape[1]
+    base = ready_ref.shape[1]
+    loops = scales_ref.shape[1] // tile
+    line = pl.multiple_of(group * height, height)
+
+    def fetch(index, slot):
+        at = pl.multiple_of(base + index * tile, tile)
+        return pltpu.make_async_copy(
+            codes_hbm.at[pl.ds(line, height), pl.ds(at, tile)], words.at[slot], sems.at[slot]
+        )
+
+    fetch(0, 0).start()
+    fetch(1, 1).start()
+
     count = len(others) + 1
     far = 4 * (count - 1)
     total = own_ref[...].astype(jnp.float32) * parity_sign(place, far)
@@ -271,37 +340,77 @@
     source = (unit // (2 * count) % 2) * (rows // 2) + (away ^ place) * each + slot % each
     pick = (column == source).astype(jnp.float32).astype(jnp.bfloat16)
     rotated = jnp.dot(pick, rotated, preferred_element_type=jnp.float32).astype(jnp.bfloat16)
-    for index, weight in enumerate(weights):
-        columns = weight.shape[1]
-
-        @pl.loop(0, columns // tile)
-        def _(i, weight=weight, index=index, columns=columns):
-            at = pl.multiple_of(i * tile, tile)
-            result = jnp.dot(
-                rotated, weight[:, pl.ds(at, tile)], preferred_element_type=jnp.float32
+
+    def multiply(weight, at):
+        result = jnp.dot(rotated, weight, preferred_element_type=jnp.float32)
+        to = pl.ds(pl.multiple_of(at, tile), tile)
+        keep_ref[:, to] = result[: rows // 2]
+        send_ref[:, to] = result[rows // 2 :].astype(jnp.bfloat16)
+
+    def unpack_tile(index, slot, target):
+        here = pl.ds(pl.multiple_of(index * tile, tile), tile)
+        for p in range(height // WORDS_PER_GROUP):
+            top = p * WORDS_PER_GROUP
+            low, high = unpack_span(
+                words[slot, top : top + WORDS_PER_GROUP, :], scales_ref[p : p + 1, here]
             )
-            to = pl.ds(pl.multiple_of(index * columns + at, tile), tile)
-            keep_ref[:, to] = result[: rows // 2]
-            send_ref[:, to] = result[rows // 2 :].astype(jnp.bfloat16)
-
-
-def product(place, own, others, weights):
+            target[top : top + WORDS_PER_GROUP, :] = low
+            target[height + top : height + top + WORDS_PER_GROUP, :] = high
+
+    def stage(index, slot, target, previous):
+        fetch(index, slot).wait()
+        ready = pl.ds(pl.multiple_of(index * tile, tile), tile)
+        multiply(ready_ref[:, ready], index * tile)
+        if previous is not None:
+            multiply(previous[...], base + (index - 1) * tile)
+        unpack_tile(index, slot, target)
+
+    stage(0, 0, first_sc, None)
+    fetch(2, 0).start()
+
+    @pl.loop(0, loops // 2 - 1)
+    def _(i):
+        stage(2 * i + 1, 1, second_sc, first_sc)
+        fetch(2 * i + 3, 1).start()
+        stage(2 * i + 2, 0, first_sc, second_sc)
+
+        @pl.when(2 * i + 4 < loops)
+        def _():
+            fetch(2 * i + 4, 0).start()
+
+    stage(loops - 1, 1, second_sc, first_sc)
+    multiply(second_sc[...], base + (loops - 1) * tile)
+
+
+def product(place, codes, own, others, ready, scales, tile):
     rows = own.shape[0]
-    width = sum(w.shape[1] for w in weights)
-    whole = pl.BlockSpec(memory_space=pltpu.VMEM)
-    weights = [pltpu.with_memory_space_constraint(w, pltpu.VMEM) for w in weights]
+    words, width = codes.shape
+    hbm = pl.BlockSpec(memory_space=pltpu.HBM)
+    vmem = pl.BlockSpec(memory_space=pltpu.VMEM)
     return pl.pallas_call(
-        functools.partial(product_kernel, 512, len(weights)),
-        in_specs=[pl.BlockSpec(memory_space=pltpu.SMEM)]
-        + [whole] * (1 + len(others) + len(weights)),
-        out_specs=[whole, whole],
+        functools.partial(product_kernel, tile),
+        in_specs=[pl.BlockSpec(memory_space=pltpu.SMEM), hbm] + [vmem] * (3 + len(others)),
+        out_specs=[vmem, vmem],
         out_shape=[
             jax.ShapeDtypeStruct((rows // 2, width), jnp.float32),
             jax.ShapeDtypeStruct((rows // 2, width), jnp.bfloat16),
         ],
-        compiler_params=pltpu.CompilerParams(vmem_limit_bytes=8 * MIB),
+        scratch_shapes=[
+            pltpu.VMEM((2, words // 2, tile), jnp.int32),
+            pltpu.VMEM((words, tile), jnp.bfloat16),
+            pltpu.VMEM((words, tile), jnp.bfloat16),
+            pltpu.SemaphoreType.DMA((2,)),
+        ],
+        compiler_params=pltpu.CompilerParams(vmem_limit_bytes=16 * MIB),
         name="product",
-    )(place, own, *others, *weights)
+    )(
+        place,
+        in_hbm(codes),
+        own,
+        *others,
+        pltpu.with_memory_space_constraint(ready, pltpu.VMEM),
+        pltpu.with_memory_space_constraint(scales, pltpu.VMEM),
+    )
 
 
 def shared_body(gate_act, up_act, codes, scales):
@@ -315,8 +424,6 @@
 
     parts = local_rotation(group, gate_act, up_act)
     near = exchanged(parts, 0, 1)
-    chunks = 4
-    weights = [unpack(group, codes, scales, c, width // chunks) for c in range(chunks)]
     core = place[0] % 2
     parts = jnp.where(
         core == 0,
@@ -335,8 +442,12 @@
             jnp.where(low, across_x + across_xy, across_xy - across_x),
         ]
     ).astype(jnp.bfloat16)
+    both, group_then = lax.optimization_barrier((both, group))
     others = [exchanged(both, 0, 4 * d) for d in range(1, count)]
-    keep, send = product(place, both, others, weights)
+    ready, rest = unpack(group_then, codes, scales, width // 2, TILE)
+    keep, send = product(
+        jnp.concatenate([group, place]), codes, both, others, ready, rest, TILE
+    )
 
     keep = keep + exchanged(send, 0, 1).astype(jnp.float32)
     quarters = keep.reshape(4, count * each, width)
@@ -347,11 +458,11 @@
         + exchanged(send[1], 1, 0).astype(jnp.float32)
         + exchanged(send[2], 1, 2).astype(jnp.float32)
     )
-    send = keep.astype(jnp.bfloat16)
-    total = keep[:each]
-    for d in range(1, count):
-        total = total + exchanged(send[d * each : (d + 1) * each], 0, 4 * d).astype(jnp.float32)
-    return total.astype(jnp.bfloat16)
+    while keep.shape[0] > each:
+        half = keep.shape[0] // 2
+        send = keep[half:].astype(jnp.bfloat16)
+        keep = keep[:half] + exchanged(send, 0, 4 * half // each).astype(jnp.float32)
+    return keep.astype(jnp.bfloat16)
 
 
 def body(gate_act, up_act, codes, scales):
@@ -363,6 +474,7 @@
         and blocks % 2 == 0
         and gate_act.shape[1] % tensor_size == 0
         and blocks * gate_act.shape[1] <= 128
+        and codes.shape[1] % (4 * TILE) == 0
     ):
         return shared_body(gate_act, up_act, codes, scales)
     return general_body(gate_act, up_act, codes, scales)

time: 66.3 us -> 54.4 us (0.82)
  Pallas kernels: 27.2 us -> 20 us
  local copies, waits for them, and re-layouts: 6.03 us -> 0.17 us
  waiting for transfers between devices: 14.3 us -> 18.1 us
  starting transfers between devices: 17.3 us -> 14.9 us
    pallas_call x5 -> x2, Pallas kernels: 26.3 us -> 17.9 us  [the longest x1 11.4 us: product(): pl.pallas_call(functools.partial(product_kernel, tile), in_specs=[pl.Bloc...]
    unnamed x8 -> x0, local copies, waits for them, and re-layouts: 5.85 us -> none
    ppermute x14 -> x13, waiting for transfers between devices: 14.3 us -> 18.1 us  [exchanged(): return lax.ppermute(value, AXES, pairs)]
    ppermute x14 -> x13, starting transfers between devices: 17.3 us -> 14.9 us  [exchanged(): return lax.ppermute(value, AXES, pairs)]
    pallas_call x1, Pallas kernels: 0.94 us -> 2.07 us  [local_rotation(): pl.pallas_call(local_kernel, in_specs=[pl.BlockSpec(memory_space=pltpu.SM...]
  transfers between devices with their start and end apart: 14 -> 13, of which waited for: 9 -> 10; matrix products, arithmetic and copies ran while one was open for 0% -> 0% of each run, Pallas kernels for 30% -> 12%
where the time goes in v2:
time: 54.4 us; the launch traced here: 54.2 us
  Pallas kernels  20 us (37%)
  waiting for transfers between devices  18.1 us (33%)
  starting transfers between devices  14.9 us (27%)
  other arithmetic  0.98 us (2%)
    ppermute x13, waiting for transfers between devices, exchanged(): return lax.ppermute(value, AXES, pairs)  18.1 us
    ppermute x13, starting transfers between devices, exchanged(): return lax.ppermute(value, AXES, pairs)  14.9 us
    pallas_call x1, Pallas kernels, product(): pl.pallas_call(functools.partial(product_kernel, tile), in_specs=[pl.Bloc...  11.4 us
    pallas_call x1, Pallas kernels, unpack(): pl.pallas_call(functools.partial(unpack_kernel, tile), in_specs=[pl.Block...  6.51 us
    pallas_call x1, Pallas kernels, local_rotation(): pl.pallas_call(local_kernel, in_specs=[pl.BlockSpec(memory_space=pltpu.SM...  2.07 us
  transfers between devices with their start and end apart: 13, of which 10 were waited for; matrix products, arithmetic and copies ran while one was open for 0% of the time, Pallas kernels for 12%

profile of v2, /device:TPU:0, one launch (start us, length us, event | category | flops | bytes accessed | tf_op | source)
XLA Modules:
  0.0 54.2 jit_solution(1070354525466150666)
XLA Ops:
  0.0 2.1 %local_rotation.1 = bf16[2,16,1664]{2,1,0:T(8,128)(2,1)S(1)} custom-call(s32[1]{0:T(128)} %bitcast.group_ref, bf16[16,3328]{1,0:T(8,128)(2,1)} %bitcast.10, bf16[16,3328]{1,0:T(8,128)(2,1)} %bitcast.11, bf16[1664,128]{1,0:T(8,128)(2,1)} %constant.40.clone.table_hbm), custom_call_target="tpu_custom_call" | custom-call | flops 100000000 | bytes 2097152 | tf_op jit(solution)/shard_map/local_rotation/pallas_call | solution.py:213
  2.1 0.5 collective-permute-start
  2.6 1.0 %collective-permute-done = bf16[2,16,1664]{2,1,0:T(8,128)(2,1)S(1)} collective-permute-done((bf16[2,16,1664]{2,1,0:T(8,128)(2,1)S(1)}, bf16[2,16,1664]{2,1,0:T(8,128)(2,1)S(1)}, u32[]{:S(2)}, u32[]{:S(2)}) %collective-permute-start) | collective-permute-done | bytes 106528 | tf_op jit(solution)/shard_map/ppermute | solution.py:131
  3.6 2.9 %collective-permute-start.1 = (bf16[16,1664]{1,0:T(8,128)(2,1)S(1)}, bf16[16,1664]{1,0:T(8,128)(2,1)S(1)}, u32[]{:S(2)}, u32[]{:S(2)}) collective-permute-start(bf16[16,1664]{1,0:T(8,128)(2,1)S(1)} %get-tuple-element.22), channel_id=1, source_target_pairs={{0,2},{1,3},{2,0},{3,1},{4,6},{5,7},{6,4},{7,5},{8,10},{9,11},{10,... | collective-permute-start | bytes 159752 | tf_op jit(solution)/shard_map/ppermute | solution.py:131
  6.6 1.4 %collective-permute-start.3 = (bf16[16,1664]{1,0:T(8,128)(2,1)S(1)}, bf16[16,1664]{1,0:T(8,128)(2,1)S(1)}, u32[]{:S(2)}, u32[]{:S(2)}) collective-permute-start(bf16[16,1664]{1,0:T(8,128)(2,1)S(1)} %get-tuple-element.23), channel_id=1, source_target_pairs={{0,18},{1,19},{2,16},{3,17},{4,22},{5,23},{6,20},{7,21},{8,26},{9,... | collective-permute-start | bytes 159752 | tf_op jit(solution)/shard_map/ppermute | solution.py:131
  8.0 0.1 collective-permute-start.2
  8.1 0.7 %collective-permute-done.1 = bf16[16,1664]{1,0:T(8,128)(2,1)S(1)} collective-permute-done((bf16[16,1664]{1,0:T(8,128)(2,1)S(1)}, bf16[16,1664]{1,0:T(8,128)(2,1)S(1)}, u32[]{:S(2)}, u32[]{:S(2)}) %collective-permute-start.1) | collective-permute-done | bytes 53280 | tf_op jit(solution)/shard_map/ppermute | solution.py:131
  8.8 3.2 %collective-permute-done.3 = bf16[16,1664]{1,0:T(8,128)(2,1)S(1)} collective-permute-done((bf16[16,1664]{1,0:T(8,128)(2,1)S(1)}, bf16[16,1664]{1,0:T(8,128)(2,1)S(1)}, u32[]{:S(2)}, u32[]{:S(2)}) %collective-permute-start.3) | collective-permute-done | bytes 53280 | tf_op jit(solution)/shard_map/ppermute | solution.py:131
  12.2 3.7 %collective-permute-start.6 = (bf16[32,1664]{1,0:T(8,128)(2,1)S(1)}, bf16[32,1664]{1,0:T(8,128)(2,1)S(1)}, u32[]{:S(2)}, u32[]{:S(2)}) collective-permute-start(bf16[32,1664]{1,0:T(8,128)(2,1)S(1)} %pad_maximum_fusion.own_ref), channel_id=1, source_target_pairs={{0,12},{1,13},{2,14},{3,15},{4,8},{5,9},{6,10},{7,11},{8,4},{9,5},... | collective-permute-start | bytes 319496 | tf_op jit(solution)/shard_map/ppermute | solution.py:131
  15.8 0.8 %collective-permute-start.4 = (bf16[32,1664]{1,0:T(8,128)(2,1)S(1)}, bf16[32,1664]{1,0:T(8,128)(2,1)S(1)}, u32[]{:S(2)}, u32[]{:S(2)}) collective-permute-start(bf16[32,1664]{1,0:T(8,128)(2,1)S(1)} %pad_maximum_fusion.own_ref), channel_id=1, source_target_pairs={{0,4},{1,5},{2,6},{3,7},{4,0},{5,1},{6,2},{7,3},{8,12},{9,13},{10,... | collective-permute-start | bytes 319496 | tf_op jit(solution)/shard_map/ppermute | solution.py:131
  16.7 6.5 %unpack.1 = (bf16[1664,4096]{1,0:T(8,128)(2,1)S(1)}, f32[52,4096]{1,0:T(8,128)S(1)}) custom-call(s32[1]{0:T(128)} %bitcast.group_ref, s32[1664,8192]{1,0:T(8,128)} %codes_hbm.3, bf16[104,8192]{1,0:T(8,128)(2,1)} %scales_hbm.1), custom_call_target="tpu_custom_call" | custom-call | flops 54525952 | bytes 27262976 | tf_op jit(solution)/shard_map/unpack/pallas_call | solution.py:285
  23.2 0.9 %collective-permute-done.5.refs_1_ = bf16[32,1664]{1,0:T(8,128)(2,1)S(1)} collective-permute-done((bf16[32,1664]{1,0:T(8,128)(2,1)S(1)}, bf16[32,1664]{1,0:T(8,128)(2,1)S(1)}, u32[]{:S(2)}, u32[]{:S(2)}) %collective-permute-start.5) | collective-permute-done | bytes 106528 | tf_op jit(solution)/shard_map/ppermute | solution.py:131
  24.2 11.4 %product.1 = (f32[16,8192]{1,0:T(8,128)S(1)}, bf16[16,8192]{1,0:T(8,128)(2,1)S(1)}) custom-call(s32[2]{0:T(128)S(1)} %pad_add_fusion.place_ref, s32[1664,8192]{1,0:T(8,128)} %codes_hbm.3, bf16[32,1664]{1,0:T(8,128)(2,1)S(1)} %pad_maximum_fusion.own_ref, bf16[32,1664]{1,0:T(8,128)(2,1)S(1)} %collective-permute-done.4.refs_0_, ...), custom_call_target="tpu_custom_call" | custom-call | tf_op jit(solution)/shard_map/product/pallas_call | solution.py:390
  35.6 1.5 %collective-permute-done.7 = bf16[16,8192]{1,0:T(8,128)(2,1)S(1)} collective-permute-done((bf16[16,8192]{1,0:T(8,128)(2,1)S(1)}, bf16[16,8192]{1,0:T(8,128)(2,1)S(1)}, u32[]{:S(2)}, u32[]{:S(2)}) %collective-permute-start.7) | collective-permute-done | bytes 262176 | tf_op jit(solution)/shard_map/ppermute | solution.py:131
  37.3 1.4 %collective-permute-start.8 = (bf16[4,8192]{1,0:T(4,128)(2,1)S(1)}, bf16[4,8192]{1,0:T(4,128)(2,1)S(1)}, u32[]{:S(2)}, u32[]{:S(2)}) collective-permute-start(bf16[4,8192]{1,0:T(4,128)(2,1)S(1)} %get-tuple-element.19), channel_id=1, source_target_pairs={{0,2},{1,3},{2,0},{3,1},{4,6},{5,7},{6,4},{7,5},{8,10},{9,11},{10,... | collective-permute-start | bytes 196616 | tf_op jit(solution)/shard_map/ppermute | solution.py:131
  38.7 0.6 %collective-permute-start.10 = (bf16[4,8192]{1,0:T(4,128)(2,1)S(1)}, bf16[4,8192]{1,0:T(4,128)(2,1)S(1)}, u32[]{:S(2)}, u32[]{:S(2)}) collective-permute-start(bf16[4,8192]{1,0:T(4,128)(2,1)S(1)} %get-tuple-element.20), channel_id=1, source_target_pairs={{0,18},{1,19},{2,16},{3,17},{4,22},{5,23},{6,20},{7,21},{8,26},{9,... | collective-permute-start | bytes 196616 | tf_op jit(solution)/shard_map/ppermute | solution.py:131
  39.3 1.5 %collective-permute-start.9 = (bf16[4,8192]{1,0:T(4,128)(2,1)S(1)}, bf16[4,8192]{1,0:T(4,128)(2,1)S(1)}, u32[]{:S(2)}, u32[]{:S(2)}) collective-permute-start(bf16[4,8192]{1,0:T(4,128)(2,1)S(1)} %get-tuple-element.21), channel_id=1, source_target_pairs={{0,16},{1,17},{2,18},{3,19},{4,20},{5,21},{6,22},{7,23},{8,24},{9,... | collective-permute-start | bytes 196616 | tf_op jit(solution)/shard_map/ppermute | solution.py:131
  40.9 0.8 %collective-permute-done.8 = bf16[4,8192]{1,0:T(4,128)(2,1)S(1)} collective-permute-done((bf16[4,8192]{1,0:T(4,128)(2,1)S(1)}, bf16[4,8192]{1,0:T(4,128)(2,1)S(1)}, u32[]{:S(2)}, u32[]{:S(2)}) %collective-permute-start.8) | collective-permute-done | bytes 65568 | tf_op jit(solution)/shard_map/ppermute | solution.py:131
  41.6 2.5 %collective-permute-done.10 = bf16[4,8192]{1,0:T(4,128)(2,1)S(1)} collective-permute-done((bf16[4,8192]{1,0:T(4,128)(2,1)S(1)}, bf16[4,8192]{1,0:T(4,128)(2,1)S(1)}, u32[]{:S(2)}, u32[]{:S(2)}) %collective-permute-start.10) | collective-permute-done | bytes 65568 | tf_op jit(solution)/shard_map/ppermute | solution.py:131
  44.3 1.5 %collective-permute-start.11 = (bf16[2,8192]{1,0:T(2,128)(2,1)S(1)}, bf16[2,8192]{1,0:T(2,128)(2,1)S(1)}, u32[]{:S(2)}, u32[]{:S(2)}) collective-permute-start(bf16[2,8192]{1,0:T(2,128)(2,1)S(1)} %slice.77), channel_id=1, source_target_pairs={{0,8},{1,9},{2,10},{3,11},{4,12},{5,13},{6,14},{7,15},{8,0},{9,1},... | collective-permute-start | bytes 98312 | tf_op jit(solution)/shard_map/ppermute | solution.py:131
  45.7 3.7 %collective-permute-done.11 = bf16[2,8192]{1,0:T(2,128)(2,1)S(1)} collective-permute-done((bf16[2,8192]{1,0:T(2,128)(2,1)S(1)}, bf16[2,8192]{1,0:T(2,128)(2,1)S(1)}, u32[]{:S(2)}, u32[]{:S(2)}) %collective-permute-start.11) | collective-permute-done | bytes 32800 | tf_op jit(solution)/shard_map/ppermute | solution.py:131
  49.5 0.3 collective-permute-start.12
  49.8 3.7 %collective-permute-done.12 = bf16[1,8192]{1,0:T(2,128)(2,1)S(1)} collective-permute-done((bf16[1,8192]{1,0:T(2,128)(2,1)S(1)}, bf16[1,8192]{1,0:T(2,128)(2,1)S(1)}, u32[]{:S(2)}, u32[]{:S(2)}) %collective-permute-start.12) | collective-permute-done | bytes 16416 | tf_op jit(solution)/shard_map/ppermute | solution.py:131
  53.5 0.7 %fusion.8 = bf16[1,8192]{1,0:T(2,128)(2,1)} fusion(f32[2,8192]{1,0:T(2,128)S(1)} %slice_add_fusion.1, bf16[1,8192]{1,0:T(2,128)(2,1)S(1)} %collective-permute-done.12), kind=kLoop, calls=%fused_computation.23 | loop fusion | flops 24576 | bytes 65536 | tf_op jit(solution)/shard_map/convert_element_type | solution.py:465
  (18 shorter events, 0.6 us)
Async XLA Ops:
  2.1 1.5 %collective-permute-start = (bf16[2,16,1664]{2,1,0:T(8,128)(2,1)S(1)}, bf16[2,16,1664]{2,1,0:T(8,128)(2,1)S(1)}, u32[]{:S(2)}, u32[]{:S(2)}) collective-permute-start(bf16[2,16,1664]{2,1,0:T(8,128)(2,1)S(1)} %local_rotation.1), channel_id=1, source_target_pairs={{0,1},{1,0},{2,3},{3,2},{4,5},{5,4},{6,7},{7,6},{8,9},{9,8},{10,11... | collective-permute-start | bytes 319496 | tf_op jit(solution)/shard_map/ppermute | solution.py:131
  3.6 5.2 %collective-permute-start.1 = (bf16[16,1664]{1,0:T(8,128)(2,1)S(1)}, bf16[16,1664]{1,0:T(8,128)(2,1)S(1)}, u32[]{:S(2)}, u32[]{:S(2)}) collective-permute-start(bf16[16,1664]{1,0:T(8,128)(2,1)S(1)} %get-tuple-element.22), channel_id=1, source_target_pairs={{0,2},{1,3},{2,0},{3,1},{4,6},{5,7},{6,4},{7,5},{8,10},{9,11},{10,... | collective-permute-start | bytes 159752 | tf_op jit(solution)/shard_map/ppermute | solution.py:131
  6.6 5.5 %collective-permute-start.3 = (bf16[16,1664]{1,0:T(8,128)(2,1)S(1)}, bf16[16,1664]{1,0:T(8,128)(2,1)S(1)}, u32[]{:S(2)}, u32[]{:S(2)}) collective-permute-start(bf16[16,1664]{1,0:T(8,128)(2,1)S(1)} %get-tuple-element.23), channel_id=1, source_target_pairs={{0,18},{1,19},{2,16},{3,17},{4,22},{5,23},{6,20},{7,21},{8,26},{9,... | collective-permute-start | bytes 159752 | tf_op jit(solution)/shard_map/ppermute | solution.py:131
  8.0 4.1 %collective-permute-start.2 = (bf16[16,1664]{1,0:T(8,128)(2,1)S(1)}, bf16[16,1664]{1,0:T(8,128)(2,1)S(1)}, u32[]{:S(2)}, u32[]{:S(2)}) collective-permute-start(bf16[16,1664]{1,0:T(8,128)(2,1)S(1)} %get-tuple-element.23), channel_id=1, source_target_pairs={{0,16},{1,17},{2,18},{3,19},{4,20},{5,21},{6,22},{7,23},{8,24},{9,... | collective-permute-start | bytes 159752 | tf_op jit(solution)/shard_map/ppermute | solution.py:131
  12.2 11.1 %collective-permute-start.6 = (bf16[32,1664]{1,0:T(8,128)(2,1)S(1)}, bf16[32,1664]{1,0:T(8,128)(2,1)S(1)}, u32[]{:S(2)}, u32[]{:S(2)}) collective-permute-start(bf16[32,1664]{1,0:T(8,128)(2,1)S(1)} %pad_maximum_fusion.own_ref), channel_id=1, source_target_pairs={{0,12},{1,13},{2,14},{3,15},{4,8},{5,9},{6,10},{7,11},{8,4},{9,5},... | collective-permute-start | bytes 319496 | tf_op jit(solution)/shard_map/ppermute | solution.py:131
  15.8 8.3 %collective-permute-start.5 = (bf16[32,1664]{1,0:T(8,128)(2,1)S(1)}, bf16[32,1664]{1,0:T(8,128)(2,1)S(1)}, u32[]{:S(2)}, u32[]{:S(2)}) collective-permute-start(bf16[32,1664]{1,0:T(8,128)(2,1)S(1)} %pad_maximum_fusion.own_ref), channel_id=1, source_target_pairs={{0,8},{1,9},{2,10},{3,11},{4,12},{5,13},{6,14},{7,15},{8,0},{9,1},... | collective-permute-start | bytes 319496 | tf_op jit(solution)/shard_map/ppermute | solution.py:131
  15.8 8.3 %collective-permute-start.4 = (bf16[32,1664]{1,0:T(8,128)(2,1)S(1)}, bf16[32,1664]{1,0:T(8,128)(2,1)S(1)}, u32[]{:S(2)}, u32[]{:S(2)}) collective-permute-start(bf16[32,1664]{1,0:T(8,128)(2,1)S(1)} %pad_maximum_fusion.own_ref), channel_id=1, source_target_pairs={{0,4},{1,5},{2,6},{3,7},{4,0},{5,1},{6,2},{7,3},{8,12},{9,13},{10,... | collective-permute-start | bytes 319496 | tf_op jit(solution)/shard_map/ppermute | solution.py:131
  35.6 1.6 %collective-permute-start.7 = (bf16[16,8192]{1,0:T(8,128)(2,1)S(1)}, bf16[16,8192]{1,0:T(8,128)(2,1)S(1)}, u32[]{:S(2)}, u32[]{:S(2)}) collective-permute-start(bf16[16,8192]{1,0:T(8,128)(2,1)S(1)} %get-tuple-element.16), channel_id=1, source_target_pairs={{0,1},{1,0},{2,3},{3,2},{4,5},{5,4},{6,7},{7,6},{8,9},{9,8},{10,11... | collective-permute-start | bytes 786440 | tf_op jit(solution)/shard_map/ppermute | solution.py:131
  37.3 4.3 %collective-permute-start.8 = (bf16[4,8192]{1,0:T(4,128)(2,1)S(1)}, bf16[4,8192]{1,0:T(4,128)(2,1)S(1)}, u32[]{:S(2)}, u32[]{:S(2)}) collective-permute-start(bf16[4,8192]{1,0:T(4,128)(2,1)S(1)} %get-tuple-element.19), channel_id=1, source_target_pairs={{0,2},{1,3},{2,0},{3,1},{4,6},{5,7},{6,4},{7,5},{8,10},{9,11},{10,... | collective-permute-start | bytes 196616 | tf_op jit(solution)/shard_map/ppermute | solution.py:131
  38.7 5.5 %collective-permute-start.10 = (bf16[4,8192]{1,0:T(4,128)(2,1)S(1)}, bf16[4,8192]{1,0:T(4,128)(2,1)S(1)}, u32[]{:S(2)}, u32[]{:S(2)}) collective-permute-start(bf16[4,8192]{1,0:T(4,128)(2,1)S(1)} %get-tuple-element.20), channel_id=1, source_target_pairs={{0,18},{1,19},{2,16},{3,17},{4,22},{5,23},{6,20},{7,21},{8,26},{9,... | collective-permute-start | bytes 196616 | tf_op jit(solution)/shard_map/ppermute | solution.py:131
  39.3 4.9 %collective-permute-start.9 = (bf16[4,8192]{1,0:T(4,128)(2,1)S(1)}, bf16[4,8192]{1,0:T(4,128)(2,1)S(1)}, u32[]{:S(2)}, u32[]{:S(2)}) collective-permute-start(bf16[4,8192]{1,0:T(4,128)(2,1)S(1)} %get-tuple-element.21), channel_id=1, source_target_pairs={{0,16},{1,17},{2,18},{3,19},{4,20},{5,21},{6,22},{7,23},{8,24},{9,... | collective-permute-start | bytes 196616 | tf_op jit(solution)/shard_map/ppermute | solution.py:131
  44.3 5.2 %collective-permute-start.11 = (bf16[2,8192]{1,0:T(2,128)(2,1)S(1)}, bf16[2,8192]{1,0:T(2,128)(2,1)S(1)}, u32[]{:S(2)}, u32[]{:S(2)}) collective-permute-start(bf16[2,8192]{1,0:T(2,128)(2,1)S(1)} %slice.77), channel_id=1, source_target_pairs={{0,8},{1,9},{2,10},{3,11},{4,12},{5,13},{6,14},{7,15},{8,0},{9,1},... | collective-permute-start | bytes 98312 | tf_op jit(solution)/shard_map/ppermute | solution.py:131
  49.5 4.0 %collective-permute-start.12 = (bf16[1,8192]{1,0:T(2,128)(2,1)S(1)}, bf16[1,8192]{1,0:T(2,128)(2,1)S(1)}, u32[]{:S(2)}, u32[]{:S(2)}) collective-permute-start(bf16[1,8192]{1,0:T(2,128)(2,1)S(1)} %slice.78), channel_id=1, source_target_pairs={{0,4},{1,5},{2,6},{3,7},{4,0},{5,1},{6,2},{7,3},{8,12},{9,13},{10,... | collective-permute-start | bytes 49160 | tf_op jit(solution)/shard_map/ppermute | solution.py:131

commit v3 on v2

--- a/solution.py
+++ b/solution.py
@@ -17,6 +17,8 @@
 AXES = ("groups", "tensor")
 MIB = 2**20
 TILE = 512
+CHUNK = 256
+FETCHES = (3, 5, 4)
 LANES = 128
 
 
@@ -145,9 +147,34 @@
     return (1 - 2 * (total % 2)).astype(jnp.float32)
 
 
+def fetches(codes_hbm, group, first, count, words, sems, sem):
+    height, tile = words.shape[1:]
+    line = pl.multiple_of(group * height, height)
+    return [
+        pltpu.make_async_copy(
+            codes_hbm.at[pl.ds(line, height), pl.ds((first + i) * tile, tile)],
+            words.at[i],
+            sems.at[sem + i],
+        )
+        for i in range(count)
+    ]
+
+
 def local_kernel(
-    group_ref, gate_hbm, up_hbm, table_hbm, out_ref, gate_in, up_in, table, hidden_sc, stack_sc, mix_sc, sems
+    group_ref,
+    gate_hbm,
+    up_hbm,
+    table_hbm,
+    out_ref,
+    gate_in,
+    up_in,
+    table,
+    hidden_sc,
+    stack_sc,
+    mix_sc,
+    sems,
 ):
+    group = group_ref[0]
     copies = [
         pltpu.make_async_copy(source, target, sems.at[index])
         for index, (source, target) in enumerate(
@@ -188,7 +215,6 @@
             walsh, local, preferred_element_type=jnp.float32
         ).astype(jnp.bfloat16)
     padded = wide * LANES // 2
-    group = group_ref[0]
     for part in range(2):
         first = (group if part == 0 else 1 - group) * half
         for parity in range(2):
@@ -210,10 +236,11 @@
     table[:, padded : padded + PAIRS] = by_parity[:, 1].T
     table = np.concatenate(np.split(table, 2 * padded // LANES, axis=1))
     hbm = pl.BlockSpec(memory_space=pltpu.HBM)
+    vmem = pl.BlockSpec(memory_space=pltpu.VMEM)
     return pl.pallas_call(
         local_kernel,
-        in_specs=[pl.BlockSpec(memory_space=pltpu.SMEM), hbm, hbm, hbm],
-        out_specs=pl.BlockSpec(memory_space=pltpu.VMEM),
+        in_specs=[pl.BlockSpec(memory_space=pltpu.SMEM)] + [hbm] * 3,
+        out_specs=vmem,
         out_shape=jax.ShapeDtypeStruct((2, rows, units // 2), jnp.bfloat16),
         scratch_shapes=[
             pltpu.VMEM((rows, units), jnp.bfloat16),
@@ -224,10 +251,15 @@
             pltpu.VMEM((blocks * rows, 2 * padded), jnp.bfloat16),
             pltpu.SemaphoreType.DMA((3,)),
         ],
-        compiler_params=pltpu.CompilerParams(vmem_limit_bytes=10 * MIB),
-        cost_estimate=pl.CostEstimate(flops=10**8, bytes_accessed=2 * MIB, transcendentals=10**5),
+        compiler_params=pltpu.CompilerParams(vmem_limit_bytes=6 * MIB),
+        cost_estimate=pl.CostEstimate(flops=10**8, bytes_accessed=8 * MIB, transcendentals=10**5),
         name="local_rotation",
-    )(group, in_hbm(gate_act.T), in_hbm(up_act.T), in_hbm(jnp.asarray(table, jnp.bfloat16)))
+    )(
+        group,
+        in_hbm(gate_act.T),
+        in_hbm(up_act.T),
+        in_hbm(jnp.asarray(table, jnp.bfloat16)),
+    )
 
 
 def unpack_span(words, scale):
@@ -238,98 +270,142 @@
     return (low - eight) * scale, (high - eight) * scale
 
 
-def unpack_kernel(tile, group_ref, codes_hbm, scales_hbm, out_ref, rest_ref, words, scales, wide, sems):
-    count, rows, columns = words.shape
-    spans = rows // WORDS_PER_GROUP
-    per = count * spans
-    plane = out_ref.shape[0] // 2
-    group = group_ref[0]
-    first = pltpu.make_async_copy(scales_hbm, scales, sems.at[count])
-    first.start()
-    copies = []
-    for step in range(count):
-        at = pl.multiple_of((group * count + step) * rows, rows)
-        copies.append(
-            pltpu.make_async_copy(
-                codes_hbm.at[pl.ds(at, rows), pl.ds(0, columns)], words.at[step], sems.at[step]
-            )
+def widen(group, scales_ref, wide_ref):
+    per = wide_ref.shape[0]
+    for part in range(2):
+
+        @pl.when(group == part)
+        def _(part=part):
+            wide_ref[...] = scales_ref[part * per : (part + 1) * per, :].astype(jnp.float32)
+
+
+def unpack_tile(words, scales_ref, column, target, at, spans):
+    height, tile = words.shape
+    for p in spans:
+        top = p * WORDS_PER_GROUP
+        low, high = unpack_span(
+            words[top : top + WORDS_PER_GROUP, :], scales_ref[p : p + 1, pl.ds(column, tile)]
         )
-        copies[-1].start()
-    first.wait()
-    wide[...] = scales[...].astype(jnp.float32)
-    rest_ref[...] = jnp.where(group == 0, wide[:per, columns:], wide[per:, columns:])
-    for step in range(count):
-        copies[step].wait()
-
-        @pl.loop(0, columns // tile)
-        def _(i, step=step):
-            here = pl.ds(pl.multiple_of(i * tile, tile), tile)
-            for p in range(spans):
-                top = p * WORDS_PER_GROUP
-                low, high = unpack_span(
-                    words[step, top : top + WORDS_PER_GROUP, here],
-                    wide[pl.ds(group * per + step * spans + p, 1), here],
-                )
-                at = step * rows + top
-                out_ref[at : at + WORDS_PER_GROUP, here] = low
-                out_ref[plane + at : plane + at + WORDS_PER_GROUP, here] = high
-
-
-def unpack(group, codes, scales, columns, tile):
+        target[top : top + WORDS_PER_GROUP, pl.ds(at, tile)] = low
+        target[height + top : height + top + WORDS_PER_GROUP, pl.ds(at, tile)] = high
+
+
+def fetch_kernel(group_ref, codes_hbm, scales_hbm, next_ref, wide_ref, scales, sems):
+    ahead = next_ref.shape[0]
+    arrival = pltpu.make_async_copy(scales_hbm, scales, sems.at[ahead])
+    arrival.start()
+    copies = fetches(codes_hbm, group_ref[0], 0, ahead, next_ref, sems, 0)
+    for copy in copies:
+        copy.start()
+    arrival.wait()
+    widen(group_ref[0], scales, wide_ref)
+    for copy in copies:
+        copy.wait()
+
+
+def fetch(group, codes, scales, ahead):
     words, width = codes.shape
-    half = words // 2
     hbm = pl.BlockSpec(memory_space=pltpu.HBM)
     vmem = pl.BlockSpec(memory_space=pltpu.VMEM)
-    count = half // PAIRS
-    per = half // WORDS_PER_GROUP
     return pl.pallas_call(
-        functools.partial(unpack_kernel, tile),
+        fetch_kernel,
         in_specs=[pl.BlockSpec(memory_space=pltpu.SMEM), hbm, hbm],
         out_specs=[vmem, vmem],
         out_shape=[
+            pltpu.VMEM((ahead, words // 2, TILE), codes.dtype),
+            pltpu.VMEM((words // 2 // WORDS_PER_GROUP, width), jnp.float32),
+        ],
+        scratch_shapes=[
+            pltpu.VMEM(scales.shape, scales.dtype),
+            pltpu.SemaphoreType.DMA((ahead + 1,)),
+        ],
+        compiler_params=pltpu.CompilerParams(vmem_limit_bytes=4 * MIB),
+        cost_estimate=pl.CostEstimate(
+            flops=0, bytes_accessed=ahead * words * TILE * 2, transcendentals=0
+        ),
+        name="fetch",
+    )(group, in_hbm(codes), in_hbm(scales))
+
+
+def unpack_kernel(group_ref, codes_hbm, scales_ref, given, out_ref, next_ref, words, sems):
+    group = group_ref[0]
+    count, height, tile = given.shape
+    own, ahead = words.shape[0], next_ref.shape[0]
+    copies = fetches(codes_hbm, group, count, own, words, sems, 0)
+    copies += fetches(codes_hbm, group, count + own, ahead, next_ref, sems, own)
+    for copy in copies:
+        copy.start()
+    spans = range(height // WORDS_PER_GROUP)
+
+    @pl.loop(0, count)
+    def _(i):
+        at = pl.multiple_of(i * tile, tile)
+        unpack_tile(given.at[i], scales_ref, at, out_ref, at, spans)
+
+    @pl.loop(0, own)
+    def _(i):
+        pltpu.make_async_copy(
+            codes_hbm.at[pl.ds(0, height), pl.ds(0, tile)], words.at[i], sems.at[i]
+        ).wait()
+        at = pl.multiple_of((count + i) * tile, tile)
+        unpack_tile(words.at[i], scales_ref, at, out_ref, at, spans)
+
+    for copy in copies[own:]:
+        copy.wait()
+
+
+def unpack(group, codes, scales, given, own, ahead):
+    words = codes.shape[0]
+    hbm = pl.BlockSpec(memory_space=pltpu.HBM)
+    vmem = pl.BlockSpec(memory_space=pltpu.VMEM)
+    columns = (given.shape[0] + own) * TILE
+    return pl.pallas_call(
+        unpack_kernel,
+        in_specs=[pl.BlockSpec(memory_space=pltpu.SMEM), hbm, vmem, vmem],
+        out_specs=[vmem, vmem],
+        out_shape=[
             pltpu.VMEM((words, columns), jnp.bfloat16),
-            pltpu.VMEM((per, width - columns), jnp.float32),
+            pltpu.VMEM((ahead, words // 2, TILE), codes.dtype),
         ],
         scratch_shapes=[
-            pltpu.VMEM((count, PAIRS, columns), jnp.int32),
-            pltpu.VMEM(scales.shape, jnp.bfloat16),
-            pltpu.VMEM(scales.shape, jnp.float32),
-            pltpu.SemaphoreType.DMA((count + 1,)),
-        ],
-        compiler_params=pltpu.CompilerParams(vmem_limit_bytes=24 * MIB),
+            pltpu.VMEM((own, words // 2, TILE), codes.dtype),
+            pltpu.SemaphoreType.DMA((own + ahead,)),
+        ],
+        compiler_params=pltpu.CompilerParams(vmem_limit_bytes=(2 + 2 * own) * MIB),
         cost_estimate=pl.CostEstimate(
             flops=words * columns * 8, bytes_accessed=words * columns * 4, transcendentals=0
         ),
         name="unpack",
-    )(group, in_hbm(codes), in_hbm(scales))
-
-
-def product_kernel(
-    tile, place_ref, codes_hbm, own_ref, *refs
-):
-    *others, ready_ref, scales_ref, keep_ref, send_ref, words, first_sc, second_sc, sems = refs
+    )(
+        group,
+        in_hbm(codes),
+        pltpu.with_memory_space_constraint(scales, pltpu.VMEM),
+        pltpu.with_memory_space_constraint(given, pltpu.VMEM),
+    )
+
+
+def product_kernel(readies, place_ref, codes_hbm, given, scales_ref, own_ref, *refs):
+    *others, keep_ref, send_ref, first_sc, second_sc, words, sems = refs
+    ready_refs, others = others[:readies], others[readies:]
     rows = own_ref.shape[0]
     group, place = place_ref[0], place_ref[1]
-    height = words.shape[1]
-    base = ready_ref.shape[1]
-    loops = scales_ref.shape[1] // tile
-    line = pl.multiple_of(group * height, height)
-
-    def fetch(index, slot):
-        at = pl.multiple_of(base + index * tile, tile)
-        return pltpu.make_async_copy(
-            codes_hbm.at[pl.ds(line, height), pl.ds(at, tile)], words.at[slot], sems.at[slot]
-        )
-
-    fetch(0, 0).start()
-    fetch(1, 1).start()
+    held, height, tile = given.shape
+    ready_tiles = [
+        (ref, i * tile) for ref in ready_refs for i in range(ref.shape[1] // tile)
+    ]
+    tiles = scales_ref.shape[1] // tile
+    base = len(ready_tiles)
+    own = tiles - base - held
+    copies = fetches(codes_hbm, group, base + held, own, words, sems, 0)
+    for copy in copies:
+        copy.start()
 
     count = len(others) + 1
     far = 4 * (count - 1)
     total = own_ref[...].astype(jnp.float32) * parity_sign(place, far)
     for index, other in enumerate(others):
         total = total + other[...].astype(jnp.float32) * parity_sign(
-            place & (place ^ (4 * (index + 1))), far
+            place & (place ^ (4 * (count - 1 - index))), far
         )
     rotated = (total * (1.0 / math.sqrt(HAD_CROSS))).astype(jnp.bfloat16)
     each = rows // (8 * count)
@@ -341,75 +417,79 @@
     pick = (column == source).astype(jnp.float32).astype(jnp.bfloat16)
     rotated = jnp.dot(pick, rotated, preferred_element_type=jnp.float32).astype(jnp.bfloat16)
 
-    def multiply(weight, at):
-        result = jnp.dot(rotated, weight, preferred_element_type=jnp.float32)
-        to = pl.ds(pl.multiple_of(at, tile), tile)
-        keep_ref[:, to] = result[: rows // 2]
-        send_ref[:, to] = result[rows // 2 :].astype(jnp.bfloat16)
-
-    def unpack_tile(index, slot, target):
-        here = pl.ds(pl.multiple_of(index * tile, tile), tile)
-        for p in range(height // WORDS_PER_GROUP):
-            top = p * WORDS_PER_GROUP
-            low, high = unpack_span(
-                words[slot, top : top + WORDS_PER_GROUP, :], scales_ref[p : p + 1, here]
-            )
-            target[top : top + WORDS_PER_GROUP, :] = low
-            target[height + top : height + top + WORDS_PER_GROUP, :] = high
-
-    def stage(index, slot, target, previous):
-        fetch(index, slot).wait()
-        ready = pl.ds(pl.multiple_of(index * tile, tile), tile)
-        multiply(ready_ref[:, ready], index * tile)
+    depth = rotated.shape[1]
+    spans = height // WORDS_PER_GROUP
+    cuts = list(range(0, depth, CHUNK)) + [depth]
+
+    def stage(products, fresh):
+        sums = [None] * len(products)
+        done = 0
+        for k, (low, high) in enumerate(zip(cuts[:-1], cuts[1:])):
+            for index, (weight, at, _) in enumerate(products):
+                part = jnp.dot(
+                    rotated[:, low:high],
+                    weight[low:high, at : at + tile],
+                    preferred_element_type=jnp.float32,
+                )
+                sums[index] = sums[index] + part if k else part
+            if fresh is not None:
+                source, column, target = fresh
+                upto = spans * (k + 1) // (len(cuts) - 1)
+                unpack_tile(source, scales_ref, column, target, 0, range(done, upto))
+                done = upto
+        for total, (_, _, to) in zip(sums, products):
+            keep_ref[:, to : to + tile] = total[: rows // 2]
+            send_ref[:, to : to + tile] = total[rows // 2 :].astype(jnp.bfloat16)
+
+    waiting = [(ref, at, index * tile) for index, (ref, at) in enumerate(ready_tiles)]
+    each_stage = -(-base // (tiles - base))
+    previous = None
+    for index in range(base, tiles):
+        number = index - base
+        if number >= held:
+            copies[number - held].wait()
+        source = given.at[number] if number < held else words.at[number - held]
+        target = second_sc if number % 2 else first_sc
+        products = waiting[:each_stage]
+        waiting = waiting[each_stage:]
         if previous is not None:
-            multiply(previous[...], base + (index - 1) * tile)
-        unpack_tile(index, slot, target)
-
-    stage(0, 0, first_sc, None)
-    fetch(2, 0).start()
-
-    @pl.loop(0, loops // 2 - 1)
-    def _(i):
-        stage(2 * i + 1, 1, second_sc, first_sc)
-        fetch(2 * i + 3, 1).start()
-        stage(2 * i + 2, 0, first_sc, second_sc)
-
-        @pl.when(2 * i + 4 < loops)
-        def _():
-            fetch(2 * i + 4, 0).start()
-
-    stage(loops - 1, 1, second_sc, first_sc)
-    multiply(second_sc[...], base + (loops - 1) * tile)
-
-
-def product(place, codes, own, others, ready, scales, tile):
+            products.append(previous)
+        stage(products, (source, index * tile, target))
+        previous = (target, 0, index * tile)
+    stage(waiting + [previous], None)
+
+
+def product(place, codes, given, scales, own, others, ready):
     rows = own.shape[0]
     words, width = codes.shape
     hbm = pl.BlockSpec(memory_space=pltpu.HBM)
     vmem = pl.BlockSpec(memory_space=pltpu.VMEM)
+    left = width // TILE - given.shape[0] - sum(r.shape[1] for r in ready) // TILE
+    held = [pltpu.with_memory_space_constraint(r, pltpu.VMEM) for r in (given, scales)]
     return pl.pallas_call(
-        functools.partial(product_kernel, tile),
-        in_specs=[pl.BlockSpec(memory_space=pltpu.SMEM), hbm] + [vmem] * (3 + len(others)),
+        functools.partial(product_kernel, len(ready)),
+        in_specs=[pl.BlockSpec(memory_space=pltpu.SMEM), hbm]
+        + [vmem] * (3 + len(ready) + len(others)),
         out_specs=[vmem, vmem],
         out_shape=[
             jax.ShapeDtypeStruct((rows // 2, width), jnp.float32),
             jax.ShapeDtypeStruct((rows // 2, width), jnp.bfloat16),
         ],
         scratch_shapes=[
-            pltpu.VMEM((2, words // 2, tile), jnp.int32),
-            pltpu.VMEM((words, tile), jnp.bfloat16),
-            pltpu.VMEM((words, tile), jnp.bfloat16),
-            pltpu.SemaphoreType.DMA((2,)),
-        ],
-        compiler_params=pltpu.CompilerParams(vmem_limit_bytes=16 * MIB),
+            pltpu.VMEM((words, TILE), jnp.bfloat16),
+            pltpu.VMEM((words, TILE), jnp.bfloat16),
+            pltpu.VMEM((max(left, 1), words // 2, TILE), codes.dtype),
+            pltpu.SemaphoreType.DMA((max(left, 1),)),
+        ],
+        compiler_params=pltpu.CompilerParams(vmem_limit_bytes=(8 + 2 * left) * MIB),
         name="product",
     )(
         place,
         in_hbm(codes),
+        *held,
         own,
+        *[pltpu.with_memory_space_constraint(r, pltpu.VMEM) for r in ready],
         *others,
-        pltpu.with_memory_space_constraint(ready, pltpu.VMEM),
-        pltpu.with_memory_space_constraint(scales, pltpu.VMEM),
     )
 
 
@@ -422,6 +502,8 @@
     group = lax.axis_index("groups").astype(jnp.int32)[None]
     place = lax.axis_index("tensor").astype(jnp.int32)[None]
 
+    tiles = width // TILE
+    at_near, at_far, for_product = (tiles * n // 16 for n in FETCHES)
     parts = local_rotation(group, gate_act, up_act)
     near = exchanged(parts, 0, 1)
     core = place[0] % 2
@@ -430,10 +512,12 @@
         parts.astype(jnp.float32) + near.astype(jnp.float32),
         near.astype(jnp.float32) - parts.astype(jnp.float32),
     ).astype(jnp.bfloat16)
+    parts, group_then = lax.optimization_barrier((parts, group))
     mine, theirs = parts[0], parts[1]
     across_y = exchanged(mine, 0, 2).astype(jnp.float32)
     across_x = exchanged(theirs, 1, 0).astype(jnp.float32)
     across_xy = exchanged(theirs, 1, 2).astype(jnp.float32)
+    words, scales = fetch(group_then, codes, scales, at_near)
     low = place[0] // 2 % 2 == 0
     here = mine.astype(jnp.float32)
     both = jnp.concatenate(
@@ -442,11 +526,11 @@
             jnp.where(low, across_x + across_xy, across_xy - across_x),
         ]
     ).astype(jnp.bfloat16)
-    both, group_then = lax.optimization_barrier((both, group))
-    others = [exchanged(both, 0, 4 * d) for d in range(1, count)]
-    ready, rest = unpack(group_then, codes, scales, width // 2, TILE)
+    both, group_then, words = lax.optimization_barrier((both, group, words))
+    others = [exchanged(both, 0, 4 * d) for d in range(count - 1, 0, -1)]
+    ready, words = unpack(group_then, codes, scales, words, at_far, for_product)
     keep, send = product(
-        jnp.concatenate([group, place]), codes, both, others, ready, rest, TILE
+        jnp.concatenate([group, place]), codes, words, scales, both, others, [ready]
     )
 
     keep = keep + exchanged(send, 0, 1).astype(jnp.float32)
@@ -474,7 +558,7 @@
         and blocks % 2 == 0
         and gate_act.shape[1] % tensor_size == 0
         and blocks * gate_act.shape[1] <= 128
-        and codes.shape[1] % (4 * TILE) == 0
+        and codes.shape[1] % (16 * TILE) == 0
     ):
         return shared_body(gate_act, up_act, codes, scales)
     return general_body(gate_act, up_act, codes, scales)

time: 54.4 us -> 50.8 us (0.934)
  waiting for transfers between devices: 18.1 us -> 16.6 us
  Pallas kernels: 20 us -> 18.6 us
  starting transfers between devices: 14.9 us -> 14.2 us
    ppermute x13, waiting for transfers between devices: 18.1 us -> 16.6 us  [exchanged(): return lax.ppermute(value, AXES, pairs)]
    pallas_call x2 -> x3, Pallas kernels: 17.9 us -> 16.5 us  [the longest x1 7.9 us: product(): pl.pallas_call(functools.partial(product_kernel, len(ready)), in_specs=[p...]
    ppermute x13, starting transfers between devices: 14.9 us -> 14.2 us  [exchanged(): return lax.ppermute(value, AXES, pairs)]
  transfers between devices with their start and end apart: 13 -> 13, of which waited for: 10 -> 9; matrix products, arithmetic and copies ran while one was open for 0% -> 0% of each run, Pallas kernels for 12% -> 17%
where the time goes in v3:
time: 50.8 us; the launch traced here: 50.7 us
  Pallas kernels  18.6 us (37%)
  waiting for transfers between devices  16.6 us (33%)
  starting transfers between devices  14.2 us (28%)
  other arithmetic  0.98 us (2%)
    ppermute x13, waiting for transfers between devices, exchanged(): return lax.ppermute(value, AXES, pairs)  16.6 us
    ppermute x13, starting transfers between devices, exchanged(): return lax.ppermute(value, AXES, pairs)  14.2 us
    pallas_call x1, Pallas kernels, product(): pl.pallas_call(functools.partial(product_kernel, len(ready)), in_specs=[p...  7.9 us
    pallas_call x1, Pallas kernels, unpack(): pl.pallas_call(unpack_kernel, in_specs=[pl.BlockSpec(memory_space=pltpu.S...  5.55 us
    pallas_call x1, Pallas kernels, fetch(): pl.pallas_call(fetch_kernel, in_specs=[pl.BlockSpec(memory_space=pltpu.SM...  3.04 us
    pallas_call x1, Pallas kernels, local_rotation(): pl.pallas_call(local_kernel, in_specs=[pl.BlockSpec(memory_space=pltpu.SM...  2.07 us
  transfers between devices with their start and end apart: 13, of which 9 were waited for; matrix products, arithmetic and copies ran while one was open for 0% of the time, Pallas kernels for 17%

profile of v3, /device:TPU:0, one launch (start us, length us, event | category | flops | bytes accessed | tf_op | source)
XLA Modules:
  0.0 50.7 jit_solution(11963400329979853586)
XLA Ops:
  0.0 2.1 %local_rotation.1 = bf16[2,16,1664]{2,1,0:T(8,128)(2,1)S(1)} custom-call(s32[1]{0:T(128)} %bitcast.group_ref, bf16[16,3328]{1,0:T(8,128)(2,1)} %bitcast.10, bf16[16,3328]{1,0:T(8,128)(2,1)} %bitcast.11, bf16[1664,128]{1,0:T(8,128)(2,1)} %constant.40.clone.table_hbm), custom_call_target="tpu_custom_call" | custom-call | flops 100000000 | bytes 8388608 | tf_op jit(solution)/shard_map/local_rotation/pallas_call | solution.py:240
  2.1 0.5 %collective-permute-start = (bf16[2,16,1664]{2,1,0:T(8,128)(2,1)S(1)}, bf16[2,16,1664]{2,1,0:T(8,128)(2,1)S(1)}, u32[]{:S(2)}, u32[]{:S(2)}) collective-permute-start(bf16[2,16,1664]{2,1,0:T(8,128)(2,1)S(1)} %local_rotation.1), channel_id=1, source_target_pairs={{0,1},{1,0},{2,3},{3,2},{4,5},{5,4},{6,7},{7,6},{8,9},{9,8},{10,11... | collective-permute-start | bytes 319496 | tf_op jit(solution)/shard_map/ppermute | solution.py:133
  2.6 1.0 %collective-permute-done = bf16[2,16,1664]{2,1,0:T(8,128)(2,1)S(1)} collective-permute-done((bf16[2,16,1664]{2,1,0:T(8,128)(2,1)S(1)}, bf16[2,16,1664]{2,1,0:T(8,128)(2,1)S(1)}, u32[]{:S(2)}, u32[]{:S(2)}) %collective-permute-start) | collective-permute-done | bytes 106528 | tf_op jit(solution)/shard_map/ppermute | solution.py:133
  3.6 2.9 %collective-permute-start.1 = (bf16[16,1664]{1,0:T(8,128)(2,1)S(1)}, bf16[16,1664]{1,0:T(8,128)(2,1)S(1)}, u32[]{:S(2)}, u32[]{:S(2)}) collective-permute-start(bf16[16,1664]{1,0:T(8,128)(2,1)S(1)} %get-tuple-element.32), channel_id=1, source_target_pairs={{0,2},{1,3},{2,0},{3,1},{4,6},{5,7},{6,4},{7,5},{8,10},{9,11},{10,... | collective-permute-start | bytes 159752 | tf_op jit(solution)/shard_map/ppermute | solution.py:133
  6.6 1.5 %collective-permute-start.2 = (bf16[16,1664]{1,0:T(8,128)(2,1)S(1)}, bf16[16,1664]{1,0:T(8,128)(2,1)S(1)}, u32[]{:S(2)}, u32[]{:S(2)}) collective-permute-start(bf16[16,1664]{1,0:T(8,128)(2,1)S(1)} %get-tuple-element.33), channel_id=1, source_target_pairs={{0,16},{1,17},{2,18},{3,19},{4,20},{5,21},{6,22},{7,23},{8,24},{9,... | collective-permute-start | bytes 159752 | tf_op jit(solution)/shard_map/ppermute | solution.py:133
  8.1 3.0 %fetch.1 = (s32[3,832,512]{2,1,0:T(8,128)S(1)}, f32[52,8192]{1,0:T(8,128)S(1)}) custom-call(s32[1]{0:T(128)} %bitcast.group_ref, s32[1664,8192]{1,0:T(8,128)} %codes_hbm.5, bf16[104,8192]{1,0:T(8,128)(2,1)} %scales_hbm.1), custom_call_target="tpu_custom_call" | custom-call | bytes 5111808 | tf_op jit(solution)/shard_map/fetch/pallas_call | solution.py:310
  11.2 1.9 %collective-permute-done.3 = bf16[16,1664]{1,0:T(8,128)(2,1)S(1)} collective-permute-done((bf16[16,1664]{1,0:T(8,128)(2,1)S(1)}, bf16[16,1664]{1,0:T(8,128)(2,1)S(1)}, u32[]{:S(2)}, u32[]{:S(2)}) %collective-permute-start.3) | collective-permute-done | bytes 53280 | tf_op jit(solution)/shard_map/ppermute | solution.py:133
  13.1 3.7 %collective-permute-start.4 = (bf16[32,1664]{1,0:T(8,128)(2,1)S(1)}, bf16[32,1664]{1,0:T(8,128)(2,1)S(1)}, u32[]{:S(2)}, u32[]{:S(2)}) collective-permute-start(bf16[32,1664]{1,0:T(8,128)(2,1)S(1)} %pad_maximum_fusion.own_ref), channel_id=1, source_target_pairs={{0,12},{1,13},{2,14},{3,15},{4,8},{5,9},{6,10},{7,11},{8,4},{9,5},... | collective-permute-start | bytes 319496 | tf_op jit(solution)/shard_map/ppermute | solution.py:133
  16.8 0.8 %collective-permute-start.6 = (bf16[32,1664]{1,0:T(8,128)(2,1)S(1)}, bf16[32,1664]{1,0:T(8,128)(2,1)S(1)}, u32[]{:S(2)}, u32[]{:S(2)}) collective-permute-start(bf16[32,1664]{1,0:T(8,128)(2,1)S(1)} %pad_maximum_fusion.own_ref), channel_id=1, source_target_pairs={{0,4},{1,5},{2,6},{3,7},{4,0},{5,1},{6,2},{7,3},{8,12},{9,13},{10,... | collective-permute-start | bytes 319496 | tf_op jit(solution)/shard_map/ppermute | solution.py:133
  17.7 5.5 %unpack.1 = (bf16[1664,4096]{1,0:T(8,128)(2,1)S(1)}, s32[4,832,512]{2,1,0:T(8,128)S(1)}) custom-call(s32[1]{0:T(128)} %bitcast.group_ref, s32[1664,8192]{1,0:T(8,128)} %codes_hbm.5, f32[52,8192]{1,0:T(8,128)S(1)} %get-tuple-element.20.scales_ref, s32[3,832,512]{2,1,0:T(8,128)S(1)} %get-tuple-element.21.given), custom_call_target="tpu_custom_call" | custom-call | flops 54525952 | bytes 27262976 | tf_op jit(solution)/shard_map/unpack/pallas_call | solution.py:362
  23.2 1.1 %collective-permute-done.5.refs_2_ = bf16[32,1664]{1,0:T(8,128)(2,1)S(1)} collective-permute-done((bf16[32,1664]{1,0:T(8,128)(2,1)S(1)}, bf16[32,1664]{1,0:T(8,128)(2,1)S(1)}, u32[]{:S(2)}, u32[]{:S(2)}) %collective-permute-start.5) | collective-permute-done | bytes 106528 | tf_op jit(solution)/shard_map/ppermute | solution.py:133
  24.4 7.9 %product.1 = (f32[16,8192]{1,0:T(8,128)S(1)}, bf16[16,8192]{1,0:T(8,128)(2,1)S(1)}) custom-call(s32[2]{0:T(128)S(1)} %pad_add_fusion.place_ref, s32[1664,8192]{1,0:T(8,128)} %codes_hbm.5, s32[4,832,512]{2,1,0:T(8,128)S(1)} %get-tuple-element.22.given, f32[52,8192]{1,0:T(8,128)S(1)} %get-tuple-element.20.scales_ref, ...), custom_call_target="tpu_custom_call" | custom-call | tf_op jit(solution)/shard_map/product/pallas_call | solution.py:469
  32.4 1.5 %collective-permute-done.7 = bf16[16,8192]{1,0:T(8,128)(2,1)S(1)} collective-permute-done((bf16[16,8192]{1,0:T(8,128)(2,1)S(1)}, bf16[16,8192]{1,0:T(8,128)(2,1)S(1)}, u32[]{:S(2)}, u32[]{:S(2)}) %collective-permute-start.7) | collective-permute-done | bytes 262176 | tf_op jit(solution)/shard_map/ppermute | solution.py:133
  34.0 1.9 %collective-permute-start.10 = (bf16[4,8192]{1,0:T(4,128)(2,1)S(1)}, bf16[4,8192]{1,0:T(4,128)(2,1)S(1)}, u32[]{:S(2)}, u32[]{:S(2)}) collective-permute-start(bf16[4,8192]{1,0:T(4,128)(2,1)S(1)} %get-tuple-element.30), channel_id=1, source_target_pairs={{0,18},{1,19},{2,16},{3,17},{4,22},{5,23},{6,20},{7,21},{8,26},{9,... | collective-permute-start | bytes 196616 | tf_op jit(solution)/shard_map/ppermute | solution.py:133
  36.0 0.6 %collective-permute-start.8 = (bf16[4,8192]{1,0:T(4,128)(2,1)S(1)}, bf16[4,8192]{1,0:T(4,128)(2,1)S(1)}, u32[]{:S(2)}, u32[]{:S(2)}) collective-permute-start(bf16[4,8192]{1,0:T(4,128)(2,1)S(1)} %get-tuple-element.29), channel_id=1, source_target_pairs={{0,2},{1,3},{2,0},{3,1},{4,6},{5,7},{6,4},{7,5},{8,10},{9,11},{10,... | collective-permute-start | bytes 196616 | tf_op jit(solution)/shard_map/ppermute | solution.py:133
  36.5 1.0 %collective-permute-start.9 = (bf16[4,8192]{1,0:T(4,128)(2,1)S(1)}, bf16[4,8192]{1,0:T(4,128)(2,1)S(1)}, u32[]{:S(2)}, u32[]{:S(2)}) collective-permute-start(bf16[4,8192]{1,0:T(4,128)(2,1)S(1)} %get-tuple-element.31), channel_id=1, source_target_pairs={{0,16},{1,17},{2,18},{3,19},{4,20},{5,21},{6,22},{7,23},{8,24},{9,... | collective-permute-start | bytes 196616 | tf_op jit(solution)/shard_map/ppermute | solution.py:133
  37.6 1.8 %collective-permute-done.10 = bf16[4,8192]{1,0:T(4,128)(2,1)S(1)} collective-permute-done((bf16[4,8192]{1,0:T(4,128)(2,1)S(1)}, bf16[4,8192]{1,0:T(4,128)(2,1)S(1)}, u32[]{:S(2)}, u32[]{:S(2)}) %collective-permute-start.10) | collective-permute-done | bytes 65568 | tf_op jit(solution)/shard_map/ppermute | solution.py:133
  39.4 1.2 %collective-permute-done.8 = bf16[4,8192]{1,0:T(4,128)(2,1)S(1)} collective-permute-done((bf16[4,8192]{1,0:T(4,128)(2,1)S(1)}, bf16[4,8192]{1,0:T(4,128)(2,1)S(1)}, u32[]{:S(2)}, u32[]{:S(2)}) %collective-permute-start.8) | collective-permute-done | bytes 65568 | tf_op jit(solution)/shard_map/ppermute | solution.py:133
  40.5 0.3 collective-permute-done.9
  40.9 0.8 %collective-permute-start.11 = (bf16[2,8192]{1,0:T(2,128)(2,1)S(1)}, bf16[2,8192]{1,0:T(2,128)(2,1)S(1)}, u32[]{:S(2)}, u32[]{:S(2)}) collective-permute-start(bf16[2,8192]{1,0:T(2,128)(2,1)S(1)} %slice.75), channel_id=1, source_target_pairs={{0,8},{1,9},{2,10},{3,11},{4,12},{5,13},{6,14},{7,15},{8,0},{9,1},... | collective-permute-start | bytes 98312 | tf_op jit(solution)/shard_map/ppermute | solution.py:133
  41.7 4.2 %collective-permute-done.11 = bf16[2,8192]{1,0:T(2,128)(2,1)S(1)} collective-permute-done((bf16[2,8192]{1,0:T(2,128)(2,1)S(1)}, bf16[2,8192]{1,0:T(2,128)(2,1)S(1)}, u32[]{:S(2)}, u32[]{:S(2)}) %collective-permute-start.11) | collective-permute-done | bytes 32800 | tf_op jit(solution)/shard_map/ppermute | solution.py:133
  46.0 0.3 collective-permute-start.12
  46.3 3.7 %collective-permute-done.12 = bf16[1,8192]{1,0:T(2,128)(2,1)S(1)} collective-permute-done((bf16[1,8192]{1,0:T(2,128)(2,1)S(1)}, bf16[1,8192]{1,0:T(2,128)(2,1)S(1)}, u32[]{:S(2)}, u32[]{:S(2)}) %collective-permute-start.12) | collective-permute-done | bytes 16416 | tf_op jit(solution)/shard_map/ppermute | solution.py:133
  50.0 0.7 %fusion.8 = bf16[1,8192]{1,0:T(2,128)(2,1)} fusion(f32[2,8192]{1,0:T(2,128)S(1)} %slice_add_fusion.1, bf16[1,8192]{1,0:T(2,128)(2,1)S(1)} %collective-permute-done.12), kind=kLoop, calls=%fused_computation.23 | loop fusion | flops 24576 | bytes 65536 | tf_op jit(solution)/shard_map/convert_element_type | solution.py:549
  (19 shorter events, 0.6 us)
Async XLA Ops:
  2.1 1.5 %collective-permute-start = (bf16[2,16,1664]{2,1,0:T(8,128)(2,1)S(1)}, bf16[2,16,1664]{2,1,0:T(8,128)(2,1)S(1)}, u32[]{:S(2)}, u32[]{:S(2)}) collective-permute-start(bf16[2,16,1664]{2,1,0:T(8,128)(2,1)S(1)} %local_rotation.1), channel_id=1, source_target_pairs={{0,1},{1,0},{2,3},{3,2},{4,5},{5,4},{6,7},{7,6},{8,9},{9,8},{10,11... | collective-permute-start | bytes 319496 | tf_op jit(solution)/shard_map/ppermute | solution.py:133
  3.6 7.6 %collective-permute-start.1 = (bf16[16,1664]{1,0:T(8,128)(2,1)S(1)}, bf16[16,1664]{1,0:T(8,128)(2,1)S(1)}, u32[]{:S(2)}, u32[]{:S(2)}) collective-permute-start(bf16[16,1664]{1,0:T(8,128)(2,1)S(1)} %get-tuple-element.32), channel_id=1, source_target_pairs={{0,2},{1,3},{2,0},{3,1},{4,6},{5,7},{6,4},{7,5},{8,10},{9,11},{10,... | collective-permute-start | bytes 159752 | tf_op jit(solution)/shard_map/ppermute | solution.py:133
  6.6 4.7 %collective-permute-start.2 = (bf16[16,1664]{1,0:T(8,128)(2,1)S(1)}, bf16[16,1664]{1,0:T(8,128)(2,1)S(1)}, u32[]{:S(2)}, u32[]{:S(2)}) collective-permute-start(bf16[16,1664]{1,0:T(8,128)(2,1)S(1)} %get-tuple-element.33), channel_id=1, source_target_pairs={{0,16},{1,17},{2,18},{3,19},{4,20},{5,21},{6,22},{7,23},{8,24},{9,... | collective-permute-start | bytes 159752 | tf_op jit(solution)/shard_map/ppermute | solution.py:133
  8.0 5.0 %collective-permute-start.3 = (bf16[16,1664]{1,0:T(8,128)(2,1)S(1)}, bf16[16,1664]{1,0:T(8,128)(2,1)S(1)}, u32[]{:S(2)}, u32[]{:S(2)}) collective-permute-start(bf16[16,1664]{1,0:T(8,128)(2,1)S(1)} %get-tuple-element.33), channel_id=1, source_target_pairs={{0,18},{1,19},{2,16},{3,17},{4,22},{5,23},{6,20},{7,21},{8,26},{9,... | collective-permute-start | bytes 159752 | tf_op jit(solution)/shard_map/ppermute | solution.py:133
  13.1 10.1 %collective-permute-start.4 = (bf16[32,1664]{1,0:T(8,128)(2,1)S(1)}, bf16[32,1664]{1,0:T(8,128)(2,1)S(1)}, u32[]{:S(2)}, u32[]{:S(2)}) collective-permute-start(bf16[32,1664]{1,0:T(8,128)(2,1)S(1)} %pad_maximum_fusion.own_ref), channel_id=1, source_target_pairs={{0,12},{1,13},{2,14},{3,15},{4,8},{5,9},{6,10},{7,11},{8,4},{9,5},... | collective-permute-start | bytes 319496 | tf_op jit(solution)/shard_map/ppermute | solution.py:133
  16.8 7.6 %collective-permute-start.5 = (bf16[32,1664]{1,0:T(8,128)(2,1)S(1)}, bf16[32,1664]{1,0:T(8,128)(2,1)S(1)}, u32[]{:S(2)}, u32[]{:S(2)}) collective-permute-start(bf16[32,1664]{1,0:T(8,128)(2,1)S(1)} %pad_maximum_fusion.own_ref), channel_id=1, source_target_pairs={{0,8},{1,9},{2,10},{3,11},{4,12},{5,13},{6,14},{7,15},{8,0},{9,1},... | collective-permute-start | bytes 319496 | tf_op jit(solution)/shard_map/ppermute | solution.py:133
  16.8 7.6 %collective-permute-start.6 = (bf16[32,1664]{1,0:T(8,128)(2,1)S(1)}, bf16[32,1664]{1,0:T(8,128)(2,1)S(1)}, u32[]{:S(2)}, u32[]{:S(2)}) collective-permute-start(bf16[32,1664]{1,0:T(8,128)(2,1)S(1)} %pad_maximum_fusion.own_ref), channel_id=1, source_target_pairs={{0,4},{1,5},{2,6},{3,7},{4,0},{5,1},{6,2},{7,3},{8,12},{9,13},{10,... | collective-permute-start | bytes 319496 | tf_op jit(solution)/shard_map/ppermute | solution.py:133
  32.3 1.6 %collective-permute-start.7 = (bf16[16,8192]{1,0:T(8,128)(2,1)S(1)}, bf16[16,8192]{1,0:T(8,128)(2,1)S(1)}, u32[]{:S(2)}, u32[]{:S(2)}) collective-permute-start(bf16[16,8192]{1,0:T(8,128)(2,1)S(1)} %get-tuple-element.26), channel_id=1, source_target_pairs={{0,1},{1,0},{2,3},{3,2},{4,5},{5,4},{6,7},{7,6},{8,9},{9,8},{10,11... | collective-permute-start | bytes 786440 | tf_op jit(solution)/shard_map/ppermute | solution.py:133
  34.0 5.3 %collective-permute-start.10 = (bf16[4,8192]{1,0:T(4,128)(2,1)S(1)}, bf16[4,8192]{1,0:T(4,128)(2,1)S(1)}, u32[]{:S(2)}, u32[]{:S(2)}) collective-permute-start(bf16[4,8192]{1,0:T(4,128)(2,1)S(1)} %get-tuple-element.30), channel_id=1, source_target_pairs={{0,18},{1,19},{2,16},{3,17},{4,22},{5,23},{6,20},{7,21},{8,26},{9,... | collective-permute-start | bytes 196616 | tf_op jit(solution)/shard_map/ppermute | solution.py:133
  36.0 4.6 %collective-permute-start.8 = (bf16[4,8192]{1,0:T(4,128)(2,1)S(1)}, bf16[4,8192]{1,0:T(4,128)(2,1)S(1)}, u32[]{:S(2)}, u32[]{:S(2)}) collective-permute-start(bf16[4,8192]{1,0:T(4,128)(2,1)S(1)} %get-tuple-element.29), channel_id=1, source_target_pairs={{0,2},{1,3},{2,0},{3,1},{4,6},{5,7},{6,4},{7,5},{8,10},{9,11},{10,... | collective-permute-start | bytes 196616 | tf_op jit(solution)/shard_map/ppermute | solution.py:133
  36.5 4.3 %collective-permute-start.9 = (bf16[4,8192]{1,0:T(4,128)(2,1)S(1)}, bf16[4,8192]{1,0:T(4,128)(2,1)S(1)}, u32[]{:S(2)}, u32[]{:S(2)}) collective-permute-start(bf16[4,8192]{1,0:T(4,128)(2,1)S(1)} %get-tuple-element.31), channel_id=1, source_target_pairs={{0,16},{1,17},{2,18},{3,19},{4,20},{5,21},{6,22},{7,23},{8,24},{9,... | collective-permute-start | bytes 196616 | tf_op jit(solution)/shard_map/ppermute | solution.py:133
  40.9 5.0 %collective-permute-start.11 = (bf16[2,8192]{1,0:T(2,128)(2,1)S(1)}, bf16[2,8192]{1,0:T(2,128)(2,1)S(1)}, u32[]{:S(2)}, u32[]{:S(2)}) collective-permute-start(bf16[2,8192]{1,0:T(2,128)(2,1)S(1)} %slice.75), channel_id=1, source_target_pairs={{0,8},{1,9},{2,10},{3,11},{4,12},{5,13},{6,14},{7,15},{8,0},{9,1},... | collective-permute-start | bytes 98312 | tf_op jit(solution)/shard_map/ppermute | solution.py:133
  46.0 4.0 %collective-permute-start.12 = (bf16[1,8192]{1,0:T(2,128)(2,1)S(1)}, bf16[1,8192]{1,0:T(2,128)(2,1)S(1)}, u32[]{:S(2)}, u32[]{:S(2)}) collective-permute-start(bf16[1,8192]{1,0:T(2,128)(2,1)S(1)} %slice.76), channel_id=1, source_target_pairs={{0,4},{1,5},{2,6},{3,7},{4,0},{5,1},{6,2},{7,3},{8,12},{9,13},{10,... | collective-permute-start | bytes 49160 | tf_op jit(solution)/shard_map/ppermute | solution.py:133

commit v4 on v3

--- a/solution.py
+++ b/solution.py
@@ -18,7 +18,7 @@
 MIB = 2**20
 TILE = 512
 CHUNK = 256
-FETCHES = (3, 5, 4)
+FETCHES = (1, 2, 7, 3)
 LANES = 128
 
 
@@ -165,7 +165,9 @@
     gate_hbm,
     up_hbm,
     table_hbm,
+    scales_hbm,
     out_ref,
+    scales_ref,
     gate_in,
     up_in,
     table,
@@ -178,7 +180,7 @@
     copies = [
         pltpu.make_async_copy(source, target, sems.at[index])
         for index, (source, target) in enumerate(
-            ((gate_hbm, gate_in), (up_hbm, up_in), (table_hbm, table))
+            ((gate_hbm, gate_in), (up_hbm, up_in), (table_hbm, table), (scales_hbm, scales_ref))
         )
     ]
     for copy in copies:
@@ -224,9 +226,10 @@
                 out_ref[part, :, offset : offset + PAIRS] = mix_sc[
                     pl.ds(start, rows), parity * padded : parity * padded + PAIRS
                 ]
-
-
-def local_rotation(group, gate_act, up_act):
+    copies[3].wait()
+
+
+def local_rotation(group, gate_act, up_act, scales):
     units, rows = gate_act.shape
     blocks = units // HAD_LOCAL
     padded = -(-PAIRS // LANES) * LANES
@@ -239,9 +242,12 @@
     vmem = pl.BlockSpec(memory_space=pltpu.VMEM)
     return pl.pallas_call(
         local_kernel,
-        in_specs=[pl.BlockSpec(memory_space=pltpu.SMEM)] + [hbm] * 3,
-        out_specs=vmem,
-        out_shape=jax.ShapeDtypeStruct((2, rows, units // 2), jnp.bfloat16),
+        in_specs=[pl.BlockSpec(memory_space=pltpu.SMEM)] + [hbm] * 4,
+        out_specs=[vmem, vmem],
+        out_shape=[
+            jax.ShapeDtypeStruct((2, rows, units // 2), jnp.bfloat16),
+            pltpu.VMEM(scales.shape, scales.dtype),
+        ],
         scratch_shapes=[
             pltpu.VMEM((rows, units), jnp.bfloat16),
             pltpu.VMEM((rows, units), jnp.bfloat16),
@@ -249,7 +255,7 @@
             pltpu.VMEM((rows, units), jnp.float32),
             pltpu.VMEM((blocks * rows, HAD_LOCAL), jnp.bfloat16),
             pltpu.VMEM((blocks * rows, 2 * padded), jnp.bfloat16),
-            pltpu.SemaphoreType.DMA((3,)),
+            pltpu.SemaphoreType.DMA((4,)),
         ],
         compiler_params=pltpu.CompilerParams(vmem_limit_bytes=6 * MIB),
         cost_estimate=pl.CostEstimate(flops=10**8, bytes_accessed=8 * MIB, transcendentals=10**5),
@@ -259,6 +265,7 @@
         in_hbm(gate_act.T),
         in_hbm(up_act.T),
         in_hbm(jnp.asarray(table, jnp.bfloat16)),
+        in_hbm(scales),
     )
 
 
@@ -290,49 +297,55 @@
         target[height + top : height + top + WORDS_PER_GROUP, pl.ds(at, tile)] = high
 
 
-def fetch_kernel(group_ref, codes_hbm, scales_hbm, next_ref, wide_ref, scales, sems):
+def first_kernel(group_ref, codes_hbm, scales_in, out_ref, next_ref, wide_ref, words, sems):
+    group = group_ref[0]
+    own, height, tile = words.shape
     ahead = next_ref.shape[0]
-    arrival = pltpu.make_async_copy(scales_hbm, scales, sems.at[ahead])
-    arrival.start()
-    copies = fetches(codes_hbm, group_ref[0], 0, ahead, next_ref, sems, 0)
+    copies = fetches(codes_hbm, group, 0, own, words, sems, 0)
+    copies += fetches(codes_hbm, group, own, ahead, next_ref, sems, own)
     for copy in copies:
         copy.start()
-    arrival.wait()
-    widen(group_ref[0], scales, wide_ref)
-    for copy in copies:
+    widen(group, scales_in, wide_ref)
+    for i in range(own):
+        copies[i].wait()
+        unpack_tile(
+            words.at[i], wide_ref, i * tile, out_ref, i * tile, range(height // WORDS_PER_GROUP)
+        )
+    for copy in copies[own:]:
         copy.wait()
 
 
-def fetch(group, codes, scales, ahead):
+def first_unpack(group, codes, scales, own, ahead):
     words, width = codes.shape
     hbm = pl.BlockSpec(memory_space=pltpu.HBM)
     vmem = pl.BlockSpec(memory_space=pltpu.VMEM)
     return pl.pallas_call(
-        fetch_kernel,
-        in_specs=[pl.BlockSpec(memory_space=pltpu.SMEM), hbm, hbm],
-        out_specs=[vmem, vmem],
+        first_kernel,
+        in_specs=[pl.BlockSpec(memory_space=pltpu.SMEM), hbm, vmem],
+        out_specs=[vmem] * 3,
         out_shape=[
+            pltpu.VMEM((words, own * TILE), jnp.bfloat16),
             pltpu.VMEM((ahead, words // 2, TILE), codes.dtype),
             pltpu.VMEM((words // 2 // WORDS_PER_GROUP, width), jnp.float32),
         ],
         scratch_shapes=[
-            pltpu.VMEM(scales.shape, scales.dtype),
-            pltpu.SemaphoreType.DMA((ahead + 1,)),
-        ],
-        compiler_params=pltpu.CompilerParams(vmem_limit_bytes=4 * MIB),
+            pltpu.VMEM((own, words // 2, TILE), codes.dtype),
+            pltpu.SemaphoreType.DMA((own + ahead,)),
+        ],
+        compiler_params=pltpu.CompilerParams(vmem_limit_bytes=(2 + 2 * own) * MIB),
         cost_estimate=pl.CostEstimate(
-            flops=0, bytes_accessed=ahead * words * TILE * 2, transcendentals=0
+            flops=0, bytes_accessed=(own + ahead) * words * TILE * 2, transcendentals=0
         ),
-        name="fetch",
-    )(group, in_hbm(codes), in_hbm(scales))
-
-
-def unpack_kernel(group_ref, codes_hbm, scales_ref, given, out_ref, next_ref, words, sems):
+        name="first_unpack",
+    )(group, in_hbm(codes), pltpu.with_memory_space_constraint(scales, pltpu.VMEM))
+
+
+def unpack_kernel(first, group_ref, codes_hbm, scales_ref, given, out_ref, next_ref, words, sems):
     group = group_ref[0]
     count, height, tile = given.shape
     own, ahead = words.shape[0], next_ref.shape[0]
-    copies = fetches(codes_hbm, group, count, own, words, sems, 0)
-    copies += fetches(codes_hbm, group, count + own, ahead, next_ref, sems, own)
+    copies = fetches(codes_hbm, group, first + count, own, words, sems, 0)
+    copies += fetches(codes_hbm, group, first + count + own, ahead, next_ref, sems, own)
     for copy in copies:
         copy.start()
     spans = range(height // WORDS_PER_GROUP)
@@ -340,7 +353,7 @@
     @pl.loop(0, count)
     def _(i):
         at = pl.multiple_of(i * tile, tile)
-        unpack_tile(given.at[i], scales_ref, at, out_ref, at, spans)
+        unpack_tile(given.at[i], scales_ref, first * tile + at, out_ref, at, spans)
 
     @pl.loop(0, own)
     def _(i):
@@ -348,19 +361,19 @@
             codes_hbm.at[pl.ds(0, height), pl.ds(0, tile)], words.at[i], sems.at[i]
         ).wait()
         at = pl.multiple_of((count + i) * tile, tile)
-        unpack_tile(words.at[i], scales_ref, at, out_ref, at, spans)
+        unpack_tile(words.at[i], scales_ref, first * tile + at, out_ref, at, spans)
 
     for copy in copies[own:]:
         copy.wait()
 
 
-def unpack(group, codes, scales, given, own, ahead):
+def unpack(group, codes, scales, given, first, own, ahead):
     words = codes.shape[0]
     hbm = pl.BlockSpec(memory_space=pltpu.HBM)
     vmem = pl.BlockSpec(memory_space=pltpu.VMEM)
     columns = (given.shape[0] + own) * TILE
     return pl.pallas_call(
-        unpack_kernel,
+        functools.partial(unpack_kernel, first),
         in_specs=[pl.BlockSpec(memory_space=pltpu.SMEM), hbm, vmem, vmem],
         out_specs=[vmem, vmem],
         out_shape=[
@@ -503,8 +516,8 @@
     place = lax.axis_index("tensor").astype(jnp.int32)[None]
 
     tiles = width // TILE
-    at_near, at_far, for_product = (tiles * n // 16 for n in FETCHES)
-    parts = local_rotation(group, gate_act, up_act)
+    at_near, for_far, at_far, for_product = (tiles * n // 16 for n in FETCHES)
+    parts, scales = local_rotation(group, gate_act, up_act, scales)
     near = exchanged(parts, 0, 1)
     core = place[0] % 2
     parts = jnp.where(
@@ -515,22 +528,18 @@
     parts, group_then = lax.optimization_barrier((parts, group))
     mine, theirs = parts[0], parts[1]
     across_y = exchanged(mine, 0, 2).astype(jnp.float32)
+    across_xy = exchanged(theirs, 1, 2).astype(jnp.float32)
     across_x = exchanged(theirs, 1, 0).astype(jnp.float32)
-    across_xy = exchanged(theirs, 1, 2).astype(jnp.float32)
-    words, scales = fetch(group_then, codes, scales, at_near)
-    low = place[0] // 2 % 2 == 0
-    here = mine.astype(jnp.float32)
+    early, words, scales = first_unpack(group_then, codes, scales, at_near, for_far)
+    sign = jnp.where(place[0] // 2 % 2 == 0, 1.0, -1.0)
     both = jnp.concatenate(
-        [
-            jnp.where(low, here + across_y, across_y - here),
-            jnp.where(low, across_x + across_xy, across_xy - across_x),
-        ]
+        [mine.astype(jnp.float32) * sign + across_y, across_xy + across_x * sign]
     ).astype(jnp.bfloat16)
     both, group_then, words = lax.optimization_barrier((both, group, words))
     others = [exchanged(both, 0, 4 * d) for d in range(count - 1, 0, -1)]
-    ready, words = unpack(group_then, codes, scales, words, at_far, for_product)
+    late, words = unpack(group_then, codes, scales, words, at_near, at_far, for_product)
     keep, send = product(
-        jnp.concatenate([group, place]), codes, words, scales, both, others, [ready]
+        jnp.concatenate([group, place]), codes, words, scales, both, others, [early, late]
     )
 
     keep = keep + exchanged(send, 0, 1).astype(jnp.float32)
@@ -542,11 +551,11 @@
         + exchanged(send[1], 1, 0).astype(jnp.float32)
         + exchanged(send[2], 1, 2).astype(jnp.float32)
     )
-    while keep.shape[0] > each:
-        half = keep.shape[0] // 2
-        send = keep[half:].astype(jnp.bfloat16)
-        keep = keep[:half] + exchanged(send, 0, 4 * half // each).astype(jnp.float32)
-    return keep.astype(jnp.bfloat16)
+    send = keep.astype(jnp.bfloat16)
+    total = keep[:each]
+    for d in range(count - 1, 0, -1):
+        total = total + exchanged(send[d * each : (d + 1) * each], 0, 4 * d).astype(jnp.float32)
+    return total.astype(jnp.bfloat16)
 
 
 def body(gate_act, up_act, codes, scales):

time: 50.8 us -> 47.4 us (0.933)
  waiting for transfers between devices: 16.6 us -> 11.2 us
  starting transfers between devices: 14.2 us -> 17.6 us
  Pallas kernels: 18.6 us -> 17.2 us
    ppermute x13 -> x14, waiting for transfers between devices: 16.6 us -> 11.2 us  [exchanged(): return lax.ppermute(value, AXES, pairs)]
    ppermute x13 -> x14, starting transfers between devices: 14.2 us -> 17.6 us  [exchanged(): return lax.ppermute(value, AXES, pairs)]
    pallas_call x1, Pallas kernels: 7.9 us -> 6.57 us  [product(): pl.pallas_call(functools.partial(product_kernel, len(ready)), in_specs=[p...]
  transfers between devices with their start and end apart: 13 -> 14, of which waited for: 9 -> 9; matrix products, arithmetic and copies ran while one was open for 0% -> 0% of each run, Pallas kernels for 17% -> 18%
where the time goes in v4:
time: 47.4 us; the launch traced here: 47.3 us
  starting transfers between devices  17.6 us (37%)
  Pallas kernels  17.2 us (36%)
  waiting for transfers between devices  11.2 us (24%)
  other arithmetic  0.99 us (2%)
    ppermute x14, starting transfers between devices, exchanged(): return lax.ppermute(value, AXES, pairs)  17.6 us
    ppermute x14, waiting for transfers between devices, exchanged(): return lax.ppermute(value, AXES, pairs)  11.2 us
    pallas_call x1, Pallas kernels, product(): pl.pallas_call(functools.partial(product_kernel, len(ready)), in_specs=[p...  6.57 us
    pallas_call x1, Pallas kernels, unpack(): pl.pallas_call(functools.partial(unpack_kernel, first), in_specs=[pl.Bloc...  6.05 us
    pallas_call x1, Pallas kernels, first_unpack(): pl.pallas_call(first_kernel, in_specs=[pl.BlockSpec(memory_space=pltpu.SM...  2.52 us
    pallas_call x1, Pallas kernels, local_rotation(): pl.pallas_call(local_kernel, in_specs=[pl.BlockSpec(memory_space=pltpu.SM...  2.08 us
  transfers between devices with their start and end apart: 14, of which 9 were waited for; matrix products, arithmetic and copies ran while one was open for 0% of the time, Pallas kernels for 18%

profile of v4, /device:TPU:0, one launch (start us, length us, event | category | flops | bytes accessed | tf_op | source)
XLA Modules:
  0.0 47.3 jit_solution(3398787208523742476)
XLA Ops:
  0.0 2.1 %local_rotation.1 = (bf16[2,16,1664]{2,1,0:T(8,128)(2,1)S(1)}, bf16[104,8192]{1,0:T(8,128)(2,1)S(1)}) custom-call(s32[1]{0:T(128)} %bitcast.group_ref, bf16[16,3328]{1,0:T(8,128)(2,1)} %bitcast.10, bf16[16,3328]{1,0:T(8,128)(2,1)} %bitcast.11, bf16[1664,128]{1,0:T(8,128)(2,1)} %constant.44.clone.table_hbm, bf16[104,8192]{1,0:T(8,128)(2,1)} %scales_hbm.1), custom_call_target="tpu_custom_call" | custom-call | flops 100000000 | bytes 8388608 | tf_op jit(solution)/shard_map/local_rotation/pallas_call | solution.py:243
  2.1 0.5 %collective-permute-start = (bf16[2,16,1664]{2,1,0:T(8,128)(2,1)S(1)}, bf16[2,16,1664]{2,1,0:T(8,128)(2,1)S(1)}, u32[]{:S(2)}, u32[]{:S(2)}) collective-permute-start(bf16[2,16,1664]{2,1,0:T(8,128)(2,1)S(1)} %get-tuple-element.19), channel_id=1, source_target_pairs={{0,1},{1,0},{2,3},{3,2},{4,5},{5,4},{6,7},{7,6},{8,9},{9,8},{10,11... | collective-permute-start | bytes 319496 | tf_op jit(solution)/shard_map/ppermute | solution.py:133
  2.6 1.0 %collective-permute-done = bf16[2,16,1664]{2,1,0:T(8,128)(2,1)S(1)} collective-permute-done((bf16[2,16,1664]{2,1,0:T(8,128)(2,1)S(1)}, bf16[2,16,1664]{2,1,0:T(8,128)(2,1)S(1)}, u32[]{:S(2)}, u32[]{:S(2)}) %collective-permute-start) | collective-permute-done | bytes 106528 | tf_op jit(solution)/shard_map/ppermute | solution.py:133
  3.6 2.9 %collective-permute-start.1 = (bf16[16,1664]{1,0:T(8,128)(2,1)S(1)}, bf16[16,1664]{1,0:T(8,128)(2,1)S(1)}, u32[]{:S(2)}, u32[]{:S(2)}) collective-permute-start(bf16[16,1664]{1,0:T(8,128)(2,1)S(1)} %get-tuple-element.40), channel_id=1, source_target_pairs={{0,2},{1,3},{2,0},{3,1},{4,6},{5,7},{6,4},{7,5},{8,10},{9,11},{10,... | collective-permute-start | bytes 159752 | tf_op jit(solution)/shard_map/ppermute | solution.py:133
  6.6 1.4 %collective-permute-start.2 = (bf16[16,1664]{1,0:T(8,128)(2,1)S(1)}, bf16[16,1664]{1,0:T(8,128)(2,1)S(1)}, u32[]{:S(2)}, u32[]{:S(2)}) collective-permute-start(bf16[16,1664]{1,0:T(8,128)(2,1)S(1)} %get-tuple-element.41), channel_id=1, source_target_pairs={{0,18},{1,19},{2,16},{3,17},{4,22},{5,23},{6,20},{7,21},{8,26},{9,... | collective-permute-start | bytes 159752 | tf_op jit(solution)/shard_map/ppermute | solution.py:133
  8.0 0.1 collective-permute-start.3
  8.1 2.5 %first_unpack.1 = (bf16[1664,512]{1,0:T(8,128)(2,1)S(1)}, s32[2,832,512]{2,1,0:T(8,128)S(1)}, f32[52,8192]{1,0:T(8,128)S(1)}) custom-call(s32[1]{0:T(128)} %bitcast.group_ref, s32[1664,8192]{1,0:T(8,128)} %codes_hbm.5, bf16[104,8192]{1,0:T(8,128)(2,1)S(1)} %get-tuple-element.22.scales_in), custom_call_target="tpu_custom_call" | custom-call | bytes 5111808 | tf_op jit(solution)/shard_map/first_unpack/pallas_call | solution.py:322
  10.7 1.3 %collective-permute-done.2 = bf16[16,1664]{1,0:T(8,128)(2,1)S(1)} collective-permute-done((bf16[16,1664]{1,0:T(8,128)(2,1)S(1)}, bf16[16,1664]{1,0:T(8,128)(2,1)S(1)}, u32[]{:S(2)}, u32[]{:S(2)}) %collective-permute-start.2) | collective-permute-done | bytes 53280 | tf_op jit(solution)/shard_map/ppermute | solution.py:133
  12.2 3.7 %collective-permute-start.4 = (bf16[32,1664]{1,0:T(8,128)(2,1)S(1)}, bf16[32,1664]{1,0:T(8,128)(2,1)S(1)}, u32[]{:S(2)}, u32[]{:S(2)}) collective-permute-start(bf16[32,1664]{1,0:T(8,128)(2,1)S(1)} %pad_maximum_fusion.own_ref), channel_id=1, source_target_pairs={{0,12},{1,13},{2,14},{3,15},{4,8},{5,9},{6,10},{7,11},{8,4},{9,5},... | collective-permute-start | bytes 319496 | tf_op jit(solution)/shard_map/ppermute | solution.py:133
  15.8 0.8 %collective-permute-start.6 = (bf16[32,1664]{1,0:T(8,128)(2,1)S(1)}, bf16[32,1664]{1,0:T(8,128)(2,1)S(1)}, u32[]{:S(2)}, u32[]{:S(2)}) collective-permute-start(bf16[32,1664]{1,0:T(8,128)(2,1)S(1)} %pad_maximum_fusion.own_ref), channel_id=1, source_target_pairs={{0,4},{1,5},{2,6},{3,7},{4,0},{5,1},{6,2},{7,3},{8,12},{9,13},{10,... | collective-permute-start | bytes 319496 | tf_op jit(solution)/shard_map/ppermute | solution.py:133
  16.7 6.0 %unpack.1 = (bf16[1664,4608]{1,0:T(8,128)(2,1)S(1)}, s32[3,832,512]{2,1,0:T(8,128)S(1)}) custom-call(s32[1]{0:T(128)} %bitcast.group_ref, s32[1664,8192]{1,0:T(8,128)} %codes_hbm.5, f32[52,8192]{1,0:T(8,128)S(1)} %get-tuple-element.25.scales_ref, s32[2,832,512]{2,1,0:T(8,128)S(1)} %get-tuple-element.26.given), custom_call_target="tpu_custom_call" | custom-call | flops 61341696 | bytes 30670848 | tf_op jit(solution)/shard_map/unpack/pallas_call | solution.py:375
  22.8 1.4 %collective-permute-done.5.refs_3_ = bf16[32,1664]{1,0:T(8,128)(2,1)S(1)} collective-permute-done((bf16[32,1664]{1,0:T(8,128)(2,1)S(1)}, bf16[32,1664]{1,0:T(8,128)(2,1)S(1)}, u32[]{:S(2)}, u32[]{:S(2)}) %collective-permute-start.5) | collective-permute-done | bytes 106528 | tf_op jit(solution)/shard_map/ppermute | solution.py:133
  24.2 6.6 %product.1 = (f32[16,8192]{1,0:T(8,128)S(1)}, bf16[16,8192]{1,0:T(8,128)(2,1)S(1)}) custom-call(s32[2]{0:T(128)S(1)} %pad_add_fusion.place_ref, s32[1664,8192]{1,0:T(8,128)} %codes_hbm.5, s32[3,832,512]{2,1,0:T(8,128)S(1)} %get-tuple-element.27.given, f32[52,8192]{1,0:T(8,128)S(1)} %get-tuple-element.25.scales_ref, ...), custom_call_target="tpu_custom_call" | custom-call | tf_op jit(solution)/shard_map/product/pallas_call | solution.py:482
  30.8 1.5 %collective-permute-done.7 = bf16[16,8192]{1,0:T(8,128)(2,1)S(1)} collective-permute-done((bf16[16,8192]{1,0:T(8,128)(2,1)S(1)}, bf16[16,8192]{1,0:T(8,128)(2,1)S(1)}, u32[]{:S(2)}, u32[]{:S(2)}) %collective-permute-start.7) | collective-permute-done | bytes 262176 | tf_op jit(solution)/shard_map/ppermute | solution.py:133
  32.5 1.6 %collective-permute-start.10 = (bf16[4,8192]{1,0:T(4,128)(2,1)S(1)}, bf16[4,8192]{1,0:T(4,128)(2,1)S(1)}, u32[]{:S(2)}, u32[]{:S(2)}) collective-permute-start(bf16[4,8192]{1,0:T(4,128)(2,1)S(1)} %get-tuple-element.38), channel_id=1, source_target_pairs={{0,18},{1,19},{2,16},{3,17},{4,22},{5,23},{6,20},{7,21},{8,26},{9,... | collective-permute-start | bytes 196616 | tf_op jit(solution)/shard_map/ppermute | solution.py:133
  34.1 0.5 %collective-permute-start.8 = (bf16[4,8192]{1,0:T(4,128)(2,1)S(1)}, bf16[4,8192]{1,0:T(4,128)(2,1)S(1)}, u32[]{:S(2)}, u32[]{:S(2)}) collective-permute-start(bf16[4,8192]{1,0:T(4,128)(2,1)S(1)} %get-tuple-element.37), channel_id=1, source_target_pairs={{0,2},{1,3},{2,0},{3,1},{4,6},{5,7},{6,4},{7,5},{8,10},{9,11},{10,... | collective-permute-start | bytes 196616 | tf_op jit(solution)/shard_map/ppermute | solution.py:133
  34.6 1.4 %collective-permute-start.9 = (bf16[4,8192]{1,0:T(4,128)(2,1)S(1)}, bf16[4,8192]{1,0:T(4,128)(2,1)S(1)}, u32[]{:S(2)}, u32[]{:S(2)}) collective-permute-start(bf16[4,8192]{1,0:T(4,128)(2,1)S(1)} %get-tuple-element.39), channel_id=1, source_target_pairs={{0,16},{1,17},{2,18},{3,19},{4,20},{5,21},{6,22},{7,23},{8,24},{9,... | collective-permute-start | bytes 196616 | tf_op jit(solution)/shard_map/ppermute | solution.py:133
  36.1 1.7 %collective-permute-done.10 = bf16[4,8192]{1,0:T(4,128)(2,1)S(1)} collective-permute-done((bf16[4,8192]{1,0:T(4,128)(2,1)S(1)}, bf16[4,8192]{1,0:T(4,128)(2,1)S(1)}, u32[]{:S(2)}, u32[]{:S(2)}) %collective-permute-start.10) | collective-permute-done | bytes 65568 | tf_op jit(solution)/shard_map/ppermute | solution.py:133
  37.8 1.2 %collective-permute-done.8 = bf16[4,8192]{1,0:T(4,128)(2,1)S(1)} collective-permute-done((bf16[4,8192]{1,0:T(4,128)(2,1)S(1)}, bf16[4,8192]{1,0:T(4,128)(2,1)S(1)}, u32[]{:S(2)}, u32[]{:S(2)}) %collective-permute-start.8) | collective-permute-done | bytes 65568 | tf_op jit(solution)/shard_map/ppermute | solution.py:133
  39.2 2.6 %collective-permute-start.11 = (bf16[1,8192]{1,0:T(2,128)(2,1)S(1)}, bf16[1,8192]{1,0:T(2,128)(2,1)S(1)}, u32[]{:S(2)}, u32[]{:S(2)}) collective-permute-start(bf16[1,8192]{1,0:T(2,128)(2,1)S(1)} %get-tuple-element.42), channel_id=1, source_target_pairs={{0,12},{1,13},{2,14},{3,15},{4,8},{5,9},{6,10},{7,11},{8,4},{9,5},... | collective-permute-start | bytes 49160 | tf_op jit(solution)/shard_map/ppermute | solution.py:133
  41.8 1.9 %collective-permute-start.13 = (bf16[1,8192]{1,0:T(2,128)(2,1)S(1)}, bf16[1,8192]{1,0:T(2,128)(2,1)S(1)}, u32[]{:S(2)}, u32[]{:S(2)}) collective-permute-start(bf16[1,8192]{1,0:T(2,128)(2,1)S(1)} %get-tuple-element.43), channel_id=1, source_target_pairs={{0,4},{1,5},{2,6},{3,7},{4,0},{5,1},{6,2},{7,3},{8,12},{9,13},{10,... | collective-permute-start | bytes 49160 | tf_op jit(solution)/shard_map/ppermute | solution.py:133
  43.6 1.3 %collective-permute-done.11 = bf16[1,8192]{1,0:T(2,128)(2,1)S(1)} collective-permute-done((bf16[1,8192]{1,0:T(2,128)(2,1)S(1)}, bf16[1,8192]{1,0:T(2,128)(2,1)S(1)}, u32[]{:S(2)}, u32[]{:S(2)}) %collective-permute-start.11) | collective-permute-done | bytes 16416 | tf_op jit(solution)/shard_map/ppermute | solution.py:133
  45.0 1.6 %collective-permute-done.12 = bf16[1,8192]{1,0:T(2,128)(2,1)S(1)} collective-permute-done((bf16[1,8192]{1,0:T(2,128)(2,1)S(1)}, bf16[1,8192]{1,0:T(2,128)(2,1)S(1)}, u32[]{:S(2)}, u32[]{:S(2)}) %collective-permute-start.12) | collective-permute-done | bytes 16416 | tf_op jit(solution)/shard_map/ppermute | solution.py:133
  46.6 0.7 %fusion.6 = bf16[1,8192]{1,0:T(2,128)(2,1)} fusion(bf16[1,8192]{1,0:T(2,128)(2,1)S(1)} %collective-permute-done.13, bf16[1,8192]{1,0:T(2,128)(2,1)S(1)} %collective-permute-done.12, bf16[1,8192]{1,0:T(2,128)(2,1)S(1)} %collective-permute-done.11, f32[4,8192]{1,0:T(4,128)S(1)} %get-tuple-element.34), kind=kLoop, calls=%fused_computation.16 | loop fusion | flops 57344 | bytes 98304 | tf_op jit(solution)/shard_map/convert_element_type | solution.py:558
  (19 shorter events, 0.6 us)
Async XLA Ops:
  2.1 1.5 %collective-permute-start = (bf16[2,16,1664]{2,1,0:T(8,128)(2,1)S(1)}, bf16[2,16,1664]{2,1,0:T(8,128)(2,1)S(1)}, u32[]{:S(2)}, u32[]{:S(2)}) collective-permute-start(bf16[2,16,1664]{2,1,0:T(8,128)(2,1)S(1)} %get-tuple-element.19), channel_id=1, source_target_pairs={{0,1},{1,0},{2,3},{3,2},{4,5},{5,4},{6,7},{7,6},{8,9},{9,8},{10,11... | collective-permute-start | bytes 319496 | tf_op jit(solution)/shard_map/ppermute | solution.py:133
  3.6 7.0 %collective-permute-start.1 = (bf16[16,1664]{1,0:T(8,128)(2,1)S(1)}, bf16[16,1664]{1,0:T(8,128)(2,1)S(1)}, u32[]{:S(2)}, u32[]{:S(2)}) collective-permute-start(bf16[16,1664]{1,0:T(8,128)(2,1)S(1)} %get-tuple-element.40), channel_id=1, source_target_pairs={{0,2},{1,3},{2,0},{3,1},{4,6},{5,7},{6,4},{7,5},{8,10},{9,11},{10,... | collective-permute-start | bytes 159752 | tf_op jit(solution)/shard_map/ppermute | solution.py:133
  6.6 5.5 %collective-permute-start.2 = (bf16[16,1664]{1,0:T(8,128)(2,1)S(1)}, bf16[16,1664]{1,0:T(8,128)(2,1)S(1)}, u32[]{:S(2)}, u32[]{:S(2)}) collective-permute-start(bf16[16,1664]{1,0:T(8,128)(2,1)S(1)} %get-tuple-element.41), channel_id=1, source_target_pairs={{0,18},{1,19},{2,16},{3,17},{4,22},{5,23},{6,20},{7,21},{8,26},{9,... | collective-permute-start | bytes 159752 | tf_op jit(solution)/shard_map/ppermute | solution.py:133
  8.0 4.1 %collective-permute-start.3 = (bf16[16,1664]{1,0:T(8,128)(2,1)S(1)}, bf16[16,1664]{1,0:T(8,128)(2,1)S(1)}, u32[]{:S(2)}, u32[]{:S(2)}) collective-permute-start(bf16[16,1664]{1,0:T(8,128)(2,1)S(1)} %get-tuple-element.41), channel_id=1, source_target_pairs={{0,16},{1,17},{2,18},{3,19},{4,20},{5,21},{6,22},{7,23},{8,24},{9,... | collective-permute-start | bytes 159752 | tf_op jit(solution)/shard_map/ppermute | solution.py:133
  12.2 10.6 %collective-permute-start.4 = (bf16[32,1664]{1,0:T(8,128)(2,1)S(1)}, bf16[32,1664]{1,0:T(8,128)(2,1)S(1)}, u32[]{:S(2)}, u32[]{:S(2)}) collective-permute-start(bf16[32,1664]{1,0:T(8,128)(2,1)S(1)} %pad_maximum_fusion.own_ref), channel_id=1, source_target_pairs={{0,12},{1,13},{2,14},{3,15},{4,8},{5,9},{6,10},{7,11},{8,4},{9,5},... | collective-permute-start | bytes 319496 | tf_op jit(solution)/shard_map/ppermute | solution.py:133
  15.8 8.3 %collective-permute-start.5 = (bf16[32,1664]{1,0:T(8,128)(2,1)S(1)}, bf16[32,1664]{1,0:T(8,128)(2,1)S(1)}, u32[]{:S(2)}, u32[]{:S(2)}) collective-permute-start(bf16[32,1664]{1,0:T(8,128)(2,1)S(1)} %pad_maximum_fusion.own_ref), channel_id=1, source_target_pairs={{0,8},{1,9},{2,10},{3,11},{4,12},{5,13},{6,14},{7,15},{8,0},{9,1},... | collective-permute-start | bytes 319496 | tf_op jit(solution)/shard_map/ppermute | solution.py:133
  15.8 8.3 %collective-permute-start.6 = (bf16[32,1664]{1,0:T(8,128)(2,1)S(1)}, bf16[32,1664]{1,0:T(8,128)(2,1)S(1)}, u32[]{:S(2)}, u32[]{:S(2)}) collective-permute-start(bf16[32,1664]{1,0:T(8,128)(2,1)S(1)} %pad_maximum_fusion.own_ref), channel_id=1, source_target_pairs={{0,4},{1,5},{2,6},{3,7},{4,0},{5,1},{6,2},{7,3},{8,12},{9,13},{10,... | collective-permute-start | bytes 319496 | tf_op jit(solution)/shard_map/ppermute | solution.py:133
  30.8 1.6 %collective-permute-start.7 = (bf16[16,8192]{1,0:T(8,128)(2,1)S(1)}, bf16[16,8192]{1,0:T(8,128)(2,1)S(1)}, u32[]{:S(2)}, u32[]{:S(2)}) collective-permute-start(bf16[16,8192]{1,0:T(8,128)(2,1)S(1)} %get-tuple-element.32), channel_id=1, source_target_pairs={{0,1},{1,0},{2,3},{3,2},{4,5},{5,4},{6,7},{7,6},{8,9},{9,8},{10,11... | collective-permute-start | bytes 786440 | tf_op jit(solution)/shard_map/ppermute | solution.py:133
  32.5 5.3 %collective-permute-start.10 = (bf16[4,8192]{1,0:T(4,128)(2,1)S(1)}, bf16[4,8192]{1,0:T(4,128)(2,1)S(1)}, u32[]{:S(2)}, u32[]{:S(2)}) collective-permute-start(bf16[4,8192]{1,0:T(4,128)(2,1)S(1)} %get-tuple-element.38), channel_id=1, source_target_pairs={{0,18},{1,19},{2,16},{3,17},{4,22},{5,23},{6,20},{7,21},{8,26},{9,... | collective-permute-start | bytes 196616 | tf_op jit(solution)/shard_map/ppermute | solution.py:133
  34.1 4.9 %collective-permute-start.8 = (bf16[4,8192]{1,0:T(4,128)(2,1)S(1)}, bf16[4,8192]{1,0:T(4,128)(2,1)S(1)}, u32[]{:S(2)}, u32[]{:S(2)}) collective-permute-start(bf16[4,8192]{1,0:T(4,128)(2,1)S(1)} %get-tuple-element.37), channel_id=1, source_target_pairs={{0,2},{1,3},{2,0},{3,1},{4,6},{5,7},{6,4},{7,5},{8,10},{9,11},{10,... | collective-permute-start | bytes 196616 | tf_op jit(solution)/shard_map/ppermute | solution.py:133
  34.6 4.4 %collective-permute-start.9 = (bf16[4,8192]{1,0:T(4,128)(2,1)S(1)}, bf16[4,8192]{1,0:T(4,128)(2,1)S(1)}, u32[]{:S(2)}, u32[]{:S(2)}) collective-permute-start(bf16[4,8192]{1,0:T(4,128)(2,1)S(1)} %get-tuple-element.39), channel_id=1, source_target_pairs={{0,16},{1,17},{2,18},{3,19},{4,20},{5,21},{6,22},{7,23},{8,24},{9,... | collective-permute-start | bytes 196616 | tf_op jit(solution)/shard_map/ppermute | solution.py:133
  39.2 5.8 %collective-permute-start.11 = (bf16[1,8192]{1,0:T(2,128)(2,1)S(1)}, bf16[1,8192]{1,0:T(2,128)(2,1)S(1)}, u32[]{:S(2)}, u32[]{:S(2)}) collective-permute-start(bf16[1,8192]{1,0:T(2,128)(2,1)S(1)} %get-tuple-element.42), channel_id=1, source_target_pairs={{0,12},{1,13},{2,14},{3,15},{4,8},{5,9},{6,10},{7,11},{8,4},{9,5},... | collective-permute-start | bytes 49160 | tf_op jit(solution)/shard_map/ppermute | solution.py:133
  41.8 4.8 %collective-permute-start.12 = (bf16[1,8192]{1,0:T(2,128)(2,1)S(1)}, bf16[1,8192]{1,0:T(2,128)(2,1)S(1)}, u32[]{:S(2)}, u32[]{:S(2)}) collective-permute-start(bf16[1,8192]{1,0:T(2,128)(2,1)S(1)} %get-tuple-element.44), channel_id=1, source_target_pairs={{0,8},{1,9},{2,10},{3,11},{4,12},{5,13},{6,14},{7,15},{8,0},{9,1},... | collective-permute-start | bytes 49160 | tf_op jit(solution)/shard_map/ppermute | solution.py:133
  41.8 4.8 %collective-permute-start.13 = (bf16[1,8192]{1,0:T(2,128)(2,1)S(1)}, bf16[1,8192]{1,0:T(2,128)(2,1)S(1)}, u32[]{:S(2)}, u32[]{:S(2)}) collective-permute-start(bf16[1,8192]{1,0:T(2,128)(2,1)S(1)} %get-tuple-element.43), channel_id=1, source_target_pairs={{0,4},{1,5},{2,6},{3,7},{4,0},{5,1},{6,2},{7,3},{8,12},{9,13},{10,... | collective-permute-start | bytes 49160 | tf_op jit(solution)/shard_map/ppermute | solution.py:133

commit v5 on v4

--- a/solution.py
+++ b/solution.py
@@ -17,7 +17,7 @@
 AXES = ("groups", "tensor")
 MIB = 2**20
 TILE = 512
-CHUNK = 256
+CHUNK = 128
 FETCHES = (1, 2, 7, 3)
 LANES = 128
 
@@ -131,6 +131,10 @@
         for t in range(tensor_size)
     ]
     return lax.ppermute(value, AXES, pairs)
+
+
+def start_order(count):
+    return [count // 2] + [d for d in range(count - 1, 0, -1) if d != count // 2]
 
 
 def in_hbm(array):
@@ -416,9 +420,9 @@
     count = len(others) + 1
     far = 4 * (count - 1)
     total = own_ref[...].astype(jnp.float32) * parity_sign(place, far)
-    for index, other in enumerate(others):
+    for distance, other in zip(range(count - 1, 0, -1), others):
         total = total + other[...].astype(jnp.float32) * parity_sign(
-            place & (place ^ (4 * (count - 1 - index))), far
+            place & (place ^ (4 * distance)), far
         )
     rotated = (total * (1.0 / math.sqrt(HAD_CROSS))).astype(jnp.bfloat16)
     each = rows // (8 * count)
@@ -553,7 +557,7 @@
     )
     send = keep.astype(jnp.bfloat16)
     total = keep[:each]
-    for d in range(count - 1, 0, -1):
+    for d in start_order(count):
         total = total + exchanged(send[d * each : (d + 1) * each], 0, 4 * d).astype(jnp.float32)
     return total.astype(jnp.bfloat16)
 

time: 47.4 us -> 46.3 us (0.977)
  starting transfers between devices: 17.6 us -> 16.7 us
  Pallas kernels: 17.2 us -> 16.5 us
  waiting for transfers between devices: 11.2 us -> 11.7 us
    ppermute x14, starting transfers between devices: 17.6 us -> 16.7 us  [exchanged(): return lax.ppermute(value, AXES, pairs)]
    pallas_call x1, Pallas kernels: 6.57 us -> 5.85 us  [product(): pl.pallas_call(functools.partial(product_kernel, len(ready)), in_specs=[p...]
    ppermute x14, waiting for transfers between devices: 11.2 us -> 11.7 us  [exchanged(): return lax.ppermute(value, AXES, pairs)]
  transfers between devices with their start and end apart: 14 -> 14, of which waited for: 9 -> 10; matrix products, arithmetic and copies ran while one was open for 0% -> 0% of each run, Pallas kernels for 18% -> 19%
where the time goes in v5:
time: 46.3 us; the launch traced here: 46.2 us
  starting transfers between devices  16.7 us (36%)
  Pallas kernels  16.5 us (36%)
  waiting for transfers between devices  11.7 us (25%)
  other arithmetic  0.99 us (2%)
    ppermute x14, starting transfers between devices, exchanged(): return lax.ppermute(value, AXES, pairs)  16.7 us
    ppermute x14, waiting for transfers between devices, exchanged(): return lax.ppermute(value, AXES, pairs)  11.7 us
    pallas_call x1, Pallas kernels, unpack(): pl.pallas_call(functools.partial(unpack_kernel, first), in_specs=[pl.Bloc...  6.05 us
    pallas_call x1, Pallas kernels, product(): pl.pallas_call(functools.partial(product_kernel, len(ready)), in_specs=[p...  5.85 us
    pallas_call x1, Pallas kernels, first_unpack(): pl.pallas_call(first_kernel, in_specs=[pl.BlockSpec(memory_space=pltpu.SM...  2.52 us
    pallas_call x1, Pallas kernels, local_rotation(): pl.pallas_call(local_kernel, in_specs=[pl.BlockSpec(memory_space=pltpu.SM...  2.08 us
  transfers between devices with their start and end apart: 14, of which 10 were waited for; matrix products, arithmetic and copies ran while one was open for 0% of the time, Pallas kernels for 19%

profile of v5, /device:TPU:0, one launch (start us, length us, event | category | flops | bytes accessed | tf_op | source)
XLA Modules:
  0.0 46.2 jit_solution(17175717146700920966)
XLA Ops:
  0.0 2.1 %local_rotation.1 = (bf16[2,16,1664]{2,1,0:T(8,128)(2,1)S(1)}, bf16[104,8192]{1,0:T(8,128)(2,1)S(1)}) custom-call(s32[1]{0:T(128)} %bitcast.group_ref, bf16[16,3328]{1,0:T(8,128)(2,1)} %bitcast.10, bf16[16,3328]{1,0:T(8,128)(2,1)} %bitcast.11, bf16[1664,128]{1,0:T(8,128)(2,1)} %constant.44.clone.table_hbm, bf16[104,8192]{1,0:T(8,128)(2,1)} %scales_hbm.1), custom_call_target="tpu_custom_call" | custom-call | flops 100000000 | bytes 8388608 | tf_op jit(solution)/shard_map/local_rotation/pallas_call | solution.py:247
  2.1 0.5 %collective-permute-start = (bf16[2,16,1664]{2,1,0:T(8,128)(2,1)S(1)}, bf16[2,16,1664]{2,1,0:T(8,128)(2,1)S(1)}, u32[]{:S(2)}, u32[]{:S(2)}) collective-permute-start(bf16[2,16,1664]{2,1,0:T(8,128)(2,1)S(1)} %get-tuple-element.19), channel_id=1, source_target_pairs={{0,1},{1,0},{2,3},{3,2},{4,5},{5,4},{6,7},{7,6},{8,9},{9,8},{10,11... | collective-permute-start | bytes 319496 | tf_op jit(solution)/shard_map/ppermute | solution.py:133
  2.6 1.0 %collective-permute-done = bf16[2,16,1664]{2,1,0:T(8,128)(2,1)S(1)} collective-permute-done((bf16[2,16,1664]{2,1,0:T(8,128)(2,1)S(1)}, bf16[2,16,1664]{2,1,0:T(8,128)(2,1)S(1)}, u32[]{:S(2)}, u32[]{:S(2)}) %collective-permute-start) | collective-permute-done | bytes 106528 | tf_op jit(solution)/shard_map/ppermute | solution.py:133
  3.6 2.9 %collective-permute-start.1 = (bf16[16,1664]{1,0:T(8,128)(2,1)S(1)}, bf16[16,1664]{1,0:T(8,128)(2,1)S(1)}, u32[]{:S(2)}, u32[]{:S(2)}) collective-permute-start(bf16[16,1664]{1,0:T(8,128)(2,1)S(1)} %get-tuple-element.40), channel_id=1, source_target_pairs={{0,2},{1,3},{2,0},{3,1},{4,6},{5,7},{6,4},{7,5},{8,10},{9,11},{10,... | collective-permute-start | bytes 159752 | tf_op jit(solution)/shard_map/ppermute | solution.py:133
  6.6 1.4 %collective-permute-start.2 = (bf16[16,1664]{1,0:T(8,128)(2,1)S(1)}, bf16[16,1664]{1,0:T(8,128)(2,1)S(1)}, u32[]{:S(2)}, u32[]{:S(2)}) collective-permute-start(bf16[16,1664]{1,0:T(8,128)(2,1)S(1)} %get-tuple-element.41), channel_id=1, source_target_pairs={{0,18},{1,19},{2,16},{3,17},{4,22},{5,23},{6,20},{7,21},{8,26},{9,... | collective-permute-start | bytes 159752 | tf_op jit(solution)/shard_map/ppermute | solution.py:133
  8.1 2.5 %first_unpack.1 = (bf16[1664,512]{1,0:T(8,128)(2,1)S(1)}, s32[2,832,512]{2,1,0:T(8,128)S(1)}, f32[52,8192]{1,0:T(8,128)S(1)}) custom-call(s32[1]{0:T(128)} %bitcast.group_ref, s32[1664,8192]{1,0:T(8,128)} %codes_hbm.5, bf16[104,8192]{1,0:T(8,128)(2,1)S(1)} %get-tuple-element.22.scales_in), custom_call_target="tpu_custom_call" | custom-call | bytes 5111808 | tf_op jit(solution)/shard_map/first_unpack/pallas_call | solution.py:326
  10.7 1.3 %collective-permute-done.2 = bf16[16,1664]{1,0:T(8,128)(2,1)S(1)} collective-permute-done((bf16[16,1664]{1,0:T(8,128)(2,1)S(1)}, bf16[16,1664]{1,0:T(8,128)(2,1)S(1)}, u32[]{:S(2)}, u32[]{:S(2)}) %collective-permute-start.2) | collective-permute-done | bytes 53280 | tf_op jit(solution)/shard_map/ppermute | solution.py:133
  12.2 3.7 %collective-permute-start.4 = (bf16[32,1664]{1,0:T(8,128)(2,1)S(1)}, bf16[32,1664]{1,0:T(8,128)(2,1)S(1)}, u32[]{:S(2)}, u32[]{:S(2)}) collective-permute-start(bf16[32,1664]{1,0:T(8,128)(2,1)S(1)} %pad_maximum_fusion.own_ref), channel_id=1, source_target_pairs={{0,12},{1,13},{2,14},{3,15},{4,8},{5,9},{6,10},{7,11},{8,4},{9,5},... | collective-permute-start | bytes 319496 | tf_op jit(solution)/shard_map/ppermute | solution.py:133
  15.8 0.8 %collective-permute-start.6 = (bf16[32,1664]{1,0:T(8,128)(2,1)S(1)}, bf16[32,1664]{1,0:T(8,128)(2,1)S(1)}, u32[]{:S(2)}, u32[]{:S(2)}) collective-permute-start(bf16[32,1664]{1,0:T(8,128)(2,1)S(1)} %pad_maximum_fusion.own_ref), channel_id=1, source_target_pairs={{0,4},{1,5},{2,6},{3,7},{4,0},{5,1},{6,2},{7,3},{8,12},{9,13},{10,... | collective-permute-start | bytes 319496 | tf_op jit(solution)/shard_map/ppermute | solution.py:133
  16.7 6.0 %unpack.1 = (bf16[1664,4608]{1,0:T(8,128)(2,1)S(1)}, s32[3,832,512]{2,1,0:T(8,128)S(1)}) custom-call(s32[1]{0:T(128)} %bitcast.group_ref, s32[1664,8192]{1,0:T(8,128)} %codes_hbm.5, f32[52,8192]{1,0:T(8,128)S(1)} %get-tuple-element.25.scales_ref, s32[2,832,512]{2,1,0:T(8,128)S(1)} %get-tuple-element.26.given), custom_call_target="tpu_custom_call" | custom-call | flops 61341696 | bytes 30670848 | tf_op jit(solution)/shard_map/unpack/pallas_call | solution.py:379
  22.8 1.4 %collective-permute-done.5.refs_3_ = bf16[32,1664]{1,0:T(8,128)(2,1)S(1)} collective-permute-done((bf16[32,1664]{1,0:T(8,128)(2,1)S(1)}, bf16[32,1664]{1,0:T(8,128)(2,1)S(1)}, u32[]{:S(2)}, u32[]{:S(2)}) %collective-permute-start.5) | collective-permute-done | bytes 106528 | tf_op jit(solution)/shard_map/ppermute | solution.py:133
  24.2 5.8 %product.1 = (f32[16,8192]{1,0:T(8,128)S(1)}, bf16[16,8192]{1,0:T(8,128)(2,1)S(1)}) custom-call(s32[2]{0:T(128)S(1)} %pad_add_fusion.place_ref, s32[1664,8192]{1,0:T(8,128)} %codes_hbm.5, s32[3,832,512]{2,1,0:T(8,128)S(1)} %get-tuple-element.27.given, f32[52,8192]{1,0:T(8,128)S(1)} %get-tuple-element.25.scales_ref, ...), custom_call_target="tpu_custom_call" | custom-call | tf_op jit(solution)/shard_map/product/pallas_call | solution.py:486
  30.1 1.5 %collective-permute-done.7 = bf16[16,8192]{1,0:T(8,128)(2,1)S(1)} collective-permute-done((bf16[16,8192]{1,0:T(8,128)(2,1)S(1)}, bf16[16,8192]{1,0:T(8,128)(2,1)S(1)}, u32[]{:S(2)}, u32[]{:S(2)}) %collective-permute-start.7) | collective-permute-done | bytes 262176 | tf_op jit(solution)/shard_map/ppermute | solution.py:133
  31.8 1.6 %collective-permute-start.10 = (bf16[4,8192]{1,0:T(4,128)(2,1)S(1)}, bf16[4,8192]{1,0:T(4,128)(2,1)S(1)}, u32[]{:S(2)}, u32[]{:S(2)}) collective-permute-start(bf16[4,8192]{1,0:T(4,128)(2,1)S(1)} %get-tuple-element.38), channel_id=1, source_target_pairs={{0,18},{1,19},{2,16},{3,17},{4,22},{5,23},{6,20},{7,21},{8,26},{9,... | collective-permute-start | bytes 196616 | tf_op jit(solution)/shard_map/ppermute | solution.py:133
  33.4 0.5 %collective-permute-start.8 = (bf16[4,8192]{1,0:T(4,128)(2,1)S(1)}, bf16[4,8192]{1,0:T(4,128)(2,1)S(1)}, u32[]{:S(2)}, u32[]{:S(2)}) collective-permute-start(bf16[4,8192]{1,0:T(4,128)(2,1)S(1)} %get-tuple-element.37), channel_id=1, source_target_pairs={{0,2},{1,3},{2,0},{3,1},{4,6},{5,7},{6,4},{7,5},{8,10},{9,11},{10,... | collective-permute-start | bytes 196616 | tf_op jit(solution)/shard_map/ppermute | solution.py:133
  33.9 1.4 %collective-permute-start.9 = (bf16[4,8192]{1,0:T(4,128)(2,1)S(1)}, bf16[4,8192]{1,0:T(4,128)(2,1)S(1)}, u32[]{:S(2)}, u32[]{:S(2)}) collective-permute-start(bf16[4,8192]{1,0:T(4,128)(2,1)S(1)} %get-tuple-element.39), channel_id=1, source_target_pairs={{0,16},{1,17},{2,18},{3,19},{4,20},{5,21},{6,22},{7,23},{8,24},{9,... | collective-permute-start | bytes 196616 | tf_op jit(solution)/shard_map/ppermute | solution.py:133
  35.3 1.7 %collective-permute-done.10 = bf16[4,8192]{1,0:T(4,128)(2,1)S(1)} collective-permute-done((bf16[4,8192]{1,0:T(4,128)(2,1)S(1)}, bf16[4,8192]{1,0:T(4,128)(2,1)S(1)}, u32[]{:S(2)}, u32[]{:S(2)}) %collective-permute-start.10) | collective-permute-done | bytes 65568 | tf_op jit(solution)/shard_map/ppermute | solution.py:133
  37.1 1.2 %collective-permute-done.8 = bf16[4,8192]{1,0:T(4,128)(2,1)S(1)} collective-permute-done((bf16[4,8192]{1,0:T(4,128)(2,1)S(1)}, bf16[4,8192]{1,0:T(4,128)(2,1)S(1)}, u32[]{:S(2)}, u32[]{:S(2)}) %collective-permute-start.8) | collective-permute-done | bytes 65568 | tf_op jit(solution)/shard_map/ppermute | solution.py:133
  38.5 1.1 %collective-permute-start.11 = (bf16[1,8192]{1,0:T(2,128)(2,1)S(1)}, bf16[1,8192]{1,0:T(2,128)(2,1)S(1)}, u32[]{:S(2)}, u32[]{:S(2)}) collective-permute-start(bf16[1,8192]{1,0:T(2,128)(2,1)S(1)} %get-tuple-element.42), channel_id=1, source_target_pairs={{0,8},{1,9},{2,10},{3,11},{4,12},{5,13},{6,14},{7,15},{8,0},{9,1},... | collective-permute-start | bytes 49160 | tf_op jit(solution)/shard_map/ppermute | solution.py:133
  39.6 1.7 %collective-permute-start.12 = (bf16[1,8192]{1,0:T(2,128)(2,1)S(1)}, bf16[1,8192]{1,0:T(2,128)(2,1)S(1)}, u32[]{:S(2)}, u32[]{:S(2)}) collective-permute-start(bf16[1,8192]{1,0:T(2,128)(2,1)S(1)} %get-tuple-element.44), channel_id=1, source_target_pairs={{0,12},{1,13},{2,14},{3,15},{4,8},{5,9},{6,10},{7,11},{8,4},{9,5},... | collective-permute-start | bytes 49160 | tf_op jit(solution)/shard_map/ppermute | solution.py:133
  41.2 0.8 %collective-permute-start.13 = (bf16[1,8192]{1,0:T(2,128)(2,1)S(1)}, bf16[1,8192]{1,0:T(2,128)(2,1)S(1)}, u32[]{:S(2)}, u32[]{:S(2)}) collective-permute-start(bf16[1,8192]{1,0:T(2,128)(2,1)S(1)} %get-tuple-element.43), channel_id=1, source_target_pairs={{0,4},{1,5},{2,6},{3,7},{4,0},{5,1},{6,2},{7,3},{8,12},{9,13},{10,... | collective-permute-start | bytes 49160 | tf_op jit(solution)/shard_map/ppermute | solution.py:133
  42.0 2.0 %collective-permute-done.11 = bf16[1,8192]{1,0:T(2,128)(2,1)S(1)} collective-permute-done((bf16[1,8192]{1,0:T(2,128)(2,1)S(1)}, bf16[1,8192]{1,0:T(2,128)(2,1)S(1)}, u32[]{:S(2)}, u32[]{:S(2)}) %collective-permute-start.11) | collective-permute-done | bytes 16416 | tf_op jit(solution)/shard_map/ppermute | solution.py:133
  44.0 1.3 %collective-permute-done.12 = bf16[1,8192]{1,0:T(2,128)(2,1)S(1)} collective-permute-done((bf16[1,8192]{1,0:T(2,128)(2,1)S(1)}, bf16[1,8192]{1,0:T(2,128)(2,1)S(1)}, u32[]{:S(2)}, u32[]{:S(2)}) %collective-permute-start.12) | collective-permute-done | bytes 16416 | tf_op jit(solution)/shard_map/ppermute | solution.py:133
  45.5 0.7 %fusion.6 = bf16[1,8192]{1,0:T(2,128)(2,1)} fusion(bf16[1,8192]{1,0:T(2,128)(2,1)S(1)} %collective-permute-done.13, bf16[1,8192]{1,0:T(2,128)(2,1)S(1)} %collective-permute-done.12, bf16[1,8192]{1,0:T(2,128)(2,1)S(1)} %collective-permute-done.11, f32[4,8192]{1,0:T(4,128)S(1)} %get-tuple-element.34), kind=kLoop, calls=%fused_computation.16 | loop fusion | flops 57344 | bytes 98304 | tf_op jit(solution)/shard_map/convert_element_type | solution.py:562
  (19 shorter events, 0.9 us)
Async XLA Ops:
  2.1 1.5 %collective-permute-start = (bf16[2,16,1664]{2,1,0:T(8,128)(2,1)S(1)}, bf16[2,16,1664]{2,1,0:T(8,128)(2,1)S(1)}, u32[]{:S(2)}, u32[]{:S(2)}) collective-permute-start(bf16[2,16,1664]{2,1,0:T(8,128)(2,1)S(1)} %get-tuple-element.19), channel_id=1, source_target_pairs={{0,1},{1,0},{2,3},{3,2},{4,5},{5,4},{6,7},{7,6},{8,9},{9,8},{10,11... | collective-permute-start | bytes 319496 | tf_op jit(solution)/shard_map/ppermute | solution.py:133
  3.6 7.0 %collective-permute-start.1 = (bf16[16,1664]{1,0:T(8,128)(2,1)S(1)}, bf16[16,1664]{1,0:T(8,128)(2,1)S(1)}, u32[]{:S(2)}, u32[]{:S(2)}) collective-permute-start(bf16[16,1664]{1,0:T(8,128)(2,1)S(1)} %get-tuple-element.40), channel_id=1, source_target_pairs={{0,2},{1,3},{2,0},{3,1},{4,6},{5,7},{6,4},{7,5},{8,10},{9,11},{10,... | collective-permute-start | bytes 159752 | tf_op jit(solution)/shard_map/ppermute | solution.py:133
  6.6 5.5 %collective-permute-start.2 = (bf16[16,1664]{1,0:T(8,128)(2,1)S(1)}, bf16[16,1664]{1,0:T(8,128)(2,1)S(1)}, u32[]{:S(2)}, u32[]{:S(2)}) collective-permute-start(bf16[16,1664]{1,0:T(8,128)(2,1)S(1)} %get-tuple-element.41), channel_id=1, source_target_pairs={{0,18},{1,19},{2,16},{3,17},{4,22},{5,23},{6,20},{7,21},{8,26},{9,... | collective-permute-start | bytes 159752 | tf_op jit(solution)/shard_map/ppermute | solution.py:133
  8.0 4.1 %collective-permute-start.3 = (bf16[16,1664]{1,0:T(8,128)(2,1)S(1)}, bf16[16,1664]{1,0:T(8,128)(2,1)S(1)}, u32[]{:S(2)}, u32[]{:S(2)}) collective-permute-start(bf16[16,1664]{1,0:T(8,128)(2,1)S(1)} %get-tuple-element.41), channel_id=1, source_target_pairs={{0,16},{1,17},{2,18},{3,19},{4,20},{5,21},{6,22},{7,23},{8,24},{9,... | collective-permute-start | bytes 159752 | tf_op jit(solution)/shard_map/ppermute | solution.py:133
  12.2 10.6 %collective-permute-start.4 = (bf16[32,1664]{1,0:T(8,128)(2,1)S(1)}, bf16[32,1664]{1,0:T(8,128)(2,1)S(1)}, u32[]{:S(2)}, u32[]{:S(2)}) collective-permute-start(bf16[32,1664]{1,0:T(8,128)(2,1)S(1)} %pad_maximum_fusion.own_ref), channel_id=1, source_target_pairs={{0,12},{1,13},{2,14},{3,15},{4,8},{5,9},{6,10},{7,11},{8,4},{9,5},... | collective-permute-start | bytes 319496 | tf_op jit(solution)/shard_map/ppermute | solution.py:133
  15.8 8.3 %collective-permute-start.5 = (bf16[32,1664]{1,0:T(8,128)(2,1)S(1)}, bf16[32,1664]{1,0:T(8,128)(2,1)S(1)}, u32[]{:S(2)}, u32[]{:S(2)}) collective-permute-start(bf16[32,1664]{1,0:T(8,128)(2,1)S(1)} %pad_maximum_fusion.own_ref), channel_id=1, source_target_pairs={{0,8},{1,9},{2,10},{3,11},{4,12},{5,13},{6,14},{7,15},{8,0},{9,1},... | collective-permute-start | bytes 319496 | tf_op jit(solution)/shard_map/ppermute | solution.py:133
  15.8 8.3 %collective-permute-start.6 = (bf16[32,1664]{1,0:T(8,128)(2,1)S(1)}, bf16[32,1664]{1,0:T(8,128)(2,1)S(1)}, u32[]{:S(2)}, u32[]{:S(2)}) collective-permute-start(bf16[32,1664]{1,0:T(8,128)(2,1)S(1)} %pad_maximum_fusion.own_ref), channel_id=1, source_target_pairs={{0,4},{1,5},{2,6},{3,7},{4,0},{5,1},{6,2},{7,3},{8,12},{9,13},{10,... | collective-permute-start | bytes 319496 | tf_op jit(solution)/shard_map/ppermute | solution.py:133
  30.0 1.6 %collective-permute-start.7 = (bf16[16,8192]{1,0:T(8,128)(2,1)S(1)}, bf16[16,8192]{1,0:T(8,128)(2,1)S(1)}, u32[]{:S(2)}, u32[]{:S(2)}) collective-permute-start(bf16[16,8192]{1,0:T(8,128)(2,1)S(1)} %get-tuple-element.32), channel_id=1, source_target_pairs={{0,1},{1,0},{2,3},{3,2},{4,5},{5,4},{6,7},{7,6},{8,9},{9,8},{10,11... | collective-permute-start | bytes 786440 | tf_op jit(solution)/shard_map/ppermute | solution.py:133
  31.8 5.3 %collective-permute-start.10 = (bf16[4,8192]{1,0:T(4,128)(2,1)S(1)}, bf16[4,8192]{1,0:T(4,128)(2,1)S(1)}, u32[]{:S(2)}, u32[]{:S(2)}) collective-permute-start(bf16[4,8192]{1,0:T(4,128)(2,1)S(1)} %get-tuple-element.38), channel_id=1, source_target_pairs={{0,18},{1,19},{2,16},{3,17},{4,22},{5,23},{6,20},{7,21},{8,26},{9,... | collective-permute-start | bytes 196616 | tf_op jit(solution)/shard_map/ppermute | solution.py:133
  33.4 4.9 %collective-permute-start.8 = (bf16[4,8192]{1,0:T(4,128)(2,1)S(1)}, bf16[4,8192]{1,0:T(4,128)(2,1)S(1)}, u32[]{:S(2)}, u32[]{:S(2)}) collective-permute-start(bf16[4,8192]{1,0:T(4,128)(2,1)S(1)} %get-tuple-element.37), channel_id=1, source_target_pairs={{0,2},{1,3},{2,0},{3,1},{4,6},{5,7},{6,4},{7,5},{8,10},{9,11},{10,... | collective-permute-start | bytes 196616 | tf_op jit(solution)/shard_map/ppermute | solution.py:133
  33.9 4.4 %collective-permute-start.9 = (bf16[4,8192]{1,0:T(4,128)(2,1)S(1)}, bf16[4,8192]{1,0:T(4,128)(2,1)S(1)}, u32[]{:S(2)}, u32[]{:S(2)}) collective-permute-start(bf16[4,8192]{1,0:T(4,128)(2,1)S(1)} %get-tuple-element.39), channel_id=1, source_target_pairs={{0,16},{1,17},{2,18},{3,19},{4,20},{5,21},{6,22},{7,23},{8,24},{9,... | collective-permute-start | bytes 196616 | tf_op jit(solution)/shard_map/ppermute | solution.py:133
  38.5 5.6 %collective-permute-start.11 = (bf16[1,8192]{1,0:T(2,128)(2,1)S(1)}, bf16[1,8192]{1,0:T(2,128)(2,1)S(1)}, u32[]{:S(2)}, u32[]{:S(2)}) collective-permute-start(bf16[1,8192]{1,0:T(2,128)(2,1)S(1)} %get-tuple-element.42), channel_id=1, source_target_pairs={{0,8},{1,9},{2,10},{3,11},{4,12},{5,13},{6,14},{7,15},{8,0},{9,1},... | collective-permute-start | bytes 49160 | tf_op jit(solution)/shard_map/ppermute | solution.py:133
  39.6 5.8 %collective-permute-start.12 = (bf16[1,8192]{1,0:T(2,128)(2,1)S(1)}, bf16[1,8192]{1,0:T(2,128)(2,1)S(1)}, u32[]{:S(2)}, u32[]{:S(2)}) collective-permute-start(bf16[1,8192]{1,0:T(2,128)(2,1)S(1)} %get-tuple-element.44), channel_id=1, source_target_pairs={{0,12},{1,13},{2,14},{3,15},{4,8},{5,9},{6,10},{7,11},{8,4},{9,5},... | collective-permute-start | bytes 49160 | tf_op jit(solution)/shard_map/ppermute | solution.py:133
  41.2 4.3 %collective-permute-start.13 = (bf16[1,8192]{1,0:T(2,128)(2,1)S(1)}, bf16[1,8192]{1,0:T(2,128)(2,1)S(1)}, u32[]{:S(2)}, u32[]{:S(2)}) collective-permute-start(bf16[1,8192]{1,0:T(2,128)(2,1)S(1)} %get-tuple-element.43), channel_id=1, source_target_pairs={{0,4},{1,5},{2,6},{3,7},{4,0},{5,1},{6,2},{7,3},{8,12},{9,13},{10,... | collective-permute-start | bytes 49160 | tf_op jit(solution)/shard_map/ppermute | solution.py:133

commit v6 on v5

--- a/solution.py
+++ b/solution.py
@@ -18,7 +18,7 @@
 MIB = 2**20
 TILE = 512
 CHUNK = 128
-FETCHES = (1, 2, 7, 3)
+FETCHES = (1, 5, 4, 3)
 LANES = 128
 
 
@@ -135,6 +135,10 @@
 
 def start_order(count):
     return [count // 2] + [d for d in range(count - 1, 0, -1) if d != count // 2]
+
+
+def middle_order(count):
+    return [count - 1] + list(range(1, count - 1))
 
 
 def in_hbm(array):
@@ -418,11 +422,11 @@
         copy.start()
 
     count = len(others) + 1
-    far = 4 * (count - 1)
-    total = own_ref[...].astype(jnp.float32) * parity_sign(place, far)
-    for distance, other in zip(range(count - 1, 0, -1), others):
+    middle = 2 * (count - 1)
+    total = own_ref[...].astype(jnp.float32) * parity_sign(place, middle)
+    for distance, other in zip(middle_order(count), others):
         total = total + other[...].astype(jnp.float32) * parity_sign(
-            place & (place ^ (4 * distance)), far
+            place & (place ^ (2 * distance)), middle
         )
     rotated = (total * (1.0 / math.sqrt(HAD_CROSS))).astype(jnp.bfloat16)
     each = rows // (8 * count)
@@ -531,16 +535,17 @@
     ).astype(jnp.bfloat16)
     parts, group_then = lax.optimization_barrier((parts, group))
     mine, theirs = parts[0], parts[1]
-    across_y = exchanged(mine, 0, 2).astype(jnp.float32)
-    across_xy = exchanged(theirs, 1, 2).astype(jnp.float32)
-    across_x = exchanged(theirs, 1, 0).astype(jnp.float32)
+    top = tensor_size // 2
+    across = exchanged(mine, 0, top).astype(jnp.float32)
+    across_both = exchanged(theirs, 1, top).astype(jnp.float32)
+    across_groups = exchanged(theirs, 1, 0).astype(jnp.float32)
     early, words, scales = first_unpack(group_then, codes, scales, at_near, for_far)
-    sign = jnp.where(place[0] // 2 % 2 == 0, 1.0, -1.0)
+    sign = jnp.where(place[0] // top % 2 == 0, 1.0, -1.0)
     both = jnp.concatenate(
-        [mine.astype(jnp.float32) * sign + across_y, across_xy + across_x * sign]
+        [mine.astype(jnp.float32) * sign + across, across_both + across_groups * sign]
     ).astype(jnp.bfloat16)
     both, group_then, words = lax.optimization_barrier((both, group, words))
-    others = [exchanged(both, 0, 4 * d) for d in range(count - 1, 0, -1)]
+    others = [exchanged(both, 0, 2 * d) for d in middle_order(count)]
     late, words = unpack(group_then, codes, scales, words, at_near, at_far, for_product)
     keep, send = product(
         jnp.concatenate([group, place]), codes, words, scales, both, others, [early, late]

time: 46.3 us -> 46.1 us (level)
  waiting for transfers between devices: 11.7 us -> 11.1 us
    pallas_call x1, Pallas kernels: 2.52 us -> 4.05 us  [first_unpack(): pl.pallas_call(first_kernel, in_specs=[pl.BlockSpec(memory_space=pltpu.SM...]
    pallas_call x1, Pallas kernels: 6.05 us -> 4.55 us  [unpack(): pl.pallas_call(functools.partial(unpack_kernel, first), in_specs=[pl.Bloc...]
    ppermute x14, waiting for transfers between devices: 11.7 us -> 11.1 us  [exchanged(): return lax.ppermute(value, AXES, pairs)]
  transfers between devices with their start and end apart: 14 -> 14, of which waited for: 10 -> 8; matrix products, arithmetic and copies ran while one was open for 0% -> 0% of each run, Pallas kernels for 19% -> 19%
where the time goes in v6:
time: 46.1 us; the launch traced here: 45.9 us
  starting transfers between devices  17 us (37%)
  Pallas kernels  16.5 us (36%)
  waiting for transfers between devices  11.1 us (24%)
  other arithmetic  0.99 us (2%)
    ppermute x14, starting transfers between devices, exchanged(): return lax.ppermute(value, AXES, pairs)  17 us
    ppermute x14, waiting for transfers between devices, exchanged(): return lax.ppermute(value, AXES, pairs)  11.1 us
    pallas_call x1, Pallas kernels, product(): pl.pallas_call(functools.partial(product_kernel, len(ready)), in_specs=[p...  5.83 us
    pallas_call x1, Pallas kernels, unpack(): pl.pallas_call(functools.partial(unpack_kernel, first), in_specs=[pl.Bloc...  4.55 us
    pallas_call x1, Pallas kernels, first_unpack(): pl.pallas_call(first_kernel, in_specs=[pl.BlockSpec(memory_space=pltpu.SM...  4.05 us
    pallas_call x1, Pallas kernels, local_rotation(): pl.pallas_call(local_kernel, in_specs=[pl.BlockSpec(memory_space=pltpu.SM...  2.08 us
  transfers between devices with their start and end apart: 14, of which 8 were waited for; matrix products, arithmetic and copies ran while one was open for 0% of the time, Pallas kernels for 19%

profile of v6, /device:TPU:0, one launch (start us, length us, event | category | flops | bytes accessed | tf_op | source)
XLA Modules:
  0.0 45.9 jit_solution(6383769595972978799)
XLA Ops:
  0.0 2.1 %local_rotation.1 = (bf16[2,16,1664]{2,1,0:T(8,128)(2,1)S(1)}, bf16[104,8192]{1,0:T(8,128)(2,1)S(1)}) custom-call(s32[1]{0:T(128)} %bitcast.group_ref, bf16[16,3328]{1,0:T(8,128)(2,1)} %bitcast.10, bf16[16,3328]{1,0:T(8,128)(2,1)} %bitcast.11, bf16[1664,128]{1,0:T(8,128)(2,1)} %constant.47.clone.table_hbm, bf16[104,8192]{1,0:T(8,128)(2,1)} %scales_hbm.1), custom_call_target="tpu_custom_call" | custom-call | flops 100000000 | bytes 8388608 | tf_op jit(solution)/shard_map/local_rotation/pallas_call | solution.py:251
  2.1 0.5 %collective-permute-start = (bf16[2,16,1664]{2,1,0:T(8,128)(2,1)S(1)}, bf16[2,16,1664]{2,1,0:T(8,128)(2,1)S(1)}, u32[]{:S(2)}, u32[]{:S(2)}) collective-permute-start(bf16[2,16,1664]{2,1,0:T(8,128)(2,1)S(1)} %get-tuple-element.19), channel_id=1, source_target_pairs={{0,1},{1,0},{2,3},{3,2},{4,5},{5,4},{6,7},{7,6},{8,9},{9,8},{10,11... | collective-permute-start | bytes 319496 | tf_op jit(solution)/shard_map/ppermute | solution.py:133
  2.6 1.0 %collective-permute-done = bf16[2,16,1664]{2,1,0:T(8,128)(2,1)S(1)} collective-permute-done((bf16[2,16,1664]{2,1,0:T(8,128)(2,1)S(1)}, bf16[2,16,1664]{2,1,0:T(8,128)(2,1)S(1)}, u32[]{:S(2)}, u32[]{:S(2)}) %collective-permute-start) | collective-permute-done | bytes 106528 | tf_op jit(solution)/shard_map/ppermute | solution.py:133
  3.6 4.0 %collective-permute-start.1 = (bf16[16,1664]{1,0:T(8,128)(2,1)S(1)}, bf16[16,1664]{1,0:T(8,128)(2,1)S(1)}, u32[]{:S(2)}, u32[]{:S(2)}) collective-permute-start(bf16[16,1664]{1,0:T(8,128)(2,1)S(1)} %get-tuple-element.40), channel_id=1, source_target_pairs={{0,8},{1,9},{2,10},{3,11},{4,12},{5,13},{6,14},{7,15},{8,0},{9,1},... | collective-permute-start | bytes 159752 | tf_op jit(solution)/shard_map/ppermute | solution.py:133
  7.6 1.3 %collective-permute-start.2 = (bf16[16,1664]{1,0:T(8,128)(2,1)S(1)}, bf16[16,1664]{1,0:T(8,128)(2,1)S(1)}, u32[]{:S(2)}, u32[]{:S(2)}) collective-permute-start(bf16[16,1664]{1,0:T(8,128)(2,1)S(1)} %get-tuple-element.41), channel_id=1, source_target_pairs={{0,24},{1,25},{2,26},{3,27},{4,28},{5,29},{6,30},{7,31},{8,16},{9,... | collective-permute-start | bytes 159752 | tf_op jit(solution)/shard_map/ppermute | solution.py:133
  9.2 4.0 %first_unpack.1 = (bf16[1664,512]{1,0:T(8,128)(2,1)S(1)}, s32[5,832,512]{2,1,0:T(8,128)S(1)}, f32[52,8192]{1,0:T(8,128)S(1)}) custom-call(s32[1]{0:T(128)} %bitcast.group_ref, s32[1664,8192]{1,0:T(8,128)} %codes_hbm.5, bf16[104,8192]{1,0:T(8,128)(2,1)S(1)} %get-tuple-element.22.scales_in), custom_call_target="tpu_custom_call" | custom-call | bytes 10223616 | tf_op jit(solution)/shard_map/first_unpack/pallas_call | solution.py:330
  13.3 0.8 %collective-permute-done.2 = bf16[16,1664]{1,0:T(8,128)(2,1)S(1)} collective-permute-done((bf16[16,1664]{1,0:T(8,128)(2,1)S(1)}, bf16[16,1664]{1,0:T(8,128)(2,1)S(1)}, u32[]{:S(2)}, u32[]{:S(2)}) %collective-permute-start.2) | collective-permute-done | bytes 53280 | tf_op jit(solution)/shard_map/ppermute | solution.py:133
  14.1 2.2 %collective-permute-start.4 = (bf16[32,1664]{1,0:T(8,128)(2,1)S(1)}, bf16[32,1664]{1,0:T(8,128)(2,1)S(1)}, u32[]{:S(2)}, u32[]{:S(2)}) collective-permute-start(bf16[32,1664]{1,0:T(8,128)(2,1)S(1)} %pad_maximum_fusion.own_ref), channel_id=1, source_target_pairs={{0,6},{1,7},{2,4},{3,5},{4,2},{5,3},{6,0},{7,1},{8,14},{9,15},{10,... | collective-permute-start | bytes 319496 | tf_op jit(solution)/shard_map/ppermute | solution.py:133
  16.3 0.5 %collective-permute-start.5 = (bf16[32,1664]{1,0:T(8,128)(2,1)S(1)}, bf16[32,1664]{1,0:T(8,128)(2,1)S(1)}, u32[]{:S(2)}, u32[]{:S(2)}) collective-permute-start(bf16[32,1664]{1,0:T(8,128)(2,1)S(1)} %pad_maximum_fusion.own_ref), channel_id=1, source_target_pairs={{0,2},{1,3},{2,0},{3,1},{4,6},{5,7},{6,4},{7,5},{8,10},{9,11},{10,... | collective-permute-start | bytes 319496 | tf_op jit(solution)/shard_map/ppermute | solution.py:133
  16.8 0.9 %collective-permute-start.6 = (bf16[32,1664]{1,0:T(8,128)(2,1)S(1)}, bf16[32,1664]{1,0:T(8,128)(2,1)S(1)}, u32[]{:S(2)}, u32[]{:S(2)}) collective-permute-start(bf16[32,1664]{1,0:T(8,128)(2,1)S(1)} %pad_maximum_fusion.own_ref), channel_id=1, source_target_pairs={{0,4},{1,5},{2,6},{3,7},{4,0},{5,1},{6,2},{7,3},{8,12},{9,13},{10,... | collective-permute-start | bytes 319496 | tf_op jit(solution)/shard_map/ppermute | solution.py:133
  17.7 4.5 %unpack.1 = (bf16[1664,4608]{1,0:T(8,128)(2,1)S(1)}, s32[3,832,512]{2,1,0:T(8,128)S(1)}) custom-call(s32[1]{0:T(128)} %bitcast.group_ref, s32[1664,8192]{1,0:T(8,128)} %codes_hbm.5, f32[52,8192]{1,0:T(8,128)S(1)} %get-tuple-element.25.scales_ref, s32[5,832,512]{2,1,0:T(8,128)S(1)} %get-tuple-element.26.given), custom_call_target="tpu_custom_call" | custom-call | flops 61341696 | bytes 30670848 | tf_op jit(solution)/shard_map/unpack/pallas_call | solution.py:383
  22.3 5.8 %product.1 = (f32[16,8192]{1,0:T(8,128)S(1)}, bf16[16,8192]{1,0:T(8,128)(2,1)S(1)}) custom-call(s32[2]{0:T(128)S(1)} %pad_add_fusion.place_ref, s32[1664,8192]{1,0:T(8,128)} %codes_hbm.5, s32[3,832,512]{2,1,0:T(8,128)S(1)} %get-tuple-element.27.given, f32[52,8192]{1,0:T(8,128)S(1)} %get-tuple-element.25.scales_ref, ...), custom_call_target="tpu_custom_call" | custom-call | tf_op jit(solution)/shard_map/product/pallas_call | solution.py:490
  28.2 1.5 %collective-permute-done.7 = bf16[16,8192]{1,0:T(8,128)(2,1)S(1)} collective-permute-done((bf16[16,8192]{1,0:T(8,128)(2,1)S(1)}, bf16[16,8192]{1,0:T(8,128)(2,1)S(1)}, u32[]{:S(2)}, u32[]{:S(2)}) %collective-permute-start.7) | collective-permute-done | bytes 262176 | tf_op jit(solution)/shard_map/ppermute | solution.py:133
  29.9 2.5 %collective-permute-start.10 = (bf16[4,8192]{1,0:T(4,128)(2,1)S(1)}, bf16[4,8192]{1,0:T(4,128)(2,1)S(1)}, u32[]{:S(2)}, u32[]{:S(2)}) collective-permute-start(bf16[4,8192]{1,0:T(4,128)(2,1)S(1)} %get-tuple-element.38), channel_id=1, source_target_pairs={{0,18},{1,19},{2,16},{3,17},{4,22},{5,23},{6,20},{7,21},{8,26},{9,... | collective-permute-start | bytes 196616 | tf_op jit(solution)/shard_map/ppermute | solution.py:133
  32.4 0.5 %collective-permute-start.8 = (bf16[4,8192]{1,0:T(4,128)(2,1)S(1)}, bf16[4,8192]{1,0:T(4,128)(2,1)S(1)}, u32[]{:S(2)}, u32[]{:S(2)}) collective-permute-start(bf16[4,8192]{1,0:T(4,128)(2,1)S(1)} %get-tuple-element.37), channel_id=1, source_target_pairs={{0,2},{1,3},{2,0},{3,1},{4,6},{5,7},{6,4},{7,5},{8,10},{9,11},{10,... | collective-permute-start | bytes 196616 | tf_op jit(solution)/shard_map/ppermute | solution.py:133
  32.9 0.5 %collective-permute-start.9 = (bf16[4,8192]{1,0:T(4,128)(2,1)S(1)}, bf16[4,8192]{1,0:T(4,128)(2,1)S(1)}, u32[]{:S(2)}, u32[]{:S(2)}) collective-permute-start(bf16[4,8192]{1,0:T(4,128)(2,1)S(1)} %get-tuple-element.39), channel_id=1, source_target_pairs={{0,16},{1,17},{2,18},{3,19},{4,20},{5,21},{6,22},{7,23},{8,24},{9,... | collective-permute-start | bytes 196616 | tf_op jit(solution)/shard_map/ppermute | solution.py:133
  33.5 1.7 %collective-permute-done.10 = bf16[4,8192]{1,0:T(4,128)(2,1)S(1)} collective-permute-done((bf16[4,8192]{1,0:T(4,128)(2,1)S(1)}, bf16[4,8192]{1,0:T(4,128)(2,1)S(1)}, u32[]{:S(2)}, u32[]{:S(2)}) %collective-permute-start.10) | collective-permute-done | bytes 65568 | tf_op jit(solution)/shard_map/ppermute | solution.py:133
  35.2 1.5 %collective-permute-done.8 = bf16[4,8192]{1,0:T(4,128)(2,1)S(1)} collective-permute-done((bf16[4,8192]{1,0:T(4,128)(2,1)S(1)}, bf16[4,8192]{1,0:T(4,128)(2,1)S(1)}, u32[]{:S(2)}, u32[]{:S(2)}) %collective-permute-start.8) | collective-permute-done | bytes 65568 | tf_op jit(solution)/shard_map/ppermute | solution.py:133
  36.7 0.5 %collective-permute-done.9 = bf16[4,8192]{1,0:T(4,128)(2,1)S(1)} collective-permute-done((bf16[4,8192]{1,0:T(4,128)(2,1)S(1)}, bf16[4,8192]{1,0:T(4,128)(2,1)S(1)}, u32[]{:S(2)}, u32[]{:S(2)}) %collective-permute-start.9) | collective-permute-done | bytes 65568 | tf_op jit(solution)/shard_map/ppermute | solution.py:133
  37.4 2.1 %collective-permute-start.11 = (bf16[1,8192]{1,0:T(2,128)(2,1)S(1)}, bf16[1,8192]{1,0:T(2,128)(2,1)S(1)}, u32[]{:S(2)}, u32[]{:S(2)}) collective-permute-start(bf16[1,8192]{1,0:T(2,128)(2,1)S(1)} %get-tuple-element.42), channel_id=1, source_target_pairs={{0,8},{1,9},{2,10},{3,11},{4,12},{5,13},{6,14},{7,15},{8,0},{9,1},... | collective-permute-start | bytes 49160 | tf_op jit(solution)/shard_map/ppermute | solution.py:133
  39.5 1.4 %collective-permute-start.12 = (bf16[1,8192]{1,0:T(2,128)(2,1)S(1)}, bf16[1,8192]{1,0:T(2,128)(2,1)S(1)}, u32[]{:S(2)}, u32[]{:S(2)}) collective-permute-start(bf16[1,8192]{1,0:T(2,128)(2,1)S(1)} %get-tuple-element.44), channel_id=1, source_target_pairs={{0,12},{1,13},{2,14},{3,15},{4,8},{5,9},{6,10},{7,11},{8,4},{9,5},... | collective-permute-start | bytes 49160 | tf_op jit(solution)/shard_map/ppermute | solution.py:133
  41.1 1.2 %collective-permute-done.11 = bf16[1,8192]{1,0:T(2,128)(2,1)S(1)} collective-permute-done((bf16[1,8192]{1,0:T(2,128)(2,1)S(1)}, bf16[1,8192]{1,0:T(2,128)(2,1)S(1)}, u32[]{:S(2)}, u32[]{:S(2)}) %collective-permute-start.11) | collective-permute-done | bytes 16416 | tf_op jit(solution)/shard_map/ppermute | solution.py:133
  42.3 3.0 %collective-permute-done.12 = bf16[1,8192]{1,0:T(2,128)(2,1)S(1)} collective-permute-done((bf16[1,8192]{1,0:T(2,128)(2,1)S(1)}, bf16[1,8192]{1,0:T(2,128)(2,1)S(1)}, u32[]{:S(2)}, u32[]{:S(2)}) %collective-permute-start.12) | collective-permute-done | bytes 16416 | tf_op jit(solution)/shard_map/ppermute | solution.py:133
  45.2 0.7 %fusion.6 = bf16[1,8192]{1,0:T(2,128)(2,1)} fusion(bf16[1,8192]{1,0:T(2,128)(2,1)S(1)} %collective-permute-done.13, bf16[1,8192]{1,0:T(2,128)(2,1)S(1)} %collective-permute-done.12, bf16[1,8192]{1,0:T(2,128)(2,1)S(1)} %collective-permute-done.11, f32[4,8192]{1,0:T(4,128)S(1)} %get-tuple-element.34), kind=kLoop, calls=%fused_computation.16 | loop fusion | flops 57344 | bytes 98304 | tf_op jit(solution)/shard_map/convert_element_type | solution.py:567
  (19 shorter events, 1.0 us)
Async XLA Ops:
  2.1 1.5 %collective-permute-start = (bf16[2,16,1664]{2,1,0:T(8,128)(2,1)S(1)}, bf16[2,16,1664]{2,1,0:T(8,128)(2,1)S(1)}, u32[]{:S(2)}, u32[]{:S(2)}) collective-permute-start(bf16[2,16,1664]{2,1,0:T(8,128)(2,1)S(1)} %get-tuple-element.19), channel_id=1, source_target_pairs={{0,1},{1,0},{2,3},{3,2},{4,5},{5,4},{6,7},{7,6},{8,9},{9,8},{10,11... | collective-permute-start | bytes 319496 | tf_op jit(solution)/shard_map/ppermute | solution.py:133
  3.6 9.6 %collective-permute-start.1 = (bf16[16,1664]{1,0:T(8,128)(2,1)S(1)}, bf16[16,1664]{1,0:T(8,128)(2,1)S(1)}, u32[]{:S(2)}, u32[]{:S(2)}) collective-permute-start(bf16[16,1664]{1,0:T(8,128)(2,1)S(1)} %get-tuple-element.40), channel_id=1, source_target_pairs={{0,8},{1,9},{2,10},{3,11},{4,12},{5,13},{6,14},{7,15},{8,0},{9,1},... | collective-permute-start | bytes 159752 | tf_op jit(solution)/shard_map/ppermute | solution.py:133
  7.6 6.4 %collective-permute-start.2 = (bf16[16,1664]{1,0:T(8,128)(2,1)S(1)}, bf16[16,1664]{1,0:T(8,128)(2,1)S(1)}, u32[]{:S(2)}, u32[]{:S(2)}) collective-permute-start(bf16[16,1664]{1,0:T(8,128)(2,1)S(1)} %get-tuple-element.41), channel_id=1, source_target_pairs={{0,24},{1,25},{2,26},{3,27},{4,28},{5,29},{6,30},{7,31},{8,16},{9,... | collective-permute-start | bytes 159752 | tf_op jit(solution)/shard_map/ppermute | solution.py:133
  8.9 5.2 %collective-permute-start.3 = (bf16[16,1664]{1,0:T(8,128)(2,1)S(1)}, bf16[16,1664]{1,0:T(8,128)(2,1)S(1)}, u32[]{:S(2)}, u32[]{:S(2)}) collective-permute-start(bf16[16,1664]{1,0:T(8,128)(2,1)S(1)} %get-tuple-element.41), channel_id=1, source_target_pairs={{0,16},{1,17},{2,18},{3,19},{4,20},{5,21},{6,22},{7,23},{8,24},{9,... | collective-permute-start | bytes 159752 | tf_op jit(solution)/shard_map/ppermute | solution.py:133
  14.1 8.2 %collective-permute-start.4 = (bf16[32,1664]{1,0:T(8,128)(2,1)S(1)}, bf16[32,1664]{1,0:T(8,128)(2,1)S(1)}, u32[]{:S(2)}, u32[]{:S(2)}) collective-permute-start(bf16[32,1664]{1,0:T(8,128)(2,1)S(1)} %pad_maximum_fusion.own_ref), channel_id=1, source_target_pairs={{0,6},{1,7},{2,4},{3,5},{4,2},{5,3},{6,0},{7,1},{8,14},{9,15},{10,... | collective-permute-start | bytes 319496 | tf_op jit(solution)/shard_map/ppermute | solution.py:133
  16.3 6.0 %collective-permute-start.5 = (bf16[32,1664]{1,0:T(8,128)(2,1)S(1)}, bf16[32,1664]{1,0:T(8,128)(2,1)S(1)}, u32[]{:S(2)}, u32[]{:S(2)}) collective-permute-start(bf16[32,1664]{1,0:T(8,128)(2,1)S(1)} %pad_maximum_fusion.own_ref), channel_id=1, source_target_pairs={{0,2},{1,3},{2,0},{3,1},{4,6},{5,7},{6,4},{7,5},{8,10},{9,11},{10,... | collective-permute-start | bytes 319496 | tf_op jit(solution)/shard_map/ppermute | solution.py:133
  16.8 5.5 %collective-permute-start.6 = (bf16[32,1664]{1,0:T(8,128)(2,1)S(1)}, bf16[32,1664]{1,0:T(8,128)(2,1)S(1)}, u32[]{:S(2)}, u32[]{:S(2)}) collective-permute-start(bf16[32,1664]{1,0:T(8,128)(2,1)S(1)} %pad_maximum_fusion.own_ref), channel_id=1, source_target_pairs={{0,4},{1,5},{2,6},{3,7},{4,0},{5,1},{6,2},{7,3},{8,12},{9,13},{10,... | collective-permute-start | bytes 319496 | tf_op jit(solution)/shard_map/ppermute | solution.py:133
  28.2 1.6 %collective-permute-start.7 = (bf16[16,8192]{1,0:T(8,128)(2,1)S(1)}, bf16[16,8192]{1,0:T(8,128)(2,1)S(1)}, u32[]{:S(2)}, u32[]{:S(2)}) collective-permute-start(bf16[16,8192]{1,0:T(8,128)(2,1)S(1)} %get-tuple-element.32), channel_id=1, source_target_pairs={{0,1},{1,0},{2,3},{3,2},{4,5},{5,4},{6,7},{7,6},{8,9},{9,8},{10,11... | collective-permute-start | bytes 786440 | tf_op jit(solution)/shard_map/ppermute | solution.py:133
  29.9 5.3 %collective-permute-start.10 = (bf16[4,8192]{1,0:T(4,128)(2,1)S(1)}, bf16[4,8192]{1,0:T(4,128)(2,1)S(1)}, u32[]{:S(2)}, u32[]{:S(2)}) collective-permute-start(bf16[4,8192]{1,0:T(4,128)(2,1)S(1)} %get-tuple-element.38), channel_id=1, source_target_pairs={{0,18},{1,19},{2,16},{3,17},{4,22},{5,23},{6,20},{7,21},{8,26},{9,... | collective-permute-start | bytes 196616 | tf_op jit(solution)/shard_map/ppermute | solution.py:133
  32.4 4.3 %collective-permute-start.8 = (bf16[4,8192]{1,0:T(4,128)(2,1)S(1)}, bf16[4,8192]{1,0:T(4,128)(2,1)S(1)}, u32[]{:S(2)}, u32[]{:S(2)}) collective-permute-start(bf16[4,8192]{1,0:T(4,128)(2,1)S(1)} %get-tuple-element.37), channel_id=1, source_target_pairs={{0,2},{1,3},{2,0},{3,1},{4,6},{5,7},{6,4},{7,5},{8,10},{9,11},{10,... | collective-permute-start | bytes 196616 | tf_op jit(solution)/shard_map/ppermute | solution.py:133
  32.9 4.3 %collective-permute-start.9 = (bf16[4,8192]{1,0:T(4,128)(2,1)S(1)}, bf16[4,8192]{1,0:T(4,128)(2,1)S(1)}, u32[]{:S(2)}, u32[]{:S(2)}) collective-permute-start(bf16[4,8192]{1,0:T(4,128)(2,1)S(1)} %get-tuple-element.39), channel_id=1, source_target_pairs={{0,16},{1,17},{2,18},{3,19},{4,20},{5,21},{6,22},{7,23},{8,24},{9,... | collective-permute-start | bytes 196616 | tf_op jit(solution)/shard_map/ppermute | solution.py:133
  37.4 4.9 %collective-permute-start.11 = (bf16[1,8192]{1,0:T(2,128)(2,1)S(1)}, bf16[1,8192]{1,0:T(2,128)(2,1)S(1)}, u32[]{:S(2)}, u32[]{:S(2)}) collective-permute-start(bf16[1,8192]{1,0:T(2,128)(2,1)S(1)} %get-tuple-element.42), channel_id=1, source_target_pairs={{0,8},{1,9},{2,10},{3,11},{4,12},{5,13},{6,14},{7,15},{8,0},{9,1},... | collective-permute-start | bytes 49160 | tf_op jit(solution)/shard_map/ppermute | solution.py:133
  39.5 5.7 %collective-permute-start.12 = (bf16[1,8192]{1,0:T(2,128)(2,1)S(1)}, bf16[1,8192]{1,0:T(2,128)(2,1)S(1)}, u32[]{:S(2)}, u32[]{:S(2)}) collective-permute-start(bf16[1,8192]{1,0:T(2,128)(2,1)S(1)} %get-tuple-element.44), channel_id=1, source_target_pairs={{0,12},{1,13},{2,14},{3,15},{4,8},{5,9},{6,10},{7,11},{8,4},{9,5},... | collective-permute-start | bytes 49160 | tf_op jit(solution)/shard_map/ppermute | solution.py:133
  40.9 4.3 %collective-permute-start.13 = (bf16[1,8192]{1,0:T(2,128)(2,1)S(1)}, bf16[1,8192]{1,0:T(2,128)(2,1)S(1)}, u32[]{:S(2)}, u32[]{:S(2)}) collective-permute-start(bf16[1,8192]{1,0:T(2,128)(2,1)S(1)} %get-tuple-element.43), channel_id=1, source_target_pairs={{0,4},{1,5},{2,6},{3,7},{4,0},{5,1},{6,2},{7,3},{8,12},{9,13},{10,... | collective-permute-start | bytes 49160 | tf_op jit(solution)/shard_map/ppermute | solution.py:133

commit v7 on v6

--- a/solution.py
+++ b/solution.py
@@ -138,7 +138,7 @@
 
 
 def middle_order(count):
-    return [count - 1] + list(range(1, count - 1))
+    return list(range(count - 1, 0, -1))
 
 
 def in_hbm(array):
@@ -288,10 +288,13 @@
 def widen(group, scales_ref, wide_ref):
     per = wide_ref.shape[0]
     for part in range(2):
+        low = part * per // 16 * 16
+        high = min(-(-(part + 1) * per // 16) * 16, scales_ref.shape[0])
 
         @pl.when(group == part)
-        def _(part=part):
-            wide_ref[...] = scales_ref[part * per : (part + 1) * per, :].astype(jnp.float32)
+        def _(part=part, low=low, high=high):
+            wide = scales_ref[low:high, :].astype(jnp.float32)
+            wide_ref[...] = wide[part * per - low : (part + 1) * per - low]
 
 
 def unpack_tile(words, scales_ref, column, target, at, spans):

time: 46.1 us -> 46.1 us (level)
  no operation moved by 1% of the time
where the time goes in v7:
time: 46.1 us; the launch traced here: 45.9 us
  starting transfers between devices  17 us (37%)
  Pallas kernels  16.5 us (36%)
  waiting for transfers between devices  11.1 us (24%)
  other arithmetic  0.99 us (2%)
    ppermute x14, starting transfers between devices, exchanged(): return lax.ppermute(value, AXES, pairs)  17 us
    ppermute x14, waiting for transfers between devices, exchanged(): return lax.ppermute(value, AXES, pairs)  11.1 us
    pallas_call x1, Pallas kernels, product(): pl.pallas_call(functools.partial(product_kernel, len(ready)), in_specs=[p...  5.83 us
    pallas_call x1, Pallas kernels, unpack(): pl.pallas_call(functools.partial(unpack_kernel, first), in_specs=[pl.Bloc...  4.55 us
    pallas_call x1, Pallas kernels, first_unpack(): pl.pallas_call(first_kernel, in_specs=[pl.BlockSpec(memory_space=pltpu.SM...  4.05 us
    pallas_call x1, Pallas kernels, local_rotation(): pl.pallas_call(local_kernel, in_specs=[pl.BlockSpec(memory_space=pltpu.SM...  2.08 us
  transfers between devices with their start and end apart: 14, of which 8 were waited for; matrix products, arithmetic and copies ran while one was open for 0% of the time, Pallas kernels for 19%

profile of v7, /device:TPU:0, one launch (start us, length us, event | category | flops | bytes accessed | tf_op | source)
XLA Modules:
  0.0 45.9 jit_solution(3024243162257472646)
XLA Ops:
  0.0 2.1 %local_rotation.1 = (bf16[2,16,1664]{2,1,0:T(8,128)(2,1)S(1)}, bf16[104,8192]{1,0:T(8,128)(2,1)S(1)}) custom-call(s32[1]{0:T(128)} %bitcast.group_ref, bf16[16,3328]{1,0:T(8,128)(2,1)} %bitcast.10, bf16[16,3328]{1,0:T(8,128)(2,1)} %bitcast.11, bf16[1664,128]{1,0:T(8,128)(2,1)} %constant.47.clone.table_hbm, bf16[104,8192]{1,0:T(8,128)(2,1)} %scales_hbm.1), custom_call_target="tpu_custom_call" | custom-call | flops 100000000 | bytes 8388608 | tf_op jit(solution)/shard_map/local_rotation/pallas_call | solution.py:251
  2.1 0.5 %collective-permute-start = (bf16[2,16,1664]{2,1,0:T(8,128)(2,1)S(1)}, bf16[2,16,1664]{2,1,0:T(8,128)(2,1)S(1)}, u32[]{:S(2)}, u32[]{:S(2)}) collective-permute-start(bf16[2,16,1664]{2,1,0:T(8,128)(2,1)S(1)} %get-tuple-element.19), channel_id=1, source_target_pairs={{0,1},{1,0},{2,3},{3,2},{4,5},{5,4},{6,7},{7,6},{8,9},{9,8},{10,11... | collective-permute-start | bytes 319496 | tf_op jit(solution)/shard_map/ppermute | solution.py:133
  2.6 1.0 %collective-permute-done = bf16[2,16,1664]{2,1,0:T(8,128)(2,1)S(1)} collective-permute-done((bf16[2,16,1664]{2,1,0:T(8,128)(2,1)S(1)}, bf16[2,16,1664]{2,1,0:T(8,128)(2,1)S(1)}, u32[]{:S(2)}, u32[]{:S(2)}) %collective-permute-start) | collective-permute-done | bytes 106528 | tf_op jit(solution)/shard_map/ppermute | solution.py:133
  3.6 4.0 %collective-permute-start.1 = (bf16[16,1664]{1,0:T(8,128)(2,1)S(1)}, bf16[16,1664]{1,0:T(8,128)(2,1)S(1)}, u32[]{:S(2)}, u32[]{:S(2)}) collective-permute-start(bf16[16,1664]{1,0:T(8,128)(2,1)S(1)} %get-tuple-element.40), channel_id=1, source_target_pairs={{0,8},{1,9},{2,10},{3,11},{4,12},{5,13},{6,14},{7,15},{8,0},{9,1},... | collective-permute-start | bytes 159752 | tf_op jit(solution)/shard_map/ppermute | solution.py:133
  7.6 1.3 %collective-permute-start.2 = (bf16[16,1664]{1,0:T(8,128)(2,1)S(1)}, bf16[16,1664]{1,0:T(8,128)(2,1)S(1)}, u32[]{:S(2)}, u32[]{:S(2)}) collective-permute-start(bf16[16,1664]{1,0:T(8,128)(2,1)S(1)} %get-tuple-element.41), channel_id=1, source_target_pairs={{0,24},{1,25},{2,26},{3,27},{4,28},{5,29},{6,30},{7,31},{8,16},{9,... | collective-permute-start | bytes 159752 | tf_op jit(solution)/shard_map/ppermute | solution.py:133
  9.2 4.0 %first_unpack.1 = (bf16[1664,512]{1,0:T(8,128)(2,1)S(1)}, s32[5,832,512]{2,1,0:T(8,128)S(1)}, f32[52,8192]{1,0:T(8,128)S(1)}) custom-call(s32[1]{0:T(128)} %bitcast.group_ref, s32[1664,8192]{1,0:T(8,128)} %codes_hbm.5, bf16[104,8192]{1,0:T(8,128)(2,1)S(1)} %get-tuple-element.22.scales_in), custom_call_target="tpu_custom_call" | custom-call | bytes 10223616 | tf_op jit(solution)/shard_map/first_unpack/pallas_call | solution.py:333
  13.3 0.8 %collective-permute-done.2 = bf16[16,1664]{1,0:T(8,128)(2,1)S(1)} collective-permute-done((bf16[16,1664]{1,0:T(8,128)(2,1)S(1)}, bf16[16,1664]{1,0:T(8,128)(2,1)S(1)}, u32[]{:S(2)}, u32[]{:S(2)}) %collective-permute-start.2) | collective-permute-done | bytes 53280 | tf_op jit(solution)/shard_map/ppermute | solution.py:133
  14.1 2.2 %collective-permute-start.4 = (bf16[32,1664]{1,0:T(8,128)(2,1)S(1)}, bf16[32,1664]{1,0:T(8,128)(2,1)S(1)}, u32[]{:S(2)}, u32[]{:S(2)}) collective-permute-start(bf16[32,1664]{1,0:T(8,128)(2,1)S(1)} %pad_maximum_fusion.own_ref), channel_id=1, source_target_pairs={{0,6},{1,7},{2,4},{3,5},{4,2},{5,3},{6,0},{7,1},{8,14},{9,15},{10,... | collective-permute-start | bytes 319496 | tf_op jit(solution)/shard_map/ppermute | solution.py:133
  16.3 0.9 %collective-permute-start.5 = (bf16[32,1664]{1,0:T(8,128)(2,1)S(1)}, bf16[32,1664]{1,0:T(8,128)(2,1)S(1)}, u32[]{:S(2)}, u32[]{:S(2)}) collective-permute-start(bf16[32,1664]{1,0:T(8,128)(2,1)S(1)} %pad_maximum_fusion.own_ref), channel_id=1, source_target_pairs={{0,4},{1,5},{2,6},{3,7},{4,0},{5,1},{6,2},{7,3},{8,12},{9,13},{10,... | collective-permute-start | bytes 319496 | tf_op jit(solution)/shard_map/ppermute | solution.py:133
  17.2 0.5 %collective-permute-start.6 = (bf16[32,1664]{1,0:T(8,128)(2,1)S(1)}, bf16[32,1664]{1,0:T(8,128)(2,1)S(1)}, u32[]{:S(2)}, u32[]{:S(2)}) collective-permute-start(bf16[32,1664]{1,0:T(8,128)(2,1)S(1)} %pad_maximum_fusion.own_ref), channel_id=1, source_target_pairs={{0,2},{1,3},{2,0},{3,1},{4,6},{5,7},{6,4},{7,5},{8,10},{9,11},{10,... | collective-permute-start | bytes 319496 | tf_op jit(solution)/shard_map/ppermute | solution.py:133
  17.7 4.5 %unpack.1 = (bf16[1664,4608]{1,0:T(8,128)(2,1)S(1)}, s32[3,832,512]{2,1,0:T(8,128)S(1)}) custom-call(s32[1]{0:T(128)} %bitcast.group_ref, s32[1664,8192]{1,0:T(8,128)} %codes_hbm.5, f32[52,8192]{1,0:T(8,128)S(1)} %get-tuple-element.25.scales_ref, s32[5,832,512]{2,1,0:T(8,128)S(1)} %get-tuple-element.26.given), custom_call_target="tpu_custom_call" | custom-call | flops 61341696 | bytes 30670848 | tf_op jit(solution)/shard_map/unpack/pallas_call | solution.py:386
  22.3 5.8 %product.1 = (f32[16,8192]{1,0:T(8,128)S(1)}, bf16[16,8192]{1,0:T(8,128)(2,1)S(1)}) custom-call(s32[2]{0:T(128)S(1)} %pad_add_fusion.place_ref, s32[1664,8192]{1,0:T(8,128)} %codes_hbm.5, s32[3,832,512]{2,1,0:T(8,128)S(1)} %get-tuple-element.27.given, f32[52,8192]{1,0:T(8,128)S(1)} %get-tuple-element.25.scales_ref, ...), custom_call_target="tpu_custom_call" | custom-call | tf_op jit(solution)/shard_map/product/pallas_call | solution.py:493
  28.2 1.5 %collective-permute-done.7 = bf16[16,8192]{1,0:T(8,128)(2,1)S(1)} collective-permute-done((bf16[16,8192]{1,0:T(8,128)(2,1)S(1)}, bf16[16,8192]{1,0:T(8,128)(2,1)S(1)}, u32[]{:S(2)}, u32[]{:S(2)}) %collective-permute-start.7) | collective-permute-done | bytes 262176 | tf_op jit(solution)/shard_map/ppermute | solution.py:133
  29.9 2.5 %collective-permute-start.10 = (bf16[4,8192]{1,0:T(4,128)(2,1)S(1)}, bf16[4,8192]{1,0:T(4,128)(2,1)S(1)}, u32[]{:S(2)}, u32[]{:S(2)}) collective-permute-start(bf16[4,8192]{1,0:T(4,128)(2,1)S(1)} %get-tuple-element.38), channel_id=1, source_target_pairs={{0,18},{1,19},{2,16},{3,17},{4,22},{5,23},{6,20},{7,21},{8,26},{9,... | collective-permute-start | bytes 196616 | tf_op jit(solution)/shard_map/ppermute | solution.py:133
  32.4 0.5 %collective-permute-start.8 = (bf16[4,8192]{1,0:T(4,128)(2,1)S(1)}, bf16[4,8192]{1,0:T(4,128)(2,1)S(1)}, u32[]{:S(2)}, u32[]{:S(2)}) collective-permute-start(bf16[4,8192]{1,0:T(4,128)(2,1)S(1)} %get-tuple-element.37), channel_id=1, source_target_pairs={{0,2},{1,3},{2,0},{3,1},{4,6},{5,7},{6,4},{7,5},{8,10},{9,11},{10,... | collective-permute-start | bytes 196616 | tf_op jit(solution)/shard_map/ppermute | solution.py:133
  32.9 0.5 %collective-permute-start.9 = (bf16[4,8192]{1,0:T(4,128)(2,1)S(1)}, bf16[4,8192]{1,0:T(4,128)(2,1)S(1)}, u32[]{:S(2)}, u32[]{:S(2)}) collective-permute-start(bf16[4,8192]{1,0:T(4,128)(2,1)S(1)} %get-tuple-element.39), channel_id=1, source_target_pairs={{0,16},{1,17},{2,18},{3,19},{4,20},{5,21},{6,22},{7,23},{8,24},{9,... | collective-permute-start | bytes 196616 | tf_op jit(solution)/shard_map/ppermute | solution.py:133
  33.5 1.7 %collective-permute-done.10 = bf16[4,8192]{1,0:T(4,128)(2,1)S(1)} collective-permute-done((bf16[4,8192]{1,0:T(4,128)(2,1)S(1)}, bf16[4,8192]{1,0:T(4,128)(2,1)S(1)}, u32[]{:S(2)}, u32[]{:S(2)}) %collective-permute-start.10) | collective-permute-done | bytes 65568 | tf_op jit(solution)/shard_map/ppermute | solution.py:133
  35.2 1.5 %collective-permute-done.8 = bf16[4,8192]{1,0:T(4,128)(2,1)S(1)} collective-permute-done((bf16[4,8192]{1,0:T(4,128)(2,1)S(1)}, bf16[4,8192]{1,0:T(4,128)(2,1)S(1)}, u32[]{:S(2)}, u32[]{:S(2)}) %collective-permute-start.8) | collective-permute-done | bytes 65568 | tf_op jit(solution)/shard_map/ppermute | solution.py:133
  36.7 0.5 %collective-permute-done.9 = bf16[4,8192]{1,0:T(4,128)(2,1)S(1)} collective-permute-done((bf16[4,8192]{1,0:T(4,128)(2,1)S(1)}, bf16[4,8192]{1,0:T(4,128)(2,1)S(1)}, u32[]{:S(2)}, u32[]{:S(2)}) %collective-permute-start.9) | collective-permute-done | bytes 65568 | tf_op jit(solution)/shard_map/ppermute | solution.py:133
  37.4 2.1 %collective-permute-start.11 = (bf16[1,8192]{1,0:T(2,128)(2,1)S(1)}, bf16[1,8192]{1,0:T(2,128)(2,1)S(1)}, u32[]{:S(2)}, u32[]{:S(2)}) collective-permute-start(bf16[1,8192]{1,0:T(2,128)(2,1)S(1)} %get-tuple-element.42), channel_id=1, source_target_pairs={{0,8},{1,9},{2,10},{3,11},{4,12},{5,13},{6,14},{7,15},{8,0},{9,1},... | collective-permute-start | bytes 49160 | tf_op jit(solution)/shard_map/ppermute | solution.py:133
  39.5 1.4 %collective-permute-start.12 = (bf16[1,8192]{1,0:T(2,128)(2,1)S(1)}, bf16[1,8192]{1,0:T(2,128)(2,1)S(1)}, u32[]{:S(2)}, u32[]{:S(2)}) collective-permute-start(bf16[1,8192]{1,0:T(2,128)(2,1)S(1)} %get-tuple-element.44), channel_id=1, source_target_pairs={{0,12},{1,13},{2,14},{3,15},{4,8},{5,9},{6,10},{7,11},{8,4},{9,5},... | collective-permute-start | bytes 49160 | tf_op jit(solution)/shard_map/ppermute | solution.py:133
  41.1 1.2 %collective-permute-done.11 = bf16[1,8192]{1,0:T(2,128)(2,1)S(1)} collective-permute-done((bf16[1,8192]{1,0:T(2,128)(2,1)S(1)}, bf16[1,8192]{1,0:T(2,128)(2,1)S(1)}, u32[]{:S(2)}, u32[]{:S(2)}) %collective-permute-start.11) | collective-permute-done | bytes 16416 | tf_op jit(solution)/shard_map/ppermute | solution.py:133
  42.3 3.0 %collective-permute-done.12 = bf16[1,8192]{1,0:T(2,128)(2,1)S(1)} collective-permute-done((bf16[1,8192]{1,0:T(2,128)(2,1)S(1)}, bf16[1,8192]{1,0:T(2,128)(2,1)S(1)}, u32[]{:S(2)}, u32[]{:S(2)}) %collective-permute-start.12) | collective-permute-done | bytes 16416 | tf_op jit(solution)/shard_map/ppermute | solution.py:133
  45.2 0.7 %fusion.6 = bf16[1,8192]{1,0:T(2,128)(2,1)} fusion(bf16[1,8192]{1,0:T(2,128)(2,1)S(1)} %collective-permute-done.13, bf16[1,8192]{1,0:T(2,128)(2,1)S(1)} %collective-permute-done.12, bf16[1,8192]{1,0:T(2,128)(2,1)S(1)} %collective-permute-done.11, f32[4,8192]{1,0:T(4,128)S(1)} %get-tuple-element.34), kind=kLoop, calls=%fused_computation.16 | loop fusion | flops 57344 | bytes 98304 | tf_op jit(solution)/shard_map/convert_element_type | solution.py:570
  (19 shorter events, 1.0 us)
Async XLA Ops:
  2.1 1.5 %collective-permute-start = (bf16[2,16,1664]{2,1,0:T(8,128)(2,1)S(1)}, bf16[2,16,1664]{2,1,0:T(8,128)(2,1)S(1)}, u32[]{:S(2)}, u32[]{:S(2)}) collective-permute-start(bf16[2,16,1664]{2,1,0:T(8,128)(2,1)S(1)} %get-tuple-element.19), channel_id=1, source_target_pairs={{0,1},{1,0},{2,3},{3,2},{4,5},{5,4},{6,7},{7,6},{8,9},{9,8},{10,11... | collective-permute-start | bytes 319496 | tf_op jit(solution)/shard_map/ppermute | solution.py:133
  3.6 9.6 %collective-permute-start.1 = (bf16[16,1664]{1,0:T(8,128)(2,1)S(1)}, bf16[16,1664]{1,0:T(8,128)(2,1)S(1)}, u32[]{:S(2)}, u32[]{:S(2)}) collective-permute-start(bf16[16,1664]{1,0:T(8,128)(2,1)S(1)} %get-tuple-element.40), channel_id=1, source_target_pairs={{0,8},{1,9},{2,10},{3,11},{4,12},{5,13},{6,14},{7,15},{8,0},{9,1},... | collective-permute-start | bytes 159752 | tf_op jit(solution)/shard_map/ppermute | solution.py:133
  7.6 6.4 %collective-permute-start.2 = (bf16[16,1664]{1,0:T(8,128)(2,1)S(1)}, bf16[16,1664]{1,0:T(8,128)(2,1)S(1)}, u32[]{:S(2)}, u32[]{:S(2)}) collective-permute-start(bf16[16,1664]{1,0:T(8,128)(2,1)S(1)} %get-tuple-element.41), channel_id=1, source_target_pairs={{0,24},{1,25},{2,26},{3,27},{4,28},{5,29},{6,30},{7,31},{8,16},{9,... | collective-permute-start | bytes 159752 | tf_op jit(solution)/shard_map/ppermute | solution.py:133
  8.9 5.2 %collective-permute-start.3 = (bf16[16,1664]{1,0:T(8,128)(2,1)S(1)}, bf16[16,1664]{1,0:T(8,128)(2,1)S(1)}, u32[]{:S(2)}, u32[]{:S(2)}) collective-permute-start(bf16[16,1664]{1,0:T(8,128)(2,1)S(1)} %get-tuple-element.41), channel_id=1, source_target_pairs={{0,16},{1,17},{2,18},{3,19},{4,20},{5,21},{6,22},{7,23},{8,24},{9,... | collective-permute-start | bytes 159752 | tf_op jit(solution)/shard_map/ppermute | solution.py:133
  14.1 8.2 %collective-permute-start.4 = (bf16[32,1664]{1,0:T(8,128)(2,1)S(1)}, bf16[32,1664]{1,0:T(8,128)(2,1)S(1)}, u32[]{:S(2)}, u32[]{:S(2)}) collective-permute-start(bf16[32,1664]{1,0:T(8,128)(2,1)S(1)} %pad_maximum_fusion.own_ref), channel_id=1, source_target_pairs={{0,6},{1,7},{2,4},{3,5},{4,2},{5,3},{6,0},{7,1},{8,14},{9,15},{10,... | collective-permute-start | bytes 319496 | tf_op jit(solution)/shard_map/ppermute | solution.py:133
  16.3 6.0 %collective-permute-start.5 = (bf16[32,1664]{1,0:T(8,128)(2,1)S(1)}, bf16[32,1664]{1,0:T(8,128)(2,1)S(1)}, u32[]{:S(2)}, u32[]{:S(2)}) collective-permute-start(bf16[32,1664]{1,0:T(8,128)(2,1)S(1)} %pad_maximum_fusion.own_ref), channel_id=1, source_target_pairs={{0,4},{1,5},{2,6},{3,7},{4,0},{5,1},{6,2},{7,3},{8,12},{9,13},{10,... | collective-permute-start | bytes 319496 | tf_op jit(solution)/shard_map/ppermute | solution.py:133
  17.2 5.2 %collective-permute-start.6 = (bf16[32,1664]{1,0:T(8,128)(2,1)S(1)}, bf16[32,1664]{1,0:T(8,128)(2,1)S(1)}, u32[]{:S(2)}, u32[]{:S(2)}) collective-permute-start(bf16[32,1664]{1,0:T(8,128)(2,1)S(1)} %pad_maximum_fusion.own_ref), channel_id=1, source_target_pairs={{0,2},{1,3},{2,0},{3,1},{4,6},{5,7},{6,4},{7,5},{8,10},{9,11},{10,... | collective-permute-start | bytes 319496 | tf_op jit(solution)/shard_map/ppermute | solution.py:133
  28.2 1.6 %collective-permute-start.7 = (bf16[16,8192]{1,0:T(8,128)(2,1)S(1)}, bf16[16,8192]{1,0:T(8,128)(2,1)S(1)}, u32[]{:S(2)}, u32[]{:S(2)}) collective-permute-start(bf16[16,8192]{1,0:T(8,128)(2,1)S(1)} %get-tuple-element.32), channel_id=1, source_target_pairs={{0,1},{1,0},{2,3},{3,2},{4,5},{5,4},{6,7},{7,6},{8,9},{9,8},{10,11... | collective-permute-start | bytes 786440 | tf_op jit(solution)/shard_map/ppermute | solution.py:133
  29.9 5.3 %collective-permute-start.10 = (bf16[4,8192]{1,0:T(4,128)(2,1)S(1)}, bf16[4,8192]{1,0:T(4,128)(2,1)S(1)}, u32[]{:S(2)}, u32[]{:S(2)}) collective-permute-start(bf16[4,8192]{1,0:T(4,128)(2,1)S(1)} %get-tuple-element.38), channel_id=1, source_target_pairs={{0,18},{1,19},{2,16},{3,17},{4,22},{5,23},{6,20},{7,21},{8,26},{9,... | collective-permute-start | bytes 196616 | tf_op jit(solution)/shard_map/ppermute | solution.py:133
  32.4 4.3 %collective-permute-start.8 = (bf16[4,8192]{1,0:T(4,128)(2,1)S(1)}, bf16[4,8192]{1,0:T(4,128)(2,1)S(1)}, u32[]{:S(2)}, u32[]{:S(2)}) collective-permute-start(bf16[4,8192]{1,0:T(4,128)(2,1)S(1)} %get-tuple-element.37), channel_id=1, source_target_pairs={{0,2},{1,3},{2,0},{3,1},{4,6},{5,7},{6,4},{7,5},{8,10},{9,11},{10,... | collective-permute-start | bytes 196616 | tf_op jit(solution)/shard_map/ppermute | solution.py:133
  32.9 4.3 %collective-permute-start.9 = (bf16[4,8192]{1,0:T(4,128)(2,1)S(1)}, bf16[4,8192]{1,0:T(4,128)(2,1)S(1)}, u32[]{:S(2)}, u32[]{:S(2)}) collective-permute-start(bf16[4,8192]{1,0:T(4,128)(2,1)S(1)} %get-tuple-element.39), channel_id=1, source_target_pairs={{0,16},{1,17},{2,18},{3,19},{4,20},{5,21},{6,22},{7,23},{8,24},{9,... | collective-permute-start | bytes 196616 | tf_op jit(solution)/shard_map/ppermute | solution.py:133
  37.4 4.9 %collective-permute-start.11 = (bf16[1,8192]{1,0:T(2,128)(2,1)S(1)}, bf16[1,8192]{1,0:T(2,128)(2,1)S(1)}, u32[]{:S(2)}, u32[]{:S(2)}) collective-permute-start(bf16[1,8192]{1,0:T(2,128)(2,1)S(1)} %get-tuple-element.42), channel_id=1, source_target_pairs={{0,8},{1,9},{2,10},{3,11},{4,12},{5,13},{6,14},{7,15},{8,0},{9,1},... | collective-permute-start | bytes 49160 | tf_op jit(solution)/shard_map/ppermute | solution.py:133
  39.5 5.7 %collective-permute-start.12 = (bf16[1,8192]{1,0:T(2,128)(2,1)S(1)}, bf16[1,8192]{1,0:T(2,128)(2,1)S(1)}, u32[]{:S(2)}, u32[]{:S(2)}) collective-permute-start(bf16[1,8192]{1,0:T(2,128)(2,1)S(1)} %get-tuple-element.44), channel_id=1, source_target_pairs={{0,12},{1,13},{2,14},{3,15},{4,8},{5,9},{6,10},{7,11},{8,4},{9,5},... | collective-permute-start | bytes 49160 | tf_op jit(solution)/shard_map/ppermute | solution.py:133
  40.9 4.3 %collective-permute-start.13 = (bf16[1,8192]{1,0:T(2,128)(2,1)S(1)}, bf16[1,8192]{1,0:T(2,128)(2,1)S(1)}, u32[]{:S(2)}, u32[]{:S(2)}) collective-permute-start(bf16[1,8192]{1,0:T(2,128)(2,1)S(1)} %get-tuple-element.43), channel_id=1, source_target_pairs={{0,4},{1,5},{2,6},{3,7},{4,0},{5,1},{6,2},{7,3},{8,12},{9,13},{10,... | collective-permute-start | bytes 49160 | tf_op jit(solution)/shard_map/ppermute | solution.py:133

commit v8 on v7

--- a/solution.py
+++ b/solution.py
@@ -424,6 +424,9 @@
     for copy in copies:
         copy.start()
 
+    unpack_tile(
+        given.at[0], scales_ref, base * tile, first_sc, 0, range(height // WORDS_PER_GROUP)
+    )
     count = len(others) + 1
     middle = 2 * (count - 1)
     total = own_ref[...].astype(jnp.float32) * parity_sign(place, middle)
@@ -466,9 +469,9 @@
             send_ref[:, to : to + tile] = total[rows // 2 :].astype(jnp.bfloat16)
 
     waiting = [(ref, at, index * tile) for index, (ref, at) in enumerate(ready_tiles)]
-    each_stage = -(-base // (tiles - base))
-    previous = None
-    for index in range(base, tiles):
+    each_stage = -(-base // (tiles - base - 1))
+    previous = (first_sc, 0, base * tile)
+    for index in range(base + 1, tiles):
         number = index - base
         if number >= held:
             copies[number - held].wait()
@@ -476,8 +479,7 @@
         target = second_sc if number % 2 else first_sc
         products = waiting[:each_stage]
         waiting = waiting[each_stage:]
-        if previous is not None:
-            products.append(previous)
+        products.append(previous)
         stage(products, (source, index * tile, target))
         previous = (target, 0, index * tile)
     stage(waiting + [previous], None)

time: 46.1 us -> 46.4 us (level)
  no operation moved by 1% of the time
where the time goes in v8:
time: 46.4 us; the launch traced here: 46.3 us
  starting transfers between devices  17 us (37%)
  Pallas kernels  16.9 us (36%)
  waiting for transfers between devices  11.1 us (24%)
  other arithmetic  0.99 us (2%)
    ppermute x14, starting transfers between devices, exchanged(): return lax.ppermute(value, AXES, pairs)  17 us
    ppermute x14, waiting for transfers between devices, exchanged(): return lax.ppermute(value, AXES, pairs)  11.1 us
    pallas_call x1, Pallas kernels, product(): pl.pallas_call(functools.partial(product_kernel, len(ready)), in_specs=[p...  6.18 us
    pallas_call x1, Pallas kernels, unpack(): pl.pallas_call(functools.partial(unpack_kernel, first), in_specs=[pl.Bloc...  4.55 us
    pallas_call x1, Pallas kernels, first_unpack(): pl.pallas_call(first_kernel, in_specs=[pl.BlockSpec(memory_space=pltpu.SM...  4.05 us
    pallas_call x1, Pallas kernels, local_rotation(): pl.pallas_call(local_kernel, in_specs=[pl.BlockSpec(memory_space=pltpu.SM...  2.08 us
  transfers between devices with their start and end apart: 14, of which 8 were waited for; matrix products, arithmetic and copies ran while one was open for 0% of the time, Pallas kernels for 19%

profile of v8, /device:TPU:0, one launch (start us, length us, event | category | flops | bytes accessed | tf_op | source)
XLA Modules:
  0.0 46.3 jit_solution(11897835771535940557)
XLA Ops:
  0.0 2.1 %local_rotation.1 = (bf16[2,16,1664]{2,1,0:T(8,128)(2,1)S(1)}, bf16[104,8192]{1,0:T(8,128)(2,1)S(1)}) custom-call(s32[1]{0:T(128)} %bitcast.group_ref, bf16[16,3328]{1,0:T(8,128)(2,1)} %bitcast.10, bf16[16,3328]{1,0:T(8,128)(2,1)} %bitcast.11, bf16[1664,128]{1,0:T(8,128)(2,1)} %constant.47.clone.table_hbm, bf16[104,8192]{1,0:T(8,128)(2,1)} %scales_hbm.1), custom_call_target="tpu_custom_call" | custom-call | flops 100000000 | bytes 8388608 | tf_op jit(solution)/shard_map/local_rotation/pallas_call | solution.py:251
  2.1 0.5 %collective-permute-start = (bf16[2,16,1664]{2,1,0:T(8,128)(2,1)S(1)}, bf16[2,16,1664]{2,1,0:T(8,128)(2,1)S(1)}, u32[]{:S(2)}, u32[]{:S(2)}) collective-permute-start(bf16[2,16,1664]{2,1,0:T(8,128)(2,1)S(1)} %get-tuple-element.19), channel_id=1, source_target_pairs={{0,1},{1,0},{2,3},{3,2},{4,5},{5,4},{6,7},{7,6},{8,9},{9,8},{10,11... | collective-permute-start | bytes 319496 | tf_op jit(solution)/shard_map/ppermute | solution.py:133
  2.6 1.0 %collective-permute-done = bf16[2,16,1664]{2,1,0:T(8,128)(2,1)S(1)} collective-permute-done((bf16[2,16,1664]{2,1,0:T(8,128)(2,1)S(1)}, bf16[2,16,1664]{2,1,0:T(8,128)(2,1)S(1)}, u32[]{:S(2)}, u32[]{:S(2)}) %collective-permute-start) | collective-permute-done | bytes 106528 | tf_op jit(solution)/shard_map/ppermute | solution.py:133
  3.6 4.0 %collective-permute-start.1 = (bf16[16,1664]{1,0:T(8,128)(2,1)S(1)}, bf16[16,1664]{1,0:T(8,128)(2,1)S(1)}, u32[]{:S(2)}, u32[]{:S(2)}) collective-permute-start(bf16[16,1664]{1,0:T(8,128)(2,1)S(1)} %get-tuple-element.40), channel_id=1, source_target_pairs={{0,8},{1,9},{2,10},{3,11},{4,12},{5,13},{6,14},{7,15},{8,0},{9,1},... | collective-permute-start | bytes 159752 | tf_op jit(solution)/shard_map/ppermute | solution.py:133
  7.6 1.3 %collective-permute-start.2 = (bf16[16,1664]{1,0:T(8,128)(2,1)S(1)}, bf16[16,1664]{1,0:T(8,128)(2,1)S(1)}, u32[]{:S(2)}, u32[]{:S(2)}) collective-permute-start(bf16[16,1664]{1,0:T(8,128)(2,1)S(1)} %get-tuple-element.41), channel_id=1, source_target_pairs={{0,24},{1,25},{2,26},{3,27},{4,28},{5,29},{6,30},{7,31},{8,16},{9,... | collective-permute-start | bytes 159752 | tf_op jit(solution)/shard_map/ppermute | solution.py:133
  9.2 4.0 %first_unpack.1 = (bf16[1664,512]{1,0:T(8,128)(2,1)S(1)}, s32[5,832,512]{2,1,0:T(8,128)S(1)}, f32[52,8192]{1,0:T(8,128)S(1)}) custom-call(s32[1]{0:T(128)} %bitcast.group_ref, s32[1664,8192]{1,0:T(8,128)} %codes_hbm.5, bf16[104,8192]{1,0:T(8,128)(2,1)S(1)} %get-tuple-element.22.scales_in), custom_call_target="tpu_custom_call" | custom-call | bytes 10223616 | tf_op jit(solution)/shard_map/first_unpack/pallas_call | solution.py:333
  13.3 0.8 %collective-permute-done.2 = bf16[16,1664]{1,0:T(8,128)(2,1)S(1)} collective-permute-done((bf16[16,1664]{1,0:T(8,128)(2,1)S(1)}, bf16[16,1664]{1,0:T(8,128)(2,1)S(1)}, u32[]{:S(2)}, u32[]{:S(2)}) %collective-permute-start.2) | collective-permute-done | bytes 53280 | tf_op jit(solution)/shard_map/ppermute | solution.py:133
  14.1 2.2 %collective-permute-start.4 = (bf16[32,1664]{1,0:T(8,128)(2,1)S(1)}, bf16[32,1664]{1,0:T(8,128)(2,1)S(1)}, u32[]{:S(2)}, u32[]{:S(2)}) collective-permute-start(bf16[32,1664]{1,0:T(8,128)(2,1)S(1)} %pad_maximum_fusion.own_ref), channel_id=1, source_target_pairs={{0,6},{1,7},{2,4},{3,5},{4,2},{5,3},{6,0},{7,1},{8,14},{9,15},{10,... | collective-permute-start | bytes 319496 | tf_op jit(solution)/shard_map/ppermute | solution.py:133
  16.3 0.9 %collective-permute-start.5 = (bf16[32,1664]{1,0:T(8,128)(2,1)S(1)}, bf16[32,1664]{1,0:T(8,128)(2,1)S(1)}, u32[]{:S(2)}, u32[]{:S(2)}) collective-permute-start(bf16[32,1664]{1,0:T(8,128)(2,1)S(1)} %pad_maximum_fusion.own_ref), channel_id=1, source_target_pairs={{0,4},{1,5},{2,6},{3,7},{4,0},{5,1},{6,2},{7,3},{8,12},{9,13},{10,... | collective-permute-start | bytes 319496 | tf_op jit(solution)/shard_map/ppermute | solution.py:133
  17.2 0.5 %collective-permute-start.6 = (bf16[32,1664]{1,0:T(8,128)(2,1)S(1)}, bf16[32,1664]{1,0:T(8,128)(2,1)S(1)}, u32[]{:S(2)}, u32[]{:S(2)}) collective-permute-start(bf16[32,1664]{1,0:T(8,128)(2,1)S(1)} %pad_maximum_fusion.own_ref), channel_id=1, source_target_pairs={{0,2},{1,3},{2,0},{3,1},{4,6},{5,7},{6,4},{7,5},{8,10},{9,11},{10,... | collective-permute-start | bytes 319496 | tf_op jit(solution)/shard_map/ppermute | solution.py:133
  17.7 4.5 %unpack.1 = (bf16[1664,4608]{1,0:T(8,128)(2,1)S(1)}, s32[3,832,512]{2,1,0:T(8,128)S(1)}) custom-call(s32[1]{0:T(128)} %bitcast.group_ref, s32[1664,8192]{1,0:T(8,128)} %codes_hbm.5, f32[52,8192]{1,0:T(8,128)S(1)} %get-tuple-element.25.scales_ref, s32[5,832,512]{2,1,0:T(8,128)S(1)} %get-tuple-element.26.given), custom_call_target="tpu_custom_call" | custom-call | flops 61341696 | bytes 30670848 | tf_op jit(solution)/shard_map/unpack/pallas_call | solution.py:386
  22.3 6.2 %product.1 = (f32[16,8192]{1,0:T(8,128)S(1)}, bf16[16,8192]{1,0:T(8,128)(2,1)S(1)}) custom-call(s32[2]{0:T(128)S(1)} %pad_add_fusion.place_ref, s32[1664,8192]{1,0:T(8,128)} %codes_hbm.5, s32[3,832,512]{2,1,0:T(8,128)S(1)} %get-tuple-element.27.given, f32[52,8192]{1,0:T(8,128)S(1)} %get-tuple-element.25.scales_ref, ...), custom_call_target="tpu_custom_call" | custom-call | tf_op jit(solution)/shard_map/product/pallas_call | solution.py:495
  28.6 1.5 %collective-permute-done.7 = bf16[16,8192]{1,0:T(8,128)(2,1)S(1)} collective-permute-done((bf16[16,8192]{1,0:T(8,128)(2,1)S(1)}, bf16[16,8192]{1,0:T(8,128)(2,1)S(1)}, u32[]{:S(2)}, u32[]{:S(2)}) %collective-permute-start.7) | collective-permute-done | bytes 262176 | tf_op jit(solution)/shard_map/ppermute | solution.py:133
  30.3 2.5 %collective-permute-start.10 = (bf16[4,8192]{1,0:T(4,128)(2,1)S(1)}, bf16[4,8192]{1,0:T(4,128)(2,1)S(1)}, u32[]{:S(2)}, u32[]{:S(2)}) collective-permute-start(bf16[4,8192]{1,0:T(4,128)(2,1)S(1)} %get-tuple-element.38), channel_id=1, source_target_pairs={{0,18},{1,19},{2,16},{3,17},{4,22},{5,23},{6,20},{7,21},{8,26},{9,... | collective-permute-start | bytes 196616 | tf_op jit(solution)/shard_map/ppermute | solution.py:133
  32.8 0.5 %collective-permute-start.8 = (bf16[4,8192]{1,0:T(4,128)(2,1)S(1)}, bf16[4,8192]{1,0:T(4,128)(2,1)S(1)}, u32[]{:S(2)}, u32[]{:S(2)}) collective-permute-start(bf16[4,8192]{1,0:T(4,128)(2,1)S(1)} %get-tuple-element.37), channel_id=1, source_target_pairs={{0,2},{1,3},{2,0},{3,1},{4,6},{5,7},{6,4},{7,5},{8,10},{9,11},{10,... | collective-permute-start | bytes 196616 | tf_op jit(solution)/shard_map/ppermute | solution.py:133
  33.3 0.5 %collective-permute-start.9 = (bf16[4,8192]{1,0:T(4,128)(2,1)S(1)}, bf16[4,8192]{1,0:T(4,128)(2,1)S(1)}, u32[]{:S(2)}, u32[]{:S(2)}) collective-permute-start(bf16[4,8192]{1,0:T(4,128)(2,1)S(1)} %get-tuple-element.39), channel_id=1, source_target_pairs={{0,16},{1,17},{2,18},{3,19},{4,20},{5,21},{6,22},{7,23},{8,24},{9,... | collective-permute-start | bytes 196616 | tf_op jit(solution)/shard_map/ppermute | solution.py:133
  33.8 1.7 %collective-permute-done.10 = bf16[4,8192]{1,0:T(4,128)(2,1)S(1)} collective-permute-done((bf16[4,8192]{1,0:T(4,128)(2,1)S(1)}, bf16[4,8192]{1,0:T(4,128)(2,1)S(1)}, u32[]{:S(2)}, u32[]{:S(2)}) %collective-permute-start.10) | collective-permute-done | bytes 65568 | tf_op jit(solution)/shard_map/ppermute | solution.py:133
  35.5 1.5 %collective-permute-done.8 = bf16[4,8192]{1,0:T(4,128)(2,1)S(1)} collective-permute-done((bf16[4,8192]{1,0:T(4,128)(2,1)S(1)}, bf16[4,8192]{1,0:T(4,128)(2,1)S(1)}, u32[]{:S(2)}, u32[]{:S(2)}) %collective-permute-start.8) | collective-permute-done | bytes 65568 | tf_op jit(solution)/shard_map/ppermute | solution.py:133
  37.0 0.5 %collective-permute-done.9 = bf16[4,8192]{1,0:T(4,128)(2,1)S(1)} collective-permute-done((bf16[4,8192]{1,0:T(4,128)(2,1)S(1)}, bf16[4,8192]{1,0:T(4,128)(2,1)S(1)}, u32[]{:S(2)}, u32[]{:S(2)}) %collective-permute-start.9) | collective-permute-done | bytes 65568 | tf_op jit(solution)/shard_map/ppermute | solution.py:133
  37.7 2.1 %collective-permute-start.11 = (bf16[1,8192]{1,0:T(2,128)(2,1)S(1)}, bf16[1,8192]{1,0:T(2,128)(2,1)S(1)}, u32[]{:S(2)}, u32[]{:S(2)}) collective-permute-start(bf16[1,8192]{1,0:T(2,128)(2,1)S(1)} %get-tuple-element.42), channel_id=1, source_target_pairs={{0,8},{1,9},{2,10},{3,11},{4,12},{5,13},{6,14},{7,15},{8,0},{9,1},... | collective-permute-start | bytes 49160 | tf_op jit(solution)/shard_map/ppermute | solution.py:133
  39.9 1.4 %collective-permute-start.12 = (bf16[1,8192]{1,0:T(2,128)(2,1)S(1)}, bf16[1,8192]{1,0:T(2,128)(2,1)S(1)}, u32[]{:S(2)}, u32[]{:S(2)}) collective-permute-start(bf16[1,8192]{1,0:T(2,128)(2,1)S(1)} %get-tuple-element.44), channel_id=1, source_target_pairs={{0,12},{1,13},{2,14},{3,15},{4,8},{5,9},{6,10},{7,11},{8,4},{9,5},... | collective-permute-start | bytes 49160 | tf_op jit(solution)/shard_map/ppermute | solution.py:133
  41.4 1.1 %collective-permute-done.11 = bf16[1,8192]{1,0:T(2,128)(2,1)S(1)} collective-permute-done((bf16[1,8192]{1,0:T(2,128)(2,1)S(1)}, bf16[1,8192]{1,0:T(2,128)(2,1)S(1)}, u32[]{:S(2)}, u32[]{:S(2)}) %collective-permute-start.11) | collective-permute-done | bytes 16416 | tf_op jit(solution)/shard_map/ppermute | solution.py:133
  42.6 3.0 %collective-permute-done.12 = bf16[1,8192]{1,0:T(2,128)(2,1)S(1)} collective-permute-done((bf16[1,8192]{1,0:T(2,128)(2,1)S(1)}, bf16[1,8192]{1,0:T(2,128)(2,1)S(1)}, u32[]{:S(2)}, u32[]{:S(2)}) %collective-permute-start.12) | collective-permute-done | bytes 16416 | tf_op jit(solution)/shard_map/ppermute | solution.py:133
  45.6 0.7 %fusion.6 = bf16[1,8192]{1,0:T(2,128)(2,1)} fusion(bf16[1,8192]{1,0:T(2,128)(2,1)S(1)} %collective-permute-done.13, bf16[1,8192]{1,0:T(2,128)(2,1)S(1)} %collective-permute-done.12, bf16[1,8192]{1,0:T(2,128)(2,1)S(1)} %collective-permute-done.11, f32[4,8192]{1,0:T(4,128)S(1)} %get-tuple-element.34), kind=kLoop, calls=%fused_computation.16 | loop fusion | flops 57344 | bytes 98304 | tf_op jit(solution)/shard_map/convert_element_type | solution.py:572
  (19 shorter events, 1.1 us)
Async XLA Ops:
  2.1 1.5 %collective-permute-start = (bf16[2,16,1664]{2,1,0:T(8,128)(2,1)S(1)}, bf16[2,16,1664]{2,1,0:T(8,128)(2,1)S(1)}, u32[]{:S(2)}, u32[]{:S(2)}) collective-permute-start(bf16[2,16,1664]{2,1,0:T(8,128)(2,1)S(1)} %get-tuple-element.19), channel_id=1, source_target_pairs={{0,1},{1,0},{2,3},{3,2},{4,5},{5,4},{6,7},{7,6},{8,9},{9,8},{10,11... | collective-permute-start | bytes 319496 | tf_op jit(solution)/shard_map/ppermute | solution.py:133
  3.6 9.6 %collective-permute-start.1 = (bf16[16,1664]{1,0:T(8,128)(2,1)S(1)}, bf16[16,1664]{1,0:T(8,128)(2,1)S(1)}, u32[]{:S(2)}, u32[]{:S(2)}) collective-permute-start(bf16[16,1664]{1,0:T(8,128)(2,1)S(1)} %get-tuple-element.40), channel_id=1, source_target_pairs={{0,8},{1,9},{2,10},{3,11},{4,12},{5,13},{6,14},{7,15},{8,0},{9,1},... | collective-permute-start | bytes 159752 | tf_op jit(solution)/shard_map/ppermute | solution.py:133
  7.6 6.4 %collective-permute-start.2 = (bf16[16,1664]{1,0:T(8,128)(2,1)S(1)}, bf16[16,1664]{1,0:T(8,128)(2,1)S(1)}, u32[]{:S(2)}, u32[]{:S(2)}) collective-permute-start(bf16[16,1664]{1,0:T(8,128)(2,1)S(1)} %get-tuple-element.41), channel_id=1, source_target_pairs={{0,24},{1,25},{2,26},{3,27},{4,28},{5,29},{6,30},{7,31},{8,16},{9,... | collective-permute-start | bytes 159752 | tf_op jit(solution)/shard_map/ppermute | solution.py:133
  8.9 5.2 %collective-permute-start.3 = (bf16[16,1664]{1,0:T(8,128)(2,1)S(1)}, bf16[16,1664]{1,0:T(8,128)(2,1)S(1)}, u32[]{:S(2)}, u32[]{:S(2)}) collective-permute-start(bf16[16,1664]{1,0:T(8,128)(2,1)S(1)} %get-tuple-element.41), channel_id=1, source_target_pairs={{0,16},{1,17},{2,18},{3,19},{4,20},{5,21},{6,22},{7,23},{8,24},{9,... | collective-permute-start | bytes 159752 | tf_op jit(solution)/shard_map/ppermute | solution.py:133
  14.1 8.2 %collective-permute-start.4 = (bf16[32,1664]{1,0:T(8,128)(2,1)S(1)}, bf16[32,1664]{1,0:T(8,128)(2,1)S(1)}, u32[]{:S(2)}, u32[]{:S(2)}) collective-permute-start(bf16[32,1664]{1,0:T(8,128)(2,1)S(1)} %pad_maximum_fusion.own_ref), channel_id=1, source_target_pairs={{0,6},{1,7},{2,4},{3,5},{4,2},{5,3},{6,0},{7,1},{8,14},{9,15},{10,... | collective-permute-start | bytes 319496 | tf_op jit(solution)/shard_map/ppermute | solution.py:133
  16.3 6.0 %collective-permute-start.5 = (bf16[32,1664]{1,0:T(8,128)(2,1)S(1)}, bf16[32,1664]{1,0:T(8,128)(2,1)S(1)}, u32[]{:S(2)}, u32[]{:S(2)}) collective-permute-start(bf16[32,1664]{1,0:T(8,128)(2,1)S(1)} %pad_maximum_fusion.own_ref), channel_id=1, source_target_pairs={{0,4},{1,5},{2,6},{3,7},{4,0},{5,1},{6,2},{7,3},{8,12},{9,13},{10,... | collective-permute-start | bytes 319496 | tf_op jit(solution)/shard_map/ppermute | solution.py:133
  17.2 5.2 %collective-permute-start.6 = (bf16[32,1664]{1,0:T(8,128)(2,1)S(1)}, bf16[32,1664]{1,0:T(8,128)(2,1)S(1)}, u32[]{:S(2)}, u32[]{:S(2)}) collective-permute-start(bf16[32,1664]{1,0:T(8,128)(2,1)S(1)} %pad_maximum_fusion.own_ref), channel_id=1, source_target_pairs={{0,2},{1,3},{2,0},{3,1},{4,6},{5,7},{6,4},{7,5},{8,10},{9,11},{10,... | collective-permute-start | bytes 319496 | tf_op jit(solution)/shard_map/ppermute | solution.py:133
  28.5 1.6 %collective-permute-start.7 = (bf16[16,8192]{1,0:T(8,128)(2,1)S(1)}, bf16[16,8192]{1,0:T(8,128)(2,1)S(1)}, u32[]{:S(2)}, u32[]{:S(2)}) collective-permute-start(bf16[16,8192]{1,0:T(8,128)(2,1)S(1)} %get-tuple-element.32), channel_id=1, source_target_pairs={{0,1},{1,0},{2,3},{3,2},{4,5},{5,4},{6,7},{7,6},{8,9},{9,8},{10,11... | collective-permute-start | bytes 786440 | tf_op jit(solution)/shard_map/ppermute | solution.py:133
  30.3 5.3 %collective-permute-start.10 = (bf16[4,8192]{1,0:T(4,128)(2,1)S(1)}, bf16[4,8192]{1,0:T(4,128)(2,1)S(1)}, u32[]{:S(2)}, u32[]{:S(2)}) collective-permute-start(bf16[4,8192]{1,0:T(4,128)(2,1)S(1)} %get-tuple-element.38), channel_id=1, source_target_pairs={{0,18},{1,19},{2,16},{3,17},{4,22},{5,23},{6,20},{7,21},{8,26},{9,... | collective-permute-start | bytes 196616 | tf_op jit(solution)/shard_map/ppermute | solution.py:133
  32.8 4.3 %collective-permute-start.8 = (bf16[4,8192]{1,0:T(4,128)(2,1)S(1)}, bf16[4,8192]{1,0:T(4,128)(2,1)S(1)}, u32[]{:S(2)}, u32[]{:S(2)}) collective-permute-start(bf16[4,8192]{1,0:T(4,128)(2,1)S(1)} %get-tuple-element.37), channel_id=1, source_target_pairs={{0,2},{1,3},{2,0},{3,1},{4,6},{5,7},{6,4},{7,5},{8,10},{9,11},{10,... | collective-permute-start | bytes 196616 | tf_op jit(solution)/shard_map/ppermute | solution.py:133
  33.3 4.3 %collective-permute-start.9 = (bf16[4,8192]{1,0:T(4,128)(2,1)S(1)}, bf16[4,8192]{1,0:T(4,128)(2,1)S(1)}, u32[]{:S(2)}, u32[]{:S(2)}) collective-permute-start(bf16[4,8192]{1,0:T(4,128)(2,1)S(1)} %get-tuple-element.39), channel_id=1, source_target_pairs={{0,16},{1,17},{2,18},{3,19},{4,20},{5,21},{6,22},{7,23},{8,24},{9,... | collective-permute-start | bytes 196616 | tf_op jit(solution)/shard_map/ppermute | solution.py:133
  37.7 4.9 %collective-permute-start.11 = (bf16[1,8192]{1,0:T(2,128)(2,1)S(1)}, bf16[1,8192]{1,0:T(2,128)(2,1)S(1)}, u32[]{:S(2)}, u32[]{:S(2)}) collective-permute-start(bf16[1,8192]{1,0:T(2,128)(2,1)S(1)} %get-tuple-element.42), channel_id=1, source_target_pairs={{0,8},{1,9},{2,10},{3,11},{4,12},{5,13},{6,14},{7,15},{8,0},{9,1},... | collective-permute-start | bytes 49160 | tf_op jit(solution)/shard_map/ppermute | solution.py:133
  39.9 5.7 %collective-permute-start.12 = (bf16[1,8192]{1,0:T(2,128)(2,1)S(1)}, bf16[1,8192]{1,0:T(2,128)(2,1)S(1)}, u32[]{:S(2)}, u32[]{:S(2)}) collective-permute-start(bf16[1,8192]{1,0:T(2,128)(2,1)S(1)} %get-tuple-element.44), channel_id=1, source_target_pairs={{0,12},{1,13},{2,14},{3,15},{4,8},{5,9},{6,10},{7,11},{8,4},{9,5},... | collective-permute-start | bytes 49160 | tf_op jit(solution)/shard_map/ppermute | solution.py:133
  41.3 4.3 %collective-permute-start.13 = (bf16[1,8192]{1,0:T(2,128)(2,1)S(1)}, bf16[1,8192]{1,0:T(2,128)(2,1)S(1)}, u32[]{:S(2)}, u32[]{:S(2)}) collective-permute-start(bf16[1,8192]{1,0:T(2,128)(2,1)S(1)} %get-tuple-element.43), channel_id=1, source_target_pairs={{0,4},{1,5},{2,6},{3,7},{4,0},{5,1},{6,2},{7,3},{8,12},{9,13},{10,... | collective-permute-start | bytes 49160 | tf_op jit(solution)/shard_map/ppermute | solution.py:133
